TPU v7x, 128 devices: a whole 4x4x4 slice. The times are simulated.
128 devices in a mesh: dp: 8 (over x, core), ctx: 16 (over z, y).
Axes of the slice: x: 4, y: 4, z: 4, core: 2. Of those that a mesh axis runs over, the one named last changes fastest.
Arguments:
- tokens: bfloat16 [32768, 512], P(('dp', 'ctx')), may hold values from -6 to 6
- cotangent: bfloat16 [32768, 512], P(('dp', 'ctx')), may hold values from -6 to 6
- lengths: int32 [8, 2], P('dp'), may hold values from 1 to 4095, as said below
- w_qkv: float32 [512, 1536], P(None, 'ctx'), may hold values from -0.25 to 0.25
- w_proj: float32 [512, 512], P(None, 'ctx'), may hold values from -6 to 6
- w_up: float32 [512, 2048], P(None, 'ctx'), may hold values from -0.25 to 0.25
- w_down: float32 [2048, 512], P('ctx'), may hold values from -0.125 to 0.125
- w_small: float32 [12, 512], P(None, 'ctx'), may hold values from -1.2 to 1.6
- mean_qkv: float32 [512, 1536], P(None, 'ctx'), may hold values from -128 to 128
- mean_proj: float32 [512, 512], P(None, 'ctx'), may hold values from -6 to 6
- mean_up: float32 [512, 2048], P(None, 'ctx'), may hold values from -32 to 32
- mean_down: float32 [2048, 512], P('ctx'), may hold values from -64 to 64
- mean_small: float32 [12, 512], P(None, 'ctx'), may hold values from -128 to 128
- square_qkv: float32 [512, 1536], P(None, 'ctx'), may hold values from 851.968 to 13762.56
- square_proj: float32 [512, 512], P(None, 'ctx'), may hold values from 8.51968 to 137.6256
- square_up: float32 [512, 2048], P(None, 'ctx'), may hold values from 78.6432 to 1245.184
- square_down: float32 [2048, 512], P('ctx'), may hold values from 311.296 to 4915.2
- square_small: float32 [12, 512], P(None, 'ctx'), may hold values from 851.968 to 13762.56
Outputs:
- out: bfloat16 [32768, 512], P(('dp', 'ctx'))
- grad_in: bfloat16 [32768, 512], P(('dp', 'ctx'))
- new_qkv: float32 [512, 1536], P(None, 'ctx')
- new_proj: float32 [512, 512], P(None, 'ctx')
- new_up: float32 [512, 2048], P(None, 'ctx')
- new_down: float32 [2048, 512], P('ctx')
- new_small: float32 [12, 512], P(None, 'ctx')
- new_mean_qkv: float32 [512, 1536], P(None, 'ctx')
- new_mean_proj: float32 [512, 512], P(None, 'ctx')
- new_mean_up: float32 [512, 2048], P(None, 'ctx')
- new_mean_down: float32 [2048, 512], P('ctx')
- new_mean_small: float32 [12, 512], P(None, 'ctx')
- new_square_qkv: float32 [512, 1536], P(None, 'ctx')
- new_square_proj: float32 [512, 512], P(None, 'ctx')
- new_square_up: float32 [512, 2048], P(None, 'ctx')
- new_square_down: float32 [2048, 512], P('ctx')
- new_square_small: float32 [12, 512], P(None, 'ctx')
Inputs may be any that keep to these rules, and one draw needn't show every extreme that they name: `lengths`: in each group's row one length is at least 3841 and the other is under 256; the two sum to at most 4096; the longer may stand first or second.
All inputs are finite; a program needn't handle non-finite values.
Results may differ from a plain program's by a relative error of at most 0.03.
Values may be sent and summed in bfloat16 or wider, within the bound.
No kernel may reach another device: no remote copies, remote signals or barrier semaphores. Data moves between devices by JAX's collectives and lax.ppermute only.
A program may use at most 128 MiB of HBM per device.

v0:
```python
import jax
import jax.numpy as jnp
from jax import lax
from jax.sharding import PartitionSpec as P

HEADS = 8
HEAD_DIM = 64
STEP = 10


epsilon = 1e-05
negative_big = -1e30
beta_first = 0.9
beta_second = 0.95
adam_epsilon = 1e-08
weight_decay = 0.1


def layer_norm(values, gain_row, bias_row):
    center = values - jnp.mean(values, axis=-1, keepdims=True)
    spread = jnp.mean(center * center, axis=-1, keepdims=True)
    return center * lax.rsqrt(spread + epsilon) * gain_row + bias_row


def doc_ids(positions, lens_row):
    return (positions >= lens_row[0]).astype(jnp.int32) + (
        positions >= lens_row[0] + lens_row[1]
    ).astype(jnp.int32)


def bfloat(values):
    return values.astype(jnp.bfloat16)


def gelu_tanh(values):
    return jax.nn.gelu(values, approximate=True)


def block_scores(query_heads, key_piece, first_row, query_rows, query_docs, lens_row):
    piece_rows = key_piece.shape[0]
    model_width = key_piece.shape[1] // 2
    key_heads = key_piece[:, :model_width].reshape(piece_rows, HEADS, HEAD_DIM)
    key_rows = first_row + jnp.arange(piece_rows, dtype=jnp.int32)
    raw_scores = jnp.einsum(
        "qhd,khd->hqk", query_heads, key_heads, preferred_element_type=jnp.float32
    )
    allowed = (query_docs[:, None] == doc_ids(key_rows, lens_row)[None, :]) & (
        key_rows[None, :] <= query_rows[:, None]
    )
    return (raw_scores * HEAD_DIM ** (-0.5), allowed[None])


def adam_update(weight, grad_sum, mean_old, square_old, step_rate, decay_on):
    mean_new = beta_first * mean_old + (1.0 - beta_first) * grad_sum
    square_new = beta_second * square_old + (1.0 - beta_second) * grad_sum * grad_sum
    mean_hat = mean_new / (1.0 - beta_first**STEP)
    square_hat = square_new / (1.0 - beta_second**STEP)
    weight_new = weight - step_rate * (
        mean_hat / (jnp.sqrt(square_hat) + adam_epsilon) + decay_on * weight_decay * weight
    )
    return (weight_new, mean_new, square_new)


def on_device(
    tokens,
    cotangent,
    lengths,
    w_qkv,
    w_proj,
    w_up,
    w_down,
    w_small,
    mean_qkv,
    mean_proj,
    mean_up,
    mean_down,
    mean_small,
    square_qkv,
    square_proj,
    square_up,
    square_down,
    square_small,
):
    rows_dev = tokens.shape[0]
    model_width = tokens.shape[1]
    group_rows = rows_dev * lax.axis_size("ctx")
    block_rows = 512
    block_count = group_rows // block_rows
    full_qkv, full_proj, full_up, full_down, full_small = (
        lax.all_gather(bfloat(w_qkv), "ctx", axis=1, tiled=True),
        lax.all_gather(bfloat(w_proj), "ctx", axis=1, tiled=True),
        lax.all_gather(bfloat(w_up), "ctx", axis=1, tiled=True),
        lax.all_gather(bfloat(w_down), "ctx", axis=0, tiled=True),
        lax.all_gather(bfloat(w_small), "ctx", axis=1, tiled=True),
    )
    packed = full_small.astype(jnp.float32)
    gain_one = packed[0]
    bias_one = packed[1]
    bias_query = packed[2]
    bias_value = packed[3]
    bias_proj = packed[4]
    gain_two = packed[5]
    bias_two = packed[6]
    bias_down = packed[7]
    bias_up = packed[8:].reshape(-1)
    lens_row = lengths[0]
    query_rows = lax.axis_index("ctx") * rows_dev + jnp.arange(rows_dev, dtype=jnp.int32)
    query_docs = doc_ids(query_rows, lens_row)
    live_rows = (query_rows < lens_row[0] + lens_row[1]).astype(jnp.float32)
    inputs = tokens.astype(jnp.float32)
    normed_one = bfloat(layer_norm(inputs, gain_one, bias_one))
    mixed_qkv = jnp.dot(normed_one, full_qkv, preferred_element_type=jnp.float32)
    queries = bfloat(mixed_qkv[:, :model_width] + bias_query)
    key_value = bfloat(
        jnp.concatenate(
            [
                mixed_qkv[:, model_width : 2 * model_width],
                mixed_qkv[:, 2 * model_width :] + bias_value,
            ],
            axis=1,
        )
    )
    query_heads = queries.reshape(rows_dev, HEADS, HEAD_DIM)
    gathered = lax.all_gather(key_value, "ctx", axis=0, tiled=True)
    block_starts = jnp.arange(block_count, dtype=jnp.int32)

    def stats_step(state_pair, block_index):
        run_max, run_sum = state_pair
        key_piece = lax.dynamic_slice_in_dim(gathered, block_index * block_rows, block_rows, 0)
        scores, allowed = block_scores(
            query_heads, key_piece, block_index * block_rows, query_rows, query_docs, lens_row
        )
        masked = jnp.where(allowed, scores, negative_big)
        new_max = jnp.maximum(run_max, jnp.max(masked, axis=-1))
        exp_terms = jnp.where(allowed, jnp.exp(masked - new_max[..., None]), 0.0)
        run_sum = run_sum * jnp.exp(run_max - new_max) + jnp.sum(exp_terms, axis=-1)
        return ((new_max, run_sum), None)

    start_stats = (
        jnp.full((HEADS, rows_dev), negative_big, jnp.float32),
        jnp.zeros((HEADS, rows_dev), jnp.float32),
    )
    (row_max, row_sum), _ = lax.scan(stats_step, start_stats, block_starts)

    def soft_weights(scores, allowed):
        return jnp.where(allowed, jnp.exp(scores - row_max[..., None]) / row_sum[..., None], 0.0)

    def value_step(running, block_index):
        key_piece = lax.dynamic_slice_in_dim(gathered, block_index * block_rows, block_rows, 0)
        scores, allowed = block_scores(
            query_heads, key_piece, block_index * block_rows, query_rows, query_docs, lens_row
        )
        value_heads = key_piece[:, model_width:].reshape(block_rows, HEADS, HEAD_DIM)
        attn_probs = bfloat(soft_weights(scores, allowed))
        return (
            running
            + jnp.einsum(
                "hqk,khd->qhd", attn_probs, value_heads, preferred_element_type=jnp.float32
            ),
            None,
        )

    zero_heads = jnp.zeros((rows_dev, HEADS, HEAD_DIM), jnp.float32)
    attended, _ = lax.scan(value_step, zero_heads, block_starts)
    attended_b = bfloat(attended.reshape(rows_dev, model_width))
    residual = (
        inputs + jnp.dot(attended_b, full_proj, preferred_element_type=jnp.float32) + bias_proj
    )
    normed_two = bfloat(layer_norm(residual, gain_two, bias_two))
    hidden = jnp.dot(normed_two, full_up, preferred_element_type=jnp.float32) + bias_up
    activated = bfloat(gelu_tanh(hidden))
    branch = jnp.dot(activated, full_down, preferred_element_type=jnp.float32) + bias_down
    output = bfloat(residual + branch)
    grad_out = cotangent.astype(jnp.float32) * live_rows[:, None]
    grad_out_b = bfloat(grad_out)
    grad_down = jnp.einsum("tf,td->fd", activated, grad_out_b, preferred_element_type=jnp.float32)
    grad_activ = jnp.einsum("td,fd->tf", grad_out_b, full_down, preferred_element_type=jnp.float32)
    _, gelu_pull = jax.vjp(gelu_tanh, hidden)
    grad_hidden = gelu_pull(grad_activ)[0]
    grad_hidden_b = bfloat(grad_hidden)
    grad_up = jnp.einsum("td,tf->df", normed_two, grad_hidden_b, preferred_element_type=jnp.float32)
    grad_normed_two = jnp.einsum(
        "tf,df->td", grad_hidden_b, full_up, preferred_element_type=jnp.float32
    )
    _, norm_pull_two = jax.vjp(layer_norm, residual, gain_two, bias_two)
    grad_resid_norm, grad_gain_two, grad_bias_two = norm_pull_two(grad_normed_two)
    grad_resid = grad_out + grad_resid_norm
    grad_resid_b = bfloat(grad_resid)
    grad_proj = jnp.einsum(
        "td,te->de", attended_b, grad_resid_b, preferred_element_type=jnp.float32
    )
    grad_attended_b = bfloat(
        jnp.einsum("te,de->td", grad_resid_b, full_proj, preferred_element_type=jnp.float32)
    )
    grad_heads = grad_attended_b.reshape(rows_dev, HEADS, HEAD_DIM)
    softmax_dot = jnp.sum(grad_heads.astype(jnp.float32) * attended, axis=-1).T

    def piece_grads(key_piece, first_row):
        piece_rows = key_piece.shape[0]
        scores, allowed = block_scores(
            query_heads, key_piece, first_row, query_rows, query_docs, lens_row
        )
        attn_probs = soft_weights(scores, allowed)
        key_heads = key_piece[:, :model_width].reshape(piece_rows, HEADS, HEAD_DIM)
        value_heads = key_piece[:, model_width:].reshape(piece_rows, HEADS, HEAD_DIM)
        grad_probs = jnp.einsum(
            "qhd,khd->hqk", grad_heads, value_heads, preferred_element_type=jnp.float32
        )
        grad_scores = bfloat(
            attn_probs * (grad_probs - softmax_dot[..., None]) * HEAD_DIM ** (-0.5)
        )
        grad_query = jnp.einsum(
            "hqk,khd->qhd", grad_scores, key_heads, preferred_element_type=jnp.float32
        )
        grad_key = jnp.einsum(
            "hqk,qhd->khd", grad_scores, query_heads, preferred_element_type=jnp.float32
        ).reshape(piece_rows, model_width)
        grad_value = jnp.einsum(
            "hqk,qhd->khd", bfloat(attn_probs), grad_heads, preferred_element_type=jnp.float32
        ).reshape(piece_rows, model_width)
        return (grad_query, jnp.concatenate([grad_key, grad_value], axis=1))

    def grad_step(running, block_index):
        key_piece = lax.dynamic_slice_in_dim(gathered, block_index * block_rows, block_rows, 0)
        grad_query, grad_pair = piece_grads(key_piece, block_index * block_rows)
        return (running + grad_query, grad_pair)

    grad_query, grad_pairs = lax.scan(grad_step, zero_heads, block_starts)
    grad_pairs = grad_pairs.reshape(group_rows, 2 * model_width)
    grad_pairs_own = lax.psum_scatter(
        grad_pairs.astype(jnp.bfloat16), "ctx", scatter_dimension=0, tiled=True
    ).astype(jnp.float32)
    grad_rows_qkv = bfloat(
        jnp.concatenate([grad_query.reshape(rows_dev, model_width), grad_pairs_own], axis=1)
    )
    grad_qkv = jnp.einsum(
        "td,te->de", normed_one, grad_rows_qkv, preferred_element_type=jnp.float32
    )
    grad_normed_one = jnp.einsum(
        "te,de->td", grad_rows_qkv, full_qkv, preferred_element_type=jnp.float32
    )
    _, norm_pull_one = jax.vjp(layer_norm, inputs, gain_one, bias_one)
    grad_in_norm, grad_gain_one, grad_bias_one = norm_pull_one(grad_normed_one)
    grad_in = bfloat(grad_resid + grad_in_norm)
    column_sums = jnp.sum(grad_rows_qkv.astype(jnp.float32), axis=0)
    grad_small = jnp.concatenate(
        [
            jnp.stack(
                [
                    grad_gain_one,
                    grad_bias_one,
                    column_sums[:model_width],
                    column_sums[2 * model_width :],
                    jnp.sum(grad_resid, axis=0),
                    grad_gain_two,
                    grad_bias_two,
                    jnp.sum(grad_out, axis=0),
                ]
            ),
            jnp.sum(grad_hidden, axis=0).reshape(-1, model_width),
        ],
        axis=0,
    )
    own_qkv, own_proj, own_up, own_down, own_small = (
        lax.psum_scatter(
            grad_qkv.astype(jnp.bfloat16), "ctx", scatter_dimension=1, tiled=True
        ).astype(jnp.float32),
        lax.psum_scatter(
            grad_proj.astype(jnp.bfloat16), "ctx", scatter_dimension=1, tiled=True
        ).astype(jnp.float32),
        lax.psum_scatter(
            grad_up.astype(jnp.bfloat16), "ctx", scatter_dimension=1, tiled=True
        ).astype(jnp.float32),
        lax.psum_scatter(
            grad_down.astype(jnp.bfloat16), "ctx", scatter_dimension=0, tiled=True
        ).astype(jnp.float32),
        lax.psum_scatter(
            grad_small.astype(jnp.bfloat16), "ctx", scatter_dimension=1, tiled=True
        ).astype(jnp.float32),
    )
    own_qkv, own_proj, own_up, own_down, own_small = (
        lax.psum(own_qkv.astype(jnp.bfloat16), "dp").astype(jnp.float32),
        lax.psum(own_proj.astype(jnp.bfloat16), "dp").astype(jnp.float32),
        lax.psum(own_up.astype(jnp.bfloat16), "dp").astype(jnp.float32),
        lax.psum(own_down.astype(jnp.bfloat16), "dp").astype(jnp.float32),
        lax.psum(own_small.astype(jnp.bfloat16), "dp").astype(jnp.float32),
    )
    new_qkv, new_mean_qkv, new_square_qkv = adam_update(
        w_qkv, own_qkv, mean_qkv, square_qkv, 0.04, 1.0
    )
    new_proj, new_mean_proj, new_square_proj = adam_update(
        w_proj, own_proj, mean_proj, square_proj, 1.0, 1.0
    )
    new_up, new_mean_up, new_square_up = adam_update(w_up, own_up, mean_up, square_up, 0.04, 1.0)
    new_down, new_mean_down, new_square_down = adam_update(
        w_down, own_down, mean_down, square_down, 0.02, 1.0
    )
    new_small, new_mean_small, new_square_small = adam_update(
        w_small, own_small, mean_small, square_small, 2.0, 0.0
    )
    return (
        output,
        grad_in,
        new_qkv,
        new_proj,
        new_up,
        new_down,
        new_small,
        new_mean_qkv,
        new_mean_proj,
        new_mean_up,
        new_mean_down,
        new_mean_small,
        new_square_qkv,
        new_square_proj,
        new_square_up,
        new_square_down,
        new_square_small,
    )


def solution(mesh):
    placed = (
        P(("dp", "ctx"), None),
        P(("dp", "ctx"), None),
        P("dp", None),
        P(None, "ctx"),
        P(None, "ctx"),
        P(None, "ctx"),
        P("ctx", None),
        P(None, "ctx"),
        P(None, "ctx"),
        P(None, "ctx"),
        P(None, "ctx"),
        P("ctx", None),
        P(None, "ctx"),
        P(None, "ctx"),
        P(None, "ctx"),
        P(None, "ctx"),
        P("ctx", None),
        P(None, "ctx"),
    )
    return jax.shard_map(
        on_device,
        mesh=mesh,
        in_specs=placed,
        out_specs=(
            P(("dp", "ctx"), None),
            P(("dp", "ctx"), None),
            P(None, "ctx"),
            P(None, "ctx"),
            P(None, "ctx"),
            P("ctx", None),
            P(None, "ctx"),
            P(None, "ctx"),
            P(None, "ctx"),
            P(None, "ctx"),
            P("ctx", None),
            P(None, "ctx"),
            P(None, "ctx"),
            P(None, "ctx"),
            P(None, "ctx"),
            P("ctx", None),
            P(None, "ctx"),
        ),
        check_vma=False,
    )
```

profile of v0, /device:TPU:1, one launch (start us, length us, event | category | flops | bytes accessed | tf_op | source)
XLA Modules:
  0.0 853.8 jit_solution(5825708153858768330)
XLA Ops:
  7.2 1.6 convert_element_type.190
  9.6 20.6 %all-gather = bf16[16,32,12]{1,2,0:T(8,128)(2,1)S(1)} all-gather(bf16[1,32,12]{1,2,0:T(8,128)(2,1)S(1)} %convert_bitcast_fusion), channel_id=1, replica_groups=mesh['dp'=8,'ctx'=16] {'ctx'}, dimensions={0}, use_global_device_ids=true | all-gather | bytes 13056 | tf_op jit(solution)/shard_map/all_gather | solution.py:94
  33.1 24.0 %all-gather.6.cloned.1.call-done = bf16[512,1536]{0,1:T(8,128)(2,1)} async-done(((bf16[512,96]{0,1:T(8,128)(2,1)}), bf16[512,1536]{0,1:T(8,128)(2,1)}) %all-gather.6.cloned.1.call-update) | async-done | bytes 1572880 | tf_op jit(solution)/shard_map/all_gather | solution.py:90
  57.2 2.1 fusion.79
  62.7 20.0 %all_gather.21 = bf16[512,512]{0,1:T(8,128)(2,1)S(1)} all-gather(bf16[512,32]{0,1:T(8,128)(2,1)S(1)} %convert_element_type.196), channel_id=1, replica_groups=mesh['dp'=8,'ctx'=16] {'ctx'}, dimensions={1}, use_global_device_ids=true | all-gather | bytes 557056 | tf_op jit(solution)/shard_map/all_gather | solution.py:91
  84.1 48.3 %all-gather.8.cloned.1.call-done = bf16[4096,1024]{1,0:T(8,128)(2,1)} async-done(((bf16[256,1024]{1,0:T(8,128)(2,1)}), bf16[4096,1024]{1,0:T(8,128)(2,1)}) %all-gather.8.cloned.1.call-update) | async-done | bytes 8388624 | tf_op jit(solution)/shard_map/all_gather | solution.py:124
  132.4 11.9 %copy.89 = bf16[4096,1024]{0,1:T(8,128)(2,1)} copy(bf16[4096,1024]{1,0:T(8,128)(2,1)} %all-gather.8.cloned.1.call-done) | data formatting | bytes 16777216
  144.3 41.4 %while.46 = (s32[]{:T(128)}, f32[8,256]{1,0:T(8,128)S(1)}, f32[8,256]{1,0:T(8,128)S(1)}, s32[8]{0:T(128)S(1)}, s32[2]{0:T(128)S(1)}, /*index=5*/s32[]{:T(128)}, ...) while((s32[]{:T(128)}, f32[8,256]{1,0:T(8,128)S(1)}, ...), condition=%wide.region_5.6_spmd.clone.clone.clone, body=%wide.region_2.5_spmd.clone.clone.clone.sunk | while | flops 143014400 | bytes 10735854 | solution.py:143
  185.8 39.4 %while.47 = (s32[]{:T(128)}, f32[256,8,64]{0,2,1:T(8,128)S(1)}, s32[8]{0:T(128)S(1)}, bf16[4096,1024]{0,1:T(8,128)(2,1)}, s32[2]{0:T(128)S(1)}, /*index=5*/s32[]...) while((s32[]{:T(128)}, f32[256,8,64]{0,2,1:T(8,128)S(1)}, ...), condition=%wide.region_7.8_spmd.clone.clone.clone, body=%wide.region_6.7_spmd.clone.clone.clone.sunk | while | flops 274338304 | bytes 4747533 | solution.py:164
  188.0 1.3 constant_dynamic-slice_fusion.6
  189.2 1.5 fusion.163
  192.9 1.3 constant_dynamic-slice_fusion.6
  194.2 1.4 fusion.163
  197.8 1.3 constant_dynamic-slice_fusion.6
  199.1 1.4 fusion.163
  202.7 1.3 constant_dynamic-slice_fusion.6
  204.0 1.5 fusion.163
  207.7 1.3 constant_dynamic-slice_fusion.6
  209.0 1.4 fusion.163
  213.9 1.4 fusion.163
  217.5 1.3 constant_dynamic-slice_fusion.6
  218.8 1.5 fusion.163
  223.7 1.5 fusion.163
  225.9 3.8 convolution_add_fusion
  229.7 4.2 fusion.100
  233.9 1.4 multiply_reduce_fusion
  237.5 79.2 %while.48 = (s32[]{:T(128)}, f32[256,8,64]{0,2,1:T(8,128)S(1)}, bf16[8,512,1024]{2,1,0:T(8,128)(2,1)}, s32[8]{0:T(128)}, bf16[4096,1024]{0,1:T(8,128)(2,1)}, /*i...) while((s32[]{:T(128)}, f32[256,8,64]{0,2,1:T(8,128)S(1)}, ...), condition=%wide.region_14.15_spmd.clone.clone.clone, body=%wide.region_13.14_spmd.clone.clone.clone.sunk | while | flops 683282944 | bytes 32280872 | solution.py:228
  240.3 1.3 fusion.174
  280.0 1.3 fusion.174
  317.8 2.1 convolution_convert_fusion.1
  319.9 2.5 copy.98
  323.3 77.0 %reduce-scatter.11.cloned.1.call-done = bf16[256,1024]{1,0:T(8,128)(2,1)} async-done(((bf16[4096,1024]{1,0:T(8,128)(2,1)}), bf16[256,1024]{1,0:T(8,128)(2,1)}) %reduce-scatter.11.cloned.1.call-update) | async-done | bytes 524304 | tf_op jit(solution)/shard_map/reduce_scatter | solution.py:230
  400.3 1.7 fusion.83
  405.9 4.0 convolution_convert_fusion
  410.9 2.9 convolution_convert_fusion.2
  414.0 3.2 fusion.36
  417.2 59.7 %reduce-scatter.19.cloned.1.call-done = bf16[128,512]{1,0:T(8,128)(2,1)} async-done(((bf16[2048,512]{1,0:T(8,128)(2,1)}), bf16[128,512]{1,0:T(8,128)(2,1)}) %reduce-scatter.19.cloned.1.call-update) | async-done | bytes 131088
  476.9 1.7 copy.99
  478.6 73.2 %reduce-scatter.21.cloned.1.call-done = bf16[32,12]{1,0:T(8,128)(2,1)} async-done(((bf16[512,12]{1,0:T(8,128)(2,1)}), bf16[32,12]{1,0:T(8,128)(2,1)}) %reduce-scatter.21.cloned.1.call-update) | async-done | bytes 784
  552.5 74.4 %reduce-scatter.15.cloned.1.call-done = bf16[512,32]{0,1:T(8,128)(2,1)} async-done(((bf16[512,512]{0,1:T(8,128)(2,1)}), bf16[512,32]{0,1:T(8,128)(2,1)}) %reduce-scatter.15.cloned.1.call-update) | async-done | bytes 32784 | tf_op jit(solution)/shard_map/reduce_scatter | solution.py:268
  627.0 23.6 %all-reduce = (bf16[512,32]{0,1:T(8,128)(2,1)S(1)}, bf16[12,32]{1,0:T(8,128)(2,1)S(1)}) all-reduce(bf16[512,32]{0,1:T(8,128)(2,1)} %reduce-scatter.15.cloned.1.call-done, bf16[12,32]{1,0:T(8,128)(2,1)S(1)} %copy.101), channel_id=1, replica_groups=mesh['dp'=8,'ctx'=16] {'dp'}, use_global_device_ids=true, to_apply=%region_21.22 | all-reduce | flops 16768 | bytes 67072 | tf_op jit(solution)/shard_map/psum | solution.py:283
  650.6 1.5 add_subtract_fusion
  652.1 52.4 %reduce-scatter.17.cloned.1.call-done = bf16[128,512]{1,0:T(8,128)(2,1)} async-done(((bf16[2048,512]{1,0:T(8,128)(2,1)}), bf16[128,512]{1,0:T(8,128)(2,1)}) %reduce-scatter.17.cloned.1.call-update) | async-done | bytes 131088 | tf_op jit(solution)/shard_map/reduce_scatter | solution.py:274
  704.5 76.0 %reduce-scatter.13.cloned.1.call-done = bf16[512,96]{0,1:T(8,128)(2,1)} async-done(((bf16[512,1536]{0,1:T(8,128)(2,1)}), bf16[512,96]{0,1:T(8,128)(2,1)}) %reduce-scatter.13.cloned.1.call-update) | async-done | bytes 98320 | tf_op jit(solution)/shard_map/reduce_scatter | solution.py:265
  780.5 1.3 multiply_subtract_fusion.3
  781.8 60.5 %all-reduce.4.cloned.1.call-done = (bf16[512,96]{0,1:T(8,128)(2,1)}, bf16[512,128]{1,0:T(8,128)(2,1)}, bf16[128,512]{1,0:T(8,128)(2,1)}) async-done(((bf16[512,96]{0,1:T(8,128)(2,1)}, bf16[512,128]{1,0:T(8,128)(2,1)}, bf16[128,512]{1,0:T(8,128)(2,1)}), (bf16[512,96]{0,1:T(8,128)(2,1)}, bf16[512,128]{1,0:T(8,128)(2,1)}, bf16[128,512]{1,0:T(8,128)(2,1)})) %all-reduce.4.cloned.1.call-update) | async-done | bytes 360464 | tf_op jit(solution)/shard_map/psum | solution.py:282
  842.3 2.0 multiply_subtract_fusion.2
  844.4 1.9 multiply_subtract_fusion.1
  (366 shorter events, 139.3 us)
Async XLA Ops:
  7.2 50.0 %all-gather.6.cloned.1.call-start = ((), (), s32[]{:S(2)}) async-start(), calls=%async_computation.6 | async-start | bytes 1671168 | tf_op jit(solution)/shard_map/all_gather | solution.py:90
  8.8 123.5 %all-gather.8.cloned.1.call-start = ((), (), s32[]{:S(2)}) async-start(), calls=%async_computation.7 | async-start | bytes 8912896 | tf_op jit(solution)/shard_map/all_gather | solution.py:124
  59.3 1.2 copy-start.15
  59.3 1.9 copy-start.17
  59.4 2.7 copy-start.27
  59.4 3.3 copy-start.22
  60.4 165.5 %all-gather.10.cloned.1.call-start = ((), (), s32[]{:S(2)}) async-start(), calls=%async_computation.8 | async-start | bytes 2228224 | tf_op jit(solution)/shard_map/all_gather | solution.py:92
  61.2 168.5 %all-gather.12.cloned.1.call-start = ((), (), s32[]{:S(2)}) async-start(), calls=%async_computation.9 | async-start | bytes 2228224 | tf_op jit(solution)/shard_map/all_gather | solution.py:93
  62.0 338.3 %reduce-scatter.11.cloned.1.call-start = ((), (), s32[]{:S(2)}) async-start(), calls=%async_computation.10 | async-start | bytes 8912896 | tf_op jit(solution)/shard_map/reduce_scatter | solution.py:230
  185.8 39.5 %copy-start.2 = (bf16[256,512]{1,0:T(8,128)(2,1)S(1)}, bf16[256,512]{1,0:T(8,128)(2,1)}, u32[]{:S(2)}) copy-start(bf16[256,512]{1,0:T(8,128)(2,1)} %param.24) | copy-start | bytes 786436
  225.2 4.5 copy-start.5
  225.7 9.7 %copy-start = (f32[256,512]{1,0:T(8,128)}, f32[256,512]{1,0:T(8,128)S(1)}, u32[]{:S(2)}) copy-start(f32[256,512]{1,0:T(8,128)S(1)} %get-tuple-element.981) | copy-start | bytes 1572868
  225.9 3.8 copy-start.7
  229.7 4.2 copy-start.10
  233.9 1.4 copy-start.19
  235.6 0.8 copy-start.3
  316.7 1.0 copy-start.1
  316.8 160.1 %reduce-scatter.19.cloned.1.call-start = ((), (), s32[]{:S(2)}) async-start(), calls=%async_computation.14 | async-start | bytes 2228224
  322.4 0.7 copy-start.32
  322.4 77.9 %copy-start.11 = (bf16[512,1536]{0,1:T(8,128)(2,1)S(1)}, bf16[512,1536]{0,1:T(8,128)(2,1)}, u32[]{:S(2)}) copy-start(bf16[512,1536]{0,1:T(8,128)(2,1)} %all-gather.6.cloned.1.call-done) | copy-start | bytes 4718596
  322.4 229.3 %reduce-scatter.21.cloned.1.call-start = ((), (), s32[]{:S(2)}) async-start(), calls=%async_computation.15 | async-start | bytes 139264
  323.3 77.0 %copy-start.12 = (bf16[256,512]{1,0:T(8,128)(2,1)}, bf16[256,512]{1,0:T(8,128)(2,1)S(1)}, u32[]{:S(2)}) copy-start(bf16[256,512]{1,0:T(8,128)(2,1)S(1)} %copy.93) | copy-start | bytes 786436
  323.3 79.1 %copy-start.4 = (f32[256,512]{1,0:T(8,128)S(1)}, f32[256,512]{1,0:T(8,128)}, u32[]{:S(2)}) copy-start(f32[256,512]{1,0:T(8,128)} %copy-done.3) | copy-start | bytes 1572868
  323.3 79.1 %copy-start.8 = (bf16[256,512]{1,0:T(8,128)(2,1)S(1)}, bf16[256,512]{1,0:T(8,128)(2,1)}, u32[]{:S(2)}) copy-start(bf16[256,512]{1,0:T(8,128)(2,1)} %param.25) | copy-start | bytes 786436
  402.0 1.5 copy-start.13
  402.0 1.5 copy-start.21
  402.0 2.6 copy-start.6
  404.5 222.4 %reduce-scatter.15.cloned.1.call-start = ((), (), s32[]{:S(2)}) async-start(), calls=%async_computation.12 | async-start | bytes 557056 | tf_op jit(solution)/shard_map/reduce_scatter | solution.py:268
  405.9 298.7 %reduce-scatter.17.cloned.1.call-start = ((), (), s32[]{:S(2)}) async-start(), calls=%async_computation.13 | async-start | bytes 2228224 | tf_op jit(solution)/shard_map/reduce_scatter | solution.py:274
  410.0 0.9 copy-start.14
  410.0 3.9 copy-start.9
  410.0 3.9 copy-start.31
  410.0 370.5 %reduce-scatter.13.cloned.1.call-start = ((), (), s32[]{:S(2)}) async-start(), calls=%async_computation.11 | async-start | bytes 1671168 | tf_op jit(solution)/shard_map/reduce_scatter | solution.py:265
  413.9 428.5 %all-reduce.4.cloned.1.call-start = ((), (), s32[]{:S(2)}) async-start(), calls=%async_computation.16 | async-start | bytes 720896 | tf_op jit(solution)/shard_map/psum | solution.py:282
  413.9 236.7 %copy-start.29 = (f32[512,32]{0,1:T(8,128)S(1)}, f32[512,32]{0,1:T(8,128)}, u32[]{:S(2)}) copy-start(f32[512,32]{0,1:T(8,128)} %param.33) | copy-start | bytes 196612
  413.9 366.6 %copy-start.30 = (f32[12,32]{1,0:T(8,128)S(1)}, f32[12,32]{1,0:T(8,128)}, u32[]{:S(2)}) copy-start(f32[12,32]{1,0:T(8,128)} %param.31) | copy-start | bytes 4612
  414.0 428.4 %copy-start.20 = (f32[512,96]{0,1:T(8,128)S(1)}, f32[512,96]{0,1:T(8,128)}, u32[]{:S(2)}) copy-start(f32[512,96]{0,1:T(8,128)} %param.27) | copy-start | bytes 589828
  417.1 427.2 %copy-start.16 = (f32[512,128]{1,0:T(8,128)S(1)}, f32[512,128]{1,0:T(8,128)}, u32[]{:S(2)}) copy-start(f32[512,128]{1,0:T(8,128)} %param.29) | copy-start | bytes 786436
  417.1 427.2 %copy-start.23 = (f32[512,128]{1,0:T(8,128)S(1)}, f32[512,128]{1,0:T(8,128)}, u32[]{:S(2)}) copy-start(f32[512,128]{1,0:T(8,128)} %param.34) | copy-start | bytes 786436
  417.1 427.2 %copy-start.24 = (f32[512,128]{1,0:T(8,128)S(1)}, f32[512,128]{1,0:T(8,128)}, u32[]{:S(2)}) copy-start(f32[512,128]{1,0:T(8,128)} %param.39) | copy-start | bytes 786436
  417.1 429.1 %copy-start.18 = (f32[128,512]{1,0:T(8,128)S(1)}, f32[128,512]{1,0:T(8,128)}, u32[]{:S(2)}) copy-start(f32[128,512]{1,0:T(8,128)} %param.30) | copy-start | bytes 786436
  417.1 429.1 %copy-start.25 = (f32[128,512]{1,0:T(8,128)S(1)}, f32[128,512]{1,0:T(8,128)}, u32[]{:S(2)}) copy-start(f32[128,512]{1,0:T(8,128)} %param.35) | copy-start | bytes 786436
  417.1 429.1 %copy-start.26 = (f32[128,512]{1,0:T(8,128)S(1)}, f32[128,512]{1,0:T(8,128)}, u32[]{:S(2)}) copy-start(f32[128,512]{1,0:T(8,128)} %param.40) | copy-start | bytes 786436
  842.3 3.9 copy-start.28
Sparse Core Ops, SparseCore 0:
  10.7 46.3 all-gather.5
  60.6 71.7 all-gather.7
  135.1 46.7 all-gather.9
  184.4 44.3 all-gather.11
  316.9 83.3 reduce-scatter.10
  403.4 73.4 reduce-scatter.18
  481.0 70.7 reduce-scatter.20
  554.9 71.9 reduce-scatter.14
  630.6 73.9 reduce-scatter.16
  707.6 72.8 reduce-scatter.12
  783.6 58.7 all-reduce.3
where the time goes:
time: 858 us; the launch traced here: 854 us
  waiting for transfers between devices  546 us (64%)
  local copies, waits for them, and re-layouts  84.8 us (10%)
  matrix products  78.6 us (9%)
  blocking collectives  64.2 us (7%)
  other arithmetic  47 us (5%)
  loops' own time  17.3 us (2%)
  between operations  15.8 us (2%)
    unnamed x13, waiting for transfers between devices  133 us
    reduce_scatter x1, waiting for transfers between devices, on_device(): lax.psum_scatter(grad_pairs.astype(jnp.bfloat16), 'ctx', scatter_dimensio...  77 us
    reduce_scatter x1, waiting for transfers between devices, on_device(): lax.psum_scatter(grad_qkv.astype(jnp.bfloat16), 'ctx', scatter_dimension=...  76 us
    reduce_scatter x1, waiting for transfers between devices, on_device(): lax.psum_scatter(grad_proj.astype(jnp.bfloat16), 'ctx', scatter_dimension...  74.4 us
    psum x1, waiting for transfers between devices, on_device(): lax.psum(own_qkv.astype(jnp.bfloat16), 'dp').astype(jnp.float32)  60.5 us
    reduce_scatter x1, waiting for transfers between devices, on_device(): lax.psum_scatter(grad_down.astype(jnp.bfloat16), 'ctx', scatter_dimension...  52.4 us
    all_gather x1, waiting for transfers between devices, on_device(): gathered = lax.all_gather(key_value, 'ctx', axis=0, tiled=True)  48.3 us
    all_gather x1, waiting for transfers between devices, on_device(): lax.all_gather(bfloat(w_qkv), 'ctx', axis=1, tiled=True)  24 us
  transfers between devices with their start and end apart: 11, of which 9 were waited for; matrix products, arithmetic and copies ran while one was open for 14% of the time, Pallas kernels for 0%

commit v1 on v0

v1 whole, which is shorter than its diff:
```python
import functools
import jax
import jax.numpy as jnp
from jax import lax
from jax.experimental import pallas as pl
from jax.experimental.pallas import tpu as pltpu
from jax.sharding import Mesh, PartitionSpec as P

HEADS = 8
HEAD_DIM = 64
STEP = 10
WIDTH = 512
HIDDEN = 2048
ROWS = 256
CHUNK = 512
TILE = 512

epsilon = 1e-05
negative_big = -1e30
beta_first = 0.9
beta_second = 0.95
adam_epsilon = 1e-08
weight_decay = 0.1
gelu_scale = 0.7978845608028654
gelu_cubic = 0.044715
log2_e = 1.4426950408889634

NN = (((1,), (0,)), ((), ()))
NT = (((1,), (1,)), ((), ()))
TN = (((0,), (0,)), ((), ()))
CTX = ("z", "y")


def dot(left, right, dims):
    return lax.dot_general(left, right, dims, preferred_element_type=jnp.float32)


def bfloat(values):
    return values.astype(jnp.bfloat16)


def f32(values):
    return values.astype(jnp.float32)


def normed(values):
    center = values - jnp.mean(values, axis=-1, keepdims=True)
    spread = jnp.mean(center * center, axis=-1, keepdims=True)
    scale = lax.rsqrt(spread + epsilon)
    return center * scale, scale


def norm_back(unit, scale, gain, grad):
    scaled = grad * gain
    first = jnp.mean(scaled, axis=-1, keepdims=True)
    second = jnp.mean(scaled * unit, axis=-1, keepdims=True)
    grad_values = (scaled - first - unit * second) * scale
    grad_gain = jnp.sum(grad * unit, axis=0, keepdims=True)
    grad_bias = jnp.sum(grad, axis=0, keepdims=True)
    return grad_values, grad_gain, grad_bias


def low_lanes(shape):
    return lax.broadcasted_iota(jnp.int32, shape, 1) < HEAD_DIM


def pair_pack(top, bottom):
    low = low_lanes(top.shape)
    first = jnp.where(low, top, pltpu.roll(bottom, HEAD_DIM, 1))
    second = jnp.where(low, pltpu.roll(top, HEAD_DIM, 1), bottom)
    return first, second


def qkv_kernel(tokens, wide, send, weights, small):
    for owner in range(16):
        for piece in range(3):
            first = owner * 96 + piece * 32
            part, offset = divmod(first, 512)
            if part == 0:
                target = first
            else:
                head, inside = divmod(offset, HEAD_DIM)
                target = 512 + head * 128 + (part - 1) * HEAD_DIM + inside
            half, row = divmod(piece * 32, 64)
            weights[target : target + 32, :] = wide[half, owner, row : row + 32, :]
    lane = lax.broadcasted_iota(jnp.int32, (16, 128), 1)
    for block in range(4):
        total = jnp.zeros((16, 128), jnp.float32)
        for inside in range(4):
            piece = f32(wide[1, block * 4 + inside, 32:48, 0:128])
            moved = pltpu.roll(piece, inside * 32, 1) if inside else piece
            keep = (lane >= inside * 32) & (lane < inside * 32 + 32)
            total = jnp.where(keep, moved, total)
        small[:, block * 128 : block * 128 + 128] = total
    unit, _ = normed(f32(tokens[...]))
    hidden = bfloat(unit * small[0:1, :] + small[1:2, :])
    for pair in range(4):
        columns = slice(pair * 128, pair * 128 + 128)
        query = dot(hidden, weights[columns, :], NT) + small[2:3, columns]
        query = f32(bfloat(query)) * HEAD_DIM**-0.5
        first, second = pair_pack(query[0:128], query[128:256])
        for offset, block in ((0, first), (1, second)):
            head = pair * 2 + offset
            send[2 * head, 256:384, :] = bfloat(block)
            send[2 * head + 1, 256:384, :] = bfloat(block)
    for head in range(HEADS):
        rows = slice(512 + head * 128, 512 + head * 128 + 128)
        bias = small[3:4, (head // 2) * 128 : (head // 2) * 128 + 128]
        if head % 2 == 0:
            bias = pltpu.roll(jnp.broadcast_to(bias, (8, 128)), HEAD_DIM, 1)[0:1]
        bias = jnp.where(low_lanes((1, 128)), 0.0, bias)
        both = bfloat(dot(hidden, weights[rows, :], NT) + bias)
        send[2 * head, 0:256, :] = both
        send[2 * head + 1, 0:256, :] = both


def block_of(step, half):
    return 2 * step + ((step & 1) ^ half)


def doc_start(position, first_end, second_end):
    return jnp.where(
        position >= second_end, second_end, jnp.where(position >= first_end, first_end, 0)
    )


def packed_t(block):
    turned = block.T
    return jnp.concatenate([turned[0:HEAD_DIM], turned[HEAD_DIM:128]], axis=1)


def chunk_loops(step, block, first_end, second_end, body, state):
    first_row = block * ROWS
    low = doc_start(first_row, first_end, second_end) // CHUNK
    last_start = doc_start(first_row + ROWS - 1, first_end, second_end)
    edge = jnp.minimum(step, (last_start + CHUNK - 1) // CHUNK)
    edge = jnp.maximum(edge, low)
    masked_count = edge - low + 1

    def masked_body(index, state):
        chunk = jnp.where(index == 0, step, low + index - 1)
        return body(chunk, True, state)

    state = lax.fori_loop(0, masked_count, masked_body, state)
    return lax.fori_loop(edge, step, lambda chunk, state: body(chunk, False, state), state)


def allowed_mask(chunk, block, first_end, second_end):
    key = lax.broadcasted_iota(jnp.int32, (CHUNK, ROWS), 0) + chunk * CHUNK
    position = lax.broadcasted_iota(jnp.int32, (1, ROWS), 1) + block * ROWS
    start = doc_start(position, first_end, second_end)
    return (key <= position) & (key >= start)


def attend_kernel(scalars, pieces, send, turned_out, out_t, stats, ones_t):
    half, first_end, second_end = scalars[1], scalars[3], scalars[4]

    def turn(source, _):
        columns = pl.ds(pl.multiple_of(source * ROWS, ROWS), ROWS)
        turned = f32(pieces[source, 0:256, :]).T
        turned_out[:, columns] = bfloat(turned)
        row = lax.broadcasted_iota(jnp.int32, (128, ROWS), 0)
        ones_t[:, columns] = bfloat(jnp.where(row < HEAD_DIM, 1.0, turned))
        send[source] = jnp.zeros((128, 128), jnp.bfloat16)
        return 0

    lax.fori_loop(0, 16, turn, 0)

    def one_block(step, _):
        block = block_of(step, half)
        query_t = packed_t(f32(pieces[block, 256:384, :]))
        query_t = bfloat(jnp.concatenate([query_t, jnp.zeros_like(query_t)], axis=0))

        def body(chunk, masked, state):
            run_max, total = state
            keys = pieces[pl.ds(chunk * 2, 2), 0:256, :].reshape(CHUNK, 128)
            scores = dot(keys, query_t, NN)
            if masked:
                scores = jnp.where(
                    allowed_mask(chunk, block, first_end, second_end), scores, negative_big
                )
            new_max = jnp.maximum(run_max, jnp.max(scores, axis=0, keepdims=True))
            weights = bfloat(jnp.exp2((scores - new_max) * log2_e))
            scale = jnp.exp2((run_max - new_max) * log2_e)
            columns = pl.ds(pl.multiple_of(chunk * CHUNK, CHUNK), CHUNK)
            total = total * scale + dot(ones_t[:, columns], weights, NN)
            return new_max, total

        state = (
            jnp.full((1, ROWS), negative_big, jnp.float32),
            jnp.zeros((128, ROWS), jnp.float32),
        )
        run_max, total = chunk_loops(step, block, first_end, second_end, body, state)
        row_sum = total[0:1]
        result = total[HEAD_DIM:128] / row_sum
        out_t[step] = result
        stats[step] = jnp.broadcast_to(run_max + jnp.log(row_sum), (8, ROWS))
        packed = jnp.concatenate([result[:, 0:128], result[:, 128:256]], axis=0).T
        send[block] = bfloat(packed)
        return 0

    lax.fori_loop(0, 8, one_block, 0)


def attend_back_kernel(scalars, pieces, turned, out_t, stats, grads, send, total):
    half, first_end, second_end = scalars[1], scalars[3], scalars[4]

    def clear(source, _):
        rows = pl.ds(pl.multiple_of(source * ROWS, ROWS), ROWS)
        total[rows, :] = jnp.zeros((ROWS, 128), jnp.float32)
        send[source, 256:384, :] = jnp.zeros((128, 128), jnp.bfloat16)
        return 0

    lax.fori_loop(0, 16, clear, 0)

    def one_block(step, _):
        block = block_of(step, half)
        low = low_lanes((128, 128))
        query = f32(pieces[block, 256:384, :])
        query_t = packed_t(query)
        query_t = bfloat(jnp.concatenate([query_t, jnp.zeros_like(query_t)], axis=0))
        query = bfloat(
            jnp.concatenate(
                [jnp.where(low, query, 0.0), jnp.where(low, pltpu.roll(query, HEAD_DIM, 1), 0.0)],
                axis=0,
            )
        )
        grad = f32(grads[block])
        grad_t = packed_t(grad)
        dots = jnp.sum(grad_t * out_t[step], axis=0, keepdims=True)
        grad_t = bfloat(jnp.concatenate([jnp.zeros_like(grad_t), grad_t], axis=0))
        grad = bfloat(
            jnp.concatenate(
                [jnp.where(low, 0.0, pltpu.roll(grad, HEAD_DIM, 1)), jnp.where(low, 0.0, grad)],
                axis=0,
            )
        )
        stat = stats[step][0:1]

        def body(chunk, masked, grad_query_t):
            keys = pieces[pl.ds(chunk * 2, 2), 0:256, :].reshape(CHUNK, 128)
            scores = dot(keys, query_t, NN)
            weights = jnp.exp2((scores - stat) * log2_e)
            if masked:
                weights = jnp.where(
                    allowed_mask(chunk, block, first_end, second_end), weights, 0.0
                )
            grad_weights = dot(keys, grad_t, NN)
            grad_scores = bfloat(weights * (grad_weights - dots))
            rows = pl.ds(pl.multiple_of(chunk * CHUNK, CHUNK), CHUNK)
            total[rows, :] += dot(grad_scores, query, NN) + dot(bfloat(weights), grad, NN)
            return grad_query_t + dot(turned[:, rows], grad_scores, NN)

        grad_query_t = chunk_loops(
            step, block, first_end, second_end, body, jnp.zeros((128, ROWS), jnp.float32)
        )
        grad_query_t = grad_query_t[0:HEAD_DIM] * HEAD_DIM**-0.5
        packed = jnp.concatenate([grad_query_t[:, 0:128], grad_query_t[:, 128:256]], axis=0).T
        send[block, 256:384, :] = bfloat(packed)
        return 0

    lax.fori_loop(0, 8, one_block, 0)

    def emit(source, _):
        rows = pl.ds(pl.multiple_of(source * ROWS, ROWS), ROWS)
        send[source, 0:256, :] = bfloat(total[rows, :])
        return 0

    lax.fori_loop(0, 16, emit, 0)


def middle_kernel(
    scalars, attended_in, tokens, cotangent, w_proj, w_up, w_down, small,
    out, send, grad_resid_out, grads, grad_small,
):
    first_row, mine, second_end = scalars[0] * ROWS, scalars[2], scalars[4]
    blocks = []
    for pair in range(4):
        top, bottom = pair_pack(
            f32(attended_in[4 * pair + mine]), f32(attended_in[4 * pair + 2 + mine])
        )
        blocks.append(jnp.concatenate([top, bottom], axis=0))
    attended = bfloat(jnp.concatenate(blocks, axis=1))
    residual = f32(tokens[...]) + dot(attended, w_proj[...], NT) + small[4:5, :]
    unit, scale = normed(residual)
    hidden_in = bfloat(unit * small[5:6, :] + small[6:7, :])
    position = lax.broadcasted_iota(jnp.int32, (ROWS, 1), 0) + first_row
    grad_out = jnp.where(position < second_end, f32(cotangent[...]), 0.0)
    grad_out_b = bfloat(grad_out)

    def one_tile(tile, state):
        branch, grad_hidden_in = state
        rows = pl.ds(pl.multiple_of(tile * TILE, TILE), TILE)
        up_rows = w_up[rows, :]
        down_rows = w_down[rows, :]
        hidden = dot(hidden_in, up_rows, NT) + small[pl.ds(8 + tile, 1), :]
        square = hidden * hidden
        bend = jnp.tanh(gelu_scale * hidden * (1.0 + gelu_cubic * square))
        half_open = 0.5 * (1.0 + bend)
        activated = bfloat(hidden * half_open)
        slope = half_open + 0.5 * hidden * (1.0 - bend * bend) * gelu_scale * (
            1.0 + 3.0 * gelu_cubic * square
        )
        branch = branch + dot(activated, down_rows, NN)
        grad_hidden = dot(grad_out_b, down_rows, NT) * slope
        grad_hidden_b = bfloat(grad_hidden)
        grad_hidden_in = grad_hidden_in + dot(grad_hidden_b, up_rows, NN)
        grad_small[pl.ds(8 + tile, 1), :] = jnp.sum(grad_hidden, axis=0, keepdims=True)
        grad_up = bfloat(dot(grad_hidden_b, hidden_in, TN))
        grad_down = bfloat(dot(activated, grad_out_b, TN))
        for part in range(4):
            owner = tile * 4 + part
            grads[owner, 32:160, :] = grad_up[part * 128 : part * 128 + 128]
            grads[owner, 160:288, :] = grad_down[part * 128 : part * 128 + 128]
        return branch, grad_hidden_in

    zeros = jnp.zeros((ROWS, WIDTH), jnp.float32)
    branch, grad_hidden_in = lax.fori_loop(0, HIDDEN // TILE, one_tile, (zeros, zeros))
    out[...] = bfloat(residual + branch + small[7:8, :])
    grad_norm, grad_gain, grad_bias = norm_back(unit, scale, small[5:6, :], grad_hidden_in)
    grad_resid = grad_out + grad_norm
    grad_resid_out[...] = grad_resid
    grad_resid_b = bfloat(grad_resid)
    grad_proj = bfloat(dot(grad_resid_b, attended, TN))
    for owner in range(16):
        grads[owner, 0:32, :] = grad_proj[owner * 32 : owner * 32 + 32]
    grad_small[0:4, :] = jnp.zeros((4, WIDTH), jnp.float32)
    grad_small[12:16, :] = jnp.zeros((4, WIDTH), jnp.float32)
    grad_small[4:5, :] = jnp.sum(grad_resid, axis=0, keepdims=True)
    grad_small[5:6, :] = grad_gain
    grad_small[6:7, :] = grad_bias
    grad_small[7:8, :] = jnp.sum(grad_out, axis=0, keepdims=True)
    grad_attended = f32(bfloat(dot(grad_resid_b, w_proj[...], NN)))
    for pair in range(4):
        columns = slice(pair * 128, pair * 128 + 128)
        first, second = pair_pack(grad_attended[0:128, columns], grad_attended[128:256, columns])
        for offset, block in ((0, first), (1, second)):
            send[4 * pair + 2 * offset] = bfloat(block)
            send[4 * pair + 2 * offset + 1] = bfloat(block)


def last_kernel(scalars, pieces, tokens, weights, small, grad_resid, part_small, grad_in, grads):
    mine = scalars[2]
    unit, scale = normed(f32(tokens[...]))
    hidden = bfloat(unit * small[0:1, :] + small[1:2, :])
    grad_hidden = jnp.zeros((ROWS, WIDTH), jnp.float32)
    sums_query = []
    sums_value = []

    def store(weight_grad, first_rows):
        for index, first in enumerate(first_rows):
            owner, row = divmod(first, 96)
            grads[row // 64, owner, row % 64 : row % 64 + 32, :] = weight_grad[
                index * 32 : index * 32 + 32
            ]

    for pair in range(4):
        top, bottom = pair_pack(
            f32(pieces[4 * pair + mine, 256:384, :]), f32(pieces[4 * pair + 2 + mine, 256:384, :])
        )
        grad_query = jnp.concatenate([top, bottom], axis=0)
        sums_query.append(jnp.sum(grad_query, axis=0, keepdims=True))
        grad_query = bfloat(grad_query)
        rows = slice(pair * 128, pair * 128 + 128)
        grad_hidden = grad_hidden + dot(grad_query, weights[rows, :], NN)
        store(
            bfloat(dot(grad_query, hidden, TN)), [pair * 128 + inside * 32 for inside in range(4)]
        )
    for head in range(HEADS):
        both = bfloat(f32(pieces[2 * head, 0:256, :]) + f32(pieces[2 * head + 1, 0:256, :]))
        sums_value.append(jnp.sum(f32(both), axis=0, keepdims=True))
        rows = slice(512 + head * 128, 512 + head * 128 + 128)
        grad_hidden = grad_hidden + dot(both, weights[rows, :], NN)
        first = 512 + head * HEAD_DIM
        store(
            bfloat(dot(both, hidden, TN)), [first, first + 32, first + 512, first + 512 + 32]
        )
    grad_norm, grad_gain, grad_bias = norm_back(unit, scale, small[0:1, :], grad_hidden)
    grad_in[...] = bfloat(grad_resid[...] + grad_norm)
    row = lax.broadcasted_iota(jnp.int32, (16, 128), 0)
    lane = lax.broadcasted_iota(jnp.int32, (16, 128), 1)
    for block in range(4):
        columns = slice(block * 128, block * 128 + 128)
        first = pltpu.roll(jnp.broadcast_to(sums_value[2 * block], (16, 128)), HEAD_DIM, 1)
        second = jnp.broadcast_to(sums_value[2 * block + 1], (16, 128))
        value_row = jnp.where(lane < HEAD_DIM, first, second)
        total = part_small[:, columns]
        total = jnp.where(row == 0, grad_gain[:, columns], total)
        total = jnp.where(row == 1, grad_bias[:, columns], total)
        total = jnp.where(row == 2, sums_query[block], total)
        total = jnp.where(row == 3, value_row, total)
        for inside in range(4):
            owner = block * 4 + inside
            moved = pltpu.roll(total, 128 - inside * 32, 1) if inside else total
            grads[1, owner, 32:48, 0:128] = bfloat(moved)
            grads[1, owner, 32:48, 128:512] = jnp.zeros((16, 384), jnp.bfloat16)
            grads[1, owner, 48:64, :] = jnp.zeros((16, 512), jnp.bfloat16)


def call(kernel, shapes, scratch=(), scalar=False, count=0, flops=0, moved=0):
    vmem = pl.BlockSpec(memory_space=pltpu.VMEM)
    specs = [vmem] * count
    if scalar:
        specs[0] = pl.BlockSpec(memory_space=pltpu.SMEM)
    return pl.pallas_call(
        kernel,
        out_shape=[jax.ShapeDtypeStruct(shape, kind) for shape, kind in shapes],
        in_specs=specs,
        out_specs=[vmem] * len(shapes),
        scratch_shapes=list(scratch),
        compiler_params=pltpu.CompilerParams(vmem_limit_bytes=52 * 1024 * 1024),
        cost_estimate=pl.CostEstimate(flops=flops, bytes_accessed=moved, transcendentals=0),
    )


def adam_update(weight, grad_sum, mean_old, square_old, step_rate, decay_on):
    mean_new = beta_first * mean_old + (1.0 - beta_first) * grad_sum
    square_new = beta_second * square_old + (1.0 - beta_second) * grad_sum * grad_sum
    mean_hat = mean_new / (1.0 - beta_first**STEP)
    square_hat = square_new / (1.0 - beta_second**STEP)
    weight_new = weight - step_rate * (
        mean_hat / (jnp.sqrt(square_hat) + adam_epsilon) + decay_on * weight_decay * weight
    )
    return (weight_new, mean_new, square_new)


def exchange(values):
    return lax.all_to_all(values, CTX, 0, 0, tiled=True)


def swap_cores(values):
    return lax.ppermute(values, "c", [(0, 1), (1, 0)])


def on_device(
    tokens, cotangent, lengths,
    w_qkv, w_proj, w_up, w_down, w_small,
    mean_qkv, mean_proj, mean_up, mean_down, mean_small,
    square_qkv, square_proj, square_up, square_down, square_small,
):
    core = lax.axis_index("c")
    place = lax.axis_index("z") * 4 + lax.axis_index("y")
    mine = (place ^ (place >> 1)) & 1
    lens_row = lengths[0]
    scalars = jnp.stack(
        [place, place & 1, mine, lens_row[0], lens_row[0] + lens_row[1], 0, 0, 0]
    ).astype(jnp.int32)

    later_own = bfloat(jnp.concatenate([w_proj.T, w_up.T, w_down], axis=0))
    later = lax.all_gather(later_own, CTX, axis=0, tiled=False)
    full_proj = later[:, 0:32].reshape(WIDTH, WIDTH)
    full_up = later[:, 32:160].reshape(HIDDEN, WIDTH)
    full_down = later[:, 160:288].reshape(HIDDEN, WIDTH)

    small_rows = jnp.pad(bfloat(w_small), ((0, 20), (0, WIDTH - 32)))
    first_own = jnp.concatenate([bfloat(w_qkv.T), small_rows], axis=0)
    first_half = lax.dynamic_slice_in_dim(first_own, core * 64, 64, 0)
    first_half = exchange(jnp.broadcast_to(first_half[None], (16, 64, WIDTH)))
    wide = lax.all_gather(first_half, "c", axis=0, tiled=False)

    kind = jnp.bfloat16
    send, weights, small = call(
        qkv_kernel,
        [((16, 384, 128), kind), ((1536, WIDTH), kind), ((16, WIDTH), jnp.float32)],
        count=2, flops=2 * 256 * 512 * 1536, moved=6 << 20,
    )(tokens, wide)
    pieces = exchange(send)
    send, turned, out_t, stats = call(
        attend_kernel,
        [
            ((16, 128, 128), kind),
            ((128, 4096), kind),
            ((8, HEAD_DIM, ROWS), jnp.float32),
            ((8, 8, ROWS), jnp.float32),
        ],
        [pltpu.VMEM((128, 4096), kind)],
        scalar=True, count=2, flops=36 * 512 * 256 * 2 * 256 * 2, moved=4 << 20,
    )(scalars, pieces)
    attended = exchange(send)
    out, send, grad_resid, grads_early, part_small = call(
        middle_kernel,
        [
            ((ROWS, WIDTH), kind),
            ((16, 128, 128), kind),
            ((ROWS, WIDTH), jnp.float32),
            ((16, 288, WIDTH), kind),
            ((16, WIDTH), jnp.float32),
        ],
        scalar=True, count=8, flops=2 * 256 * 512 * (3 * 512 + 6 * 2048), moved=12 << 20,
    )(scalars, attended, tokens, cotangent, full_proj, full_up, full_down, small)
    early = lax.psum_scatter(
        grads_early.reshape(16 * 288, WIDTH), CTX, scatter_dimension=0, tiled=True
    )
    grads = exchange(send)
    (send,) = call(
        attend_back_kernel,
        [((16, 384, 128), kind)],
        [pltpu.VMEM((4096, 128), jnp.float32)],
        scalar=True, count=6, flops=36 * 512 * 256 * 2 * 256 * 5, moved=5 << 20,
    )(scalars, pieces, turned, out_t, stats, grads)
    pieces = exchange(send)
    grad_in, grads_late = call(
        last_kernel,
        [((ROWS, WIDTH), kind), ((2, 16, 64, WIDTH), kind)],
        scalar=True, count=7, flops=4 * 256 * 512 * 1536, moved=8 << 20,
    )(scalars, pieces, tokens, weights, small, grad_resid, part_small)

    other = swap_cores(lax.dynamic_index_in_dim(grads_late, 1 - core, 0, keepdims=False))
    own = lax.dynamic_index_in_dim(grads_late, core, 0, keepdims=False)
    late = exchange(bfloat(f32(own) + f32(other)))
    late = bfloat(jnp.sum(f32(late), axis=0))
    early_other = swap_cores(lax.dynamic_slice_in_dim(early, (1 - core) * 144, 144, 0))
    early_own = lax.dynamic_slice_in_dim(early, core * 144, 144, 0)
    joined = jnp.concatenate([bfloat(f32(early_own) + f32(early_other)), late], axis=0)
    joined = lax.all_to_all(
        jnp.broadcast_to(joined[None], (4, 208, WIDTH)), "x", 0, 0, tiled=True
    )
    joined = bfloat(jnp.sum(f32(joined), axis=0))
    joined = f32(lax.all_gather(joined, "c", axis=0, tiled=False))
    early = joined[:, 0:144].reshape(288, WIDTH)
    late = joined[:, 144:208].reshape(128, WIDTH)
    own_qkv = late[0:96].T
    own_small = late[96:108, 0:32]
    own_proj = early[0:32].T
    own_up = early[32:160].T
    own_down = early[160:288]

    new_qkv, new_mean_qkv, new_square_qkv = adam_update(
        w_qkv, own_qkv, mean_qkv, square_qkv, 0.04, 1.0
    )
    new_proj, new_mean_proj, new_square_proj = adam_update(
        w_proj, own_proj, mean_proj, square_proj, 1.0, 1.0
    )
    new_up, new_mean_up, new_square_up = adam_update(w_up, own_up, mean_up, square_up, 0.04, 1.0)
    new_down, new_mean_down, new_square_down = adam_update(
        w_down, own_down, mean_down, square_down, 0.02, 1.0
    )
    new_small, new_mean_small, new_square_small = adam_update(
        w_small, own_small, mean_small, square_small, 2.0, 0.0
    )
    return (
        out, grad_in,
        new_qkv, new_proj, new_up, new_down, new_small,
        new_mean_qkv, new_mean_proj, new_mean_up, new_mean_down, new_mean_small,
        new_square_qkv, new_square_proj, new_square_up, new_square_down, new_square_small,
    )


def solution(mesh):
    fine = Mesh(mesh.devices.reshape(4, 2, 4, 4), ("x", "c", "z", "y"))
    rows = P(("x", "c", "z", "y"), None)
    columns = P(None, CTX)
    shards = (columns, columns, columns, P(CTX, None), columns)
    return jax.shard_map(
        on_device,
        mesh=fine,
        in_specs=(rows, rows, P(("x", "c"), None)) + shards * 3,
        out_specs=(rows, rows) + shards * 3,
        check_vma=False,
    )
```

time: 858 us -> 277 us (0.32)
  waiting for transfers between devices: 546 us -> 90.2 us
  matrix products: 78.6 us -> 0 us
  Pallas kernels: 0 us -> 67.7 us
  local copies, waits for them, and re-layouts: 84.8 us -> 18.8 us
  other arithmetic: 47 us -> 9.85 us
  starting transfers between devices: 0.46 us -> 32.7 us
  blocking collectives: 64.2 us -> 41.1 us
  loops' own time: 17.3 us -> 0 us
    reduce_scatter x4 -> x1, waiting for transfers between devices: 280 us -> 3.88 us  [on_device(): lax.psum_scatter(grads_early.reshape(16 * 288, WIDTH), CTX, scatter_dimen...]
    unnamed x13 -> x3, waiting for transfers between devices: 133 us -> 0.05 us
    dot_general x68 -> x0, matrix products: 78.6 us -> none  [the longest x16 16.8 us: block_scores(): jnp.einsum('qhd,khd->hqk', query_heads, key_heads, preferred_element_type...]
    all_to_all x0 -> x5, waiting for transfers between devices: none -> 72.1 us  [the longest x4 60.7 us: exchange(): return lax.all_to_all(values, CTX, 0, 0, tiled=True)]
    pallas_call x0 -> x5, Pallas kernels: none -> 67.7 us  [the longest x1 23.9 us: on_device(): call(attend_kernel, [((16, 128, 128), kind), ((128, 4096), kind), ((8, HE...]
    all_gather x4 -> x2, waiting for transfers between devices: 72.3 us -> 11.6 us  [the longest x1 11.6 us: on_device(): wide = lax.all_gather(first_half, 'c', axis=0, tiled=False)]
    psum x1 -> x0, waiting for transfers between devices: 60.5 us -> none  [on_device(): lax.psum(own_qkv.astype(jnp.bfloat16), 'dp').astype(jnp.float32)]
    all_to_all x0 -> x2, blocking collectives: none -> 37.2 us  [exchange(): return lax.all_to_all(values, CTX, 0, 0, tiled=True)]
  transfers between devices with their start and end apart: 11 -> 10, of which waited for: 9 -> 8; matrix products, arithmetic and copies ran while one was open for 14% -> 6% of each run, Pallas kernels for 0% -> 20%
where the time goes in v1:
time: 277 us; the launch traced here: 276 us
  waiting for transfers between devices  90.2 us (33%)
  Pallas kernels  67.7 us (24%)
  blocking collectives  41.1 us (15%)
  starting transfers between devices  32.7 us (12%)
  local copies, waits for them, and re-layouts  18.8 us (7%)
  between operations  15.4 us (6%)
  other arithmetic  9.85 us (4%)
    all_to_all x4, waiting for transfers between devices, exchange(): return lax.all_to_all(values, CTX, 0, 0, tiled=True)  60.7 us
    all_to_all x2, blocking collectives, exchange(): return lax.all_to_all(values, CTX, 0, 0, tiled=True)  37.2 us
    pallas_call x1, Pallas kernels, on_device(): call(attend_kernel, [((16, 128, 128), kind), ((128, 4096), kind), ((8, HE...  23.9 us
    pallas_call x1, Pallas kernels, on_device(): call(attend_back_kernel, [((16, 384, 128), kind)], [pltpu.VMEM((4096, 128...  22.7 us
    all_to_all x4, starting transfers between devices, exchange(): return lax.all_to_all(values, CTX, 0, 0, tiled=True)  17.9 us
    pallas_call x1, Pallas kernels, on_device(): call(middle_kernel, [((ROWS, WIDTH), kind), ((16, 128, 128), kind), ((ROW...  11.6 us
    all_gather x1, waiting for transfers between devices, on_device(): wide = lax.all_gather(first_half, 'c', axis=0, tiled=False)  11.6 us
    all_to_all x1, waiting for transfers between devices, on_device(): lax.all_to_all(jnp.broadcast_to(joined[None], (4, 208, WIDTH)), 'x', 0, 0...  11.4 us
  transfers between devices with their start and end apart: 10, of which 8 were waited for; matrix products, arithmetic and copies ran while one was open for 6% of the time, Pallas kernels for 20%

profile of v1, /device:TPU:1, one launch (start us, length us, event | category | flops | bytes accessed | tf_op | source)
XLA Modules:
  0.0 275.9 jit_solution(12922366455884008937)
XLA Ops:
  7.2 0.9 convert_bitcast_fusion.2
  8.2 0.7 convert_element_type.49
  9.1 24.8 %all_to_all.35 = bf16[16,64,512]{2,1,0:T(8,128)(2,1)} all-to-all(bf16[16,64,512]{2,1,0:T(8,128)(2,1)S(1)} %broadcast_in_dim.4), channel_id=1, replica_groups=mesh['x'=4,'c'=2,'z'=4,'y'=4] {'z','y'}, dimensions={0} | all-to-all | bytes 2097152 | tf_op jit(solution)/shard_map/all_to_all | solution.py:428
  34.2 0.8 pad_maximum_fusion
  35.0 11.6 %all-gather.7.cloned.1.call-done = bf16[32,64,512]{2,1,0:T(8,128)(2,1)} async-done(((bf16[16,64,512]{2,1,0:T(8,128)(2,1)}), bf16[32,64,512]{2,1,0:T(8,128)(2,1)}) %all-gather.7.cloned.1.call-update) | async-done | bytes 2097168 | tf_op jit(solution)/shard_map/all_gather | solution.py:459
  46.5 4.3 %shard_map.305 = (bf16[16,384,128]{2,1,0:T(8,128)(2,1)}, bf16[1536,512]{1,0:T(8,128)(2,1)}, f32[16,512]{1,0:T(8,128)S(1)}) custom-call(bf16[256,512]{1,0:T(8,128)(2,1)S(1)} %copy-done, bf16[2,16,64,512]{3,2,1,0:T(8,128)(2,1)} %bitcast.61), custom_call_target="tpu_custom_call" | custom-call | flops 402653184 | bytes 6291456 | tf_op jit(solution)/shard_map/pallas_call | solution.py:462
  50.8 6.9 %all-to-all-start.1 = ((bf16[16,384,128]{2,1,0:T(8,128)(2,1)}), bf16[16,384,128]{2,1,0:T(8,128)(2,1)S(1)}, u32[]{:S(2)}, u32[]{:S(2)}) async-start(bf16[16,384,128]{2,1,0:T(8,128)(2,1)} %get-tuple-element.31), calls=%async_computation.1 | async-start | bytes 3145728 | tf_op jit(solution)/shard_map/all_to_all | solution.py:428
  57.8 0.6 fusion.14
  59.7 0.7 stack.19.scalars
  60.4 26.6 %all-to-all-done.1.pieces = bf16[16,384,128]{2,1,0:T(8,128)(2,1)S(1)} async-done(((bf16[16,384,128]{2,1,0:T(8,128)(2,1)}), bf16[16,384,128]{2,1,0:T(8,128)(2,1)S(1)}, u32[]{:S(2)}, u32[]{:S(2)}) %all-to-all-start.1) | async-done | bytes 1572896 | tf_op jit(solution)/shard_map/all_to_all | solution.py:428
  86.9 1.2 copy-done.4
  88.1 23.9 %shard_map.306 = (bf16[16,128,128]{2,1,0:T(8,128)(2,1)}, bf16[128,4096]{1,0:T(8,128)(2,1)}, f32[8,64,256]{2,1,0:T(8,128)S(1)}, f32[8,8,256]{2,1,0:T(8,128)S(1)}) custom-call(s32[8]{0:T(128)S(1)} %stack.19.scalars, bf16[16,384,128]{2,1,0:T(8,128)(2,1)} %copy-done.4), custom_call_target="tpu_custom_call" | custom-call | flops 4831838208 | bytes 4194304 | tf_op jit(solution)/shard_map/pallas_call | solution.py:468
  112.0 3.6 %all-to-all-start.2 = ((bf16[16,128,128]{2,1,0:T(8,128)(2,1)}), bf16[16,128,128]{2,1,0:T(8,128)(2,1)S(1)}, u32[]{:S(2)}, u32[]{:S(2)}) async-start(bf16[16,128,128]{2,1,0:T(8,128)(2,1)} %get-tuple-element.32), calls=%async_computation.2 | async-start | bytes 1048576 | tf_op jit(solution)/shard_map/all_to_all | solution.py:428
  115.7 1.9 slice.54
  117.6 4.7 %fusion.13 = (bf16[16,128,512]{2,1,0:T(8,128)(2,1)}, bf16[16,128,512]{2,1,0:T(8,128)(2,1)}) fusion(bf16[16,288,512]{2,1,0:T(8,128)(2,1)} %all-gather.5.cloned.1.call-done), kind=kLoop, calls=%fused_computation.39 | loop fusion | bytes 8388608 | tf_op jit(solution)/shard_map/slice | solution.py:453
  122.3 3.5 %all-to-all-done.2.attended_in = bf16[16,128,128]{2,1,0:T(8,128)(2,1)S(1)} async-done(((bf16[16,128,128]{2,1,0:T(8,128)(2,1)}), bf16[16,128,128]{2,1,0:T(8,128)(2,1)S(1)}, u32[]{:S(2)}, u32[]{:S(2)}) %all-to-all-start.2) | async-done | bytes 524320 | tf_op jit(solution)/shard_map/all_to_all | solution.py:428
  125.8 0.8 copy-done.7
  126.7 11.6 %shard_map.307 = (bf16[256,512]{1,0:T(8,128)(2,1)}, bf16[16,128,128]{2,1,0:T(8,128)(2,1)S(1)}, f32[256,512]{1,0:T(8,128)S(1)}, bf16[16,288,512]{2,1,0:T(8,128)(2,1)}, f32[16,512]{1,0:T(8,128)S(1)}) custom-call(s32[8]{0:T(128)S(1)} %stack.19.scalars, bf16[16,128,128]{2,1,0:T(8,128)(2,1)} %copy-done.7, bf16[256,512]{1,0:T(8,128)(2,1)S(1)} %copy-done, ...), custom_call_target="tpu_custom_call" | custom-call | flops 3623878656 | bytes 12582912 | tf_op jit(solution)/shard_map/pallas_call | solution.py:480
  138.3 12.4 %all_to_all.36.grads = bf16[16,128,128]{2,1,0:T(8,128)(2,1)S(1)} all-to-all(bf16[16,128,128]{2,1,0:T(8,128)(2,1)S(1)} %get-tuple-element.38), channel_id=1, replica_groups=mesh['x'=4,'c'=2,'z'=4,'y'=4] {'z','y'}, dimensions={0} | all-to-all | bytes 1048576 | tf_op jit(solution)/shard_map/all_to_all | solution.py:428
  150.7 22.7 %shard_map.308 = bf16[16,384,128]{2,1,0:T(8,128)(2,1)} custom-call(s32[8]{0:T(128)S(1)} %stack.19.scalars, bf16[16,384,128]{2,1,0:T(8,128)(2,1)} %copy-done.4, bf16[128,4096]{1,0:T(8,128)(2,1)} %get-tuple-element.35.turned, f32[8,64,256]{2,1,0:T(8,128)S(1)} %get-tuple-element.36.out_t, f32[8,8,256]{2,1,0:T(8,128)S(1)} %get-tuple-element.37.stats, ...), custom_call_target="tpu_custom_call" | custom-call | flops 12079595520 | bytes 5242880 | tf_op jit(solution)/shard_map/pallas_call | solution.py:495
  173.4 3.7 %all-to-all-start.4 = ((bf16[16,384,128]{2,1,0:T(8,128)(2,1)}), bf16[16,384,128]{2,1,0:T(8,128)(2,1)S(1)}, u32[]{:S(2)}, u32[]{:S(2)}) async-start(bf16[16,384,128]{2,1,0:T(8,128)(2,1)} %shard_map.308), calls=%async_computation.4 | async-start | bytes 3145728 | tf_op jit(solution)/shard_map/all_to_all | solution.py:428
  177.1 23.6 %all-to-all-done.4.pieces = bf16[16,384,128]{2,1,0:T(8,128)(2,1)S(1)} async-done(((bf16[16,384,128]{2,1,0:T(8,128)(2,1)}), bf16[16,384,128]{2,1,0:T(8,128)(2,1)S(1)}, u32[]{:S(2)}, u32[]{:S(2)}) %all-to-all-start.4) | async-done | bytes 1572896 | tf_op jit(solution)/shard_map/all_to_all | solution.py:428
  200.7 1.2 copy-done.2
  201.9 5.3 %shard_map.309 = (bf16[256,512]{1,0:T(8,128)(2,1)}, bf16[2,16,64,512]{3,2,1,0:T(8,128)(2,1)}) custom-call(s32[8]{0:T(128)S(1)} %stack.19.scalars, bf16[16,384,128]{2,1,0:T(8,128)(2,1)} %copy-done.2, bf16[256,512]{1,0:T(8,128)(2,1)S(1)} %copy-done, bf16[1536,512]{1,0:T(8,128)(2,1)} %get-tuple-element.39.weights, f32[16,512]{1,0:T(8,128)S(1)} %get-tuple-element.33.small, ...), custom_call_target="tpu_custom_call" | custom-call | flops 805306368 | bytes 8388608 | tf_op jit(solution)/shard_map/pallas_call | solution.py:502
  207.2 2.5 dynamic-slice_bitcast_fusion
  209.7 4.2 %collective-permute-start.1 = (bf16[16,64,512]{2,1,0:T(8,128)(2,1)}, bf16[16,64,512]{2,1,0:T(8,128)(2,1)}, u32[]{:S(2)}, u32[]{:S(2)}) collective-permute-start(bf16[16,64,512]{2,1,0:T(8,128)(2,1)} %dynamic-slice_bitcast_fusion), channel_id=1, source_target_pairs={{0,16},{16,0},{1,17},{17,1},{2,18},{18,2},{3,19},{19,3},{4,20},{20... | collective-permute-start | bytes 3145736 | tf_op jit(solution)/shard_map/ppermute | solution.py:432
  213.9 2.6 collective-permute-done.1
  216.5 2.6 fusion
  219.1 3.7 %all-to-all-start.5 = ((bf16[16,64,512]{2,1,0:T(8,128)(2,1)}), bf16[16,64,512]{2,1,0:T(8,128)(2,1)S(1)}, u32[]{:S(2)}, u32[]{:S(2)}) async-start(bf16[16,64,512]{2,1,0:T(8,128)(2,1)} %fusion), calls=%async_computation.6 | async-start | bytes 2097152 | tf_op jit(solution)/shard_map/all_to_all | solution.py:428
  222.7 3.9 %reduce-scatter.2.cloned.1.call-done = bf16[288,512]{1,0:T(8,128)(2,1)} async-done(((bf16[4608,512]{1,0:T(8,128)(2,1)}), bf16[288,512]{1,0:T(8,128)(2,1)}) %reduce-scatter.2.cloned.1.call-update) | async-done | bytes 294928 | tf_op jit(solution)/shard_map/reduce_scatter | solution.py:491
  226.6 0.9 constant_dynamic-slice_fusion
  227.5 6.6 %collective-permute-start = (bf16[144,512]{1,0:T(8,128)(2,1)S(1)}, bf16[144,512]{1,0:T(8,128)(2,1)S(1)}, u32[]{:S(2)}, u32[]{:S(2)}) collective-permute-start(bf16[144,512]{1,0:T(8,128)(2,1)S(1)} %constant_dynamic-slice_fusion), channel_id=1, source_target_pairs={{0,16},{16,0},{1,17},{17,1},{2,18},{18,2},{3,19},{19,3},{4,20},{20... | collective-permute-start | bytes 442376 | tf_op jit(solution)/shard_map/ppermute | solution.py:432
  234.1 7.0 %all-to-all-done.5 = bf16[16,64,512]{2,1,0:T(8,128)(2,1)S(1)} async-done(((bf16[16,64,512]{2,1,0:T(8,128)(2,1)}), bf16[16,64,512]{2,1,0:T(8,128)(2,1)S(1)}, u32[]{:S(2)}, u32[]{:S(2)}) %all-to-all-start.5) | async-done | bytes 1048608 | tf_op jit(solution)/shard_map/all_to_all | solution.py:428
  241.1 0.1 reduce_sum.24
  241.3 1.0 add_convert_fusion
  242.3 1.0 broadcast_in_dim.5
  243.3 4.0 %all-to-all-start.6 = ((bf16[4,208,512]{2,1,0:T(8,128)(2,1)}), bf16[4,208,512]{2,1,0:T(8,128)(2,1)S(1)}, u32[]{:S(2)}, u32[]{:S(2)}) async-start(bf16[4,208,512]{2,1,0:T(8,128)(2,1)} %broadcast_in_dim.5), calls=%async_computation.7 | async-start | bytes 1703936 | tf_op jit(solution)/shard_map/all_to_all | solution.py:515
  247.6 11.4 %all-to-all-done.6 = bf16[4,208,512]{2,1,0:T(8,128)(2,1)S(1)} async-done(((bf16[4,208,512]{2,1,0:T(8,128)(2,1)}), bf16[4,208,512]{2,1,0:T(8,128)(2,1)S(1)}, u32[]{:S(2)}, u32[]{:S(2)}) %all-to-all-start.6) | async-done | bytes 852000 | tf_op jit(solution)/shard_map/all_to_all | solution.py:515
  259.0 0.2 reduce_sum.25
  259.2 4.0 %all-gather.1 = bf16[416,512]{1,0:T(8,128)(2,1)S(1)} all-gather(bf16[208,512]{1,0:T(8,128)(2,1)S(1)} %reduce_sum.25), channel_id=3, replica_groups=mesh['x'=4,'c'=2,'z'=4,'y'=4] {'c'}, dimensions={0}, use_global_device_ids=true | all-gather | bytes 638976 | tf_op jit(solution)/shard_map/all_gather | solution.py:519
  263.3 0.2 multiply_subtract_fusion.1
  263.6 0.8 copy.56
  264.4 0.8 copy.57
  265.3 0.8 copy.58
  266.1 1.0 multiply_subtract_fusion
  267.1 0.7 add_subtract_fusion
  267.8 0.9 multiply_subtract_fusion.2
  268.7 0.6 multiply_subtract_fusion.3
  (63 shorter events, 1.0 us)
Async XLA Ops:
  7.2 39.4 %all-gather.7.cloned.1.call-start = ((), (), s32[]{:S(2)}) async-start(), calls=%async_computation.10 | async-start | bytes 3145728 | tf_op jit(solution)/shard_map/all_gather | solution.py:459
  9.0 25.0 %copy-start.12 = (f32[512,128]{1,0:T(8,128)S(1)}, f32[512,128]{1,0:T(8,128)}, u32[]{:S(2)}) copy-start(f32[512,128]{1,0:T(8,128)} %param.23) | copy-start | bytes 786436
  9.1 25.0 %copy-start.10 = (f32[512,32]{0,1:T(8,128)S(1)}, f32[512,32]{0,1:T(8,128)}, u32[]{:S(2)}) copy-start(f32[512,32]{0,1:T(8,128)} %param.22) | copy-start | bytes 196612
  9.1 25.1 %copy-start.5 = (f32[128,512]{1,0:T(8,128)S(1)}, f32[128,512]{1,0:T(8,128)}, u32[]{:S(2)}) copy-start(f32[128,512]{1,0:T(8,128)} %param.24) | copy-start | bytes 786436
  33.9 12.7 %copy-start = (bf16[256,512]{1,0:T(8,128)(2,1)S(1)}, bf16[256,512]{1,0:T(8,128)(2,1)}, u32[]{:S(2)}) copy-start(bf16[256,512]{1,0:T(8,128)(2,1)} %tokens.5) | copy-start | bytes 786436
  33.9 81.8 %all-gather.5.cloned.1.call-start = ((), (), s32[]{:S(2)}) async-start(), calls=%async_computation.8 | async-start | bytes 5013504 | tf_op jit(solution)/shard_map/all_gather | solution.py:450
  50.8 7.0 %copy-start.22 = (s32[1,2]{1,0:T(1,128)S(1)}, s32[1,2]{1,0:T(1,128)}, u32[]{:S(2)}) copy-start(s32[1,2]{1,0:T(1,128)} %param.20) | copy-start | bytes 28
  50.8 36.1 %all-to-all-start.1 = ((bf16[16,384,128]{2,1,0:T(8,128)(2,1)}), bf16[16,384,128]{2,1,0:T(8,128)(2,1)S(1)}, u32[]{:S(2)}, u32[]{:S(2)}) async-start(bf16[16,384,128]{2,1,0:T(8,128)(2,1)} %get-tuple-element.31), calls=%async_computation.1 | async-start | bytes 3145728 | tf_op jit(solution)/shard_map/all_to_all | solution.py:428
  86.9 1.2 copy-start.4
  112.0 13.8 %all-to-all-start.2 = ((bf16[16,128,128]{2,1,0:T(8,128)(2,1)}), bf16[16,128,128]{2,1,0:T(8,128)(2,1)S(1)}, u32[]{:S(2)}, u32[]{:S(2)}) async-start(bf16[16,128,128]{2,1,0:T(8,128)(2,1)} %get-tuple-element.32), calls=%async_computation.2 | async-start | bytes 1048576 | tf_op jit(solution)/shard_map/all_to_all | solution.py:428
  115.6 111.0 %reduce-scatter.2.cloned.1.call-start = ((), (), s32[]{:S(2)}) async-start(), calls=%async_computation.9 | async-start | bytes 5013504 | tf_op jit(solution)/shard_map/reduce_scatter | solution.py:491
  117.6 9.1 %copy-start.1 = (bf16[256,512]{1,0:T(8,128)(2,1)S(1)}, bf16[256,512]{1,0:T(8,128)(2,1)}, u32[]{:S(2)}) copy-start(bf16[256,512]{1,0:T(8,128)(2,1)} %cotangent.1) | copy-start | bytes 786436
  125.8 0.8 copy-start.7
  173.4 27.3 %all-to-all-start.4 = ((bf16[16,384,128]{2,1,0:T(8,128)(2,1)}), bf16[16,384,128]{2,1,0:T(8,128)(2,1)S(1)}, u32[]{:S(2)}, u32[]{:S(2)}) async-start(bf16[16,384,128]{2,1,0:T(8,128)(2,1)} %shard_map.308), calls=%async_computation.4 | async-start | bytes 3145728 | tf_op jit(solution)/shard_map/all_to_all | solution.py:428
  200.7 1.2 copy-start.2
  207.2 9.3 %copy-start.3 = (bf16[2,16,64,512]{3,2,1,0:T(8,128)(2,1)S(1)}, bf16[2,16,64,512]{3,2,1,0:T(8,128)(2,1)}, u32[]{:S(2)}) copy-start(bf16[2,16,64,512]{3,2,1,0:T(8,128)(2,1)} %get-tuple-element.44) | copy-start | bytes 6291460
  209.7 6.8 %collective-permute-start.1 = (bf16[16,64,512]{2,1,0:T(8,128)(2,1)}, bf16[16,64,512]{2,1,0:T(8,128)(2,1)}, u32[]{:S(2)}, u32[]{:S(2)}) collective-permute-start(bf16[16,64,512]{2,1,0:T(8,128)(2,1)} %dynamic-slice_bitcast_fusion), channel_id=1, source_target_pairs={{0,16},{16,0},{1,17},{17,1},{2,18},{18,2},{3,19},{19,3},{4,20},{20... | collective-permute-start | bytes 3145736 | tf_op jit(solution)/shard_map/ppermute | solution.py:432
  219.1 22.0 %all-to-all-start.5 = ((bf16[16,64,512]{2,1,0:T(8,128)(2,1)}), bf16[16,64,512]{2,1,0:T(8,128)(2,1)S(1)}, u32[]{:S(2)}, u32[]{:S(2)}) async-start(bf16[16,64,512]{2,1,0:T(8,128)(2,1)} %fusion), calls=%async_computation.6 | async-start | bytes 2097152 | tf_op jit(solution)/shard_map/all_to_all | solution.py:428
  227.5 13.7 %collective-permute-start = (bf16[144,512]{1,0:T(8,128)(2,1)S(1)}, bf16[144,512]{1,0:T(8,128)(2,1)S(1)}, u32[]{:S(2)}, u32[]{:S(2)}) collective-permute-start(bf16[144,512]{1,0:T(8,128)(2,1)S(1)} %constant_dynamic-slice_fusion), channel_id=1, source_target_pairs={{0,16},{16,0},{1,17},{17,1},{2,18},{18,2},{3,19},{19,3},{4,20},{20... | collective-permute-start | bytes 442376 | tf_op jit(solution)/shard_map/ppermute | solution.py:432
  241.2 6.1 %copy-start.13 = (f32[512,128]{1,0:T(8,128)S(1)}, f32[512,128]{1,0:T(8,128)}, u32[]{:S(2)}) copy-start(f32[512,128]{1,0:T(8,128)} %param.28) | copy-start | bytes 786436
  241.3 6.2 %copy-start.14 = (f32[512,128]{1,0:T(8,128)S(1)}, f32[512,128]{1,0:T(8,128)}, u32[]{:S(2)}) copy-start(f32[512,128]{1,0:T(8,128)} %param.33) | copy-start | bytes 786436
  243.3 15.7 %all-to-all-start.6 = ((bf16[4,208,512]{2,1,0:T(8,128)(2,1)}), bf16[4,208,512]{2,1,0:T(8,128)(2,1)S(1)}, u32[]{:S(2)}, u32[]{:S(2)}) async-start(bf16[4,208,512]{2,1,0:T(8,128)(2,1)} %broadcast_in_dim.5), calls=%async_computation.7 | async-start | bytes 1703936 | tf_op jit(solution)/shard_map/all_to_all | solution.py:515
  263.2 2.9 %copy-start.8 = (f32[128,512]{1,0:T(8,128)S(1)}, f32[128,512]{1,0:T(8,128)}, u32[]{:S(2)}) copy-start(f32[128,512]{1,0:T(8,128)} %param.29) | copy-start | bytes 786436
  263.3 2.9 %copy-start.9 = (f32[128,512]{1,0:T(8,128)S(1)}, f32[128,512]{1,0:T(8,128)}, u32[]{:S(2)}) copy-start(f32[128,512]{1,0:T(8,128)} %param.34) | copy-start | bytes 786436
  263.5 3.6 %copy-start.11 = (f32[512,32]{0,1:T(8,128)S(1)}, f32[512,32]{0,1:T(8,128)}, u32[]{:S(2)}) copy-start(f32[512,32]{0,1:T(8,128)} %param.22) | copy-start | bytes 196612
  263.5 3.6 %copy-start.17 = (f32[512,32]{0,1:T(8,128)S(1)}, f32[512,32]{0,1:T(8,128)}, u32[]{:S(2)}) copy-start(f32[512,32]{0,1:T(8,128)} %param.27) | copy-start | bytes 196612
  263.5 3.6 %copy-start.18 = (f32[512,32]{0,1:T(8,128)S(1)}, f32[512,32]{0,1:T(8,128)}, u32[]{:S(2)}) copy-start(f32[512,32]{0,1:T(8,128)} %param.32) | copy-start | bytes 196612
  263.6 4.3 %copy-start.6 = (f32[512,96]{0,1:T(8,128)S(1)}, f32[512,96]{0,1:T(8,128)}, u32[]{:S(2)}) copy-start(f32[512,96]{0,1:T(8,128)} %param.21) | copy-start | bytes 589828
  263.6 4.3 %copy-start.15 = (f32[512,96]{0,1:T(8,128)S(1)}, f32[512,96]{0,1:T(8,128)}, u32[]{:S(2)}) copy-start(f32[512,96]{0,1:T(8,128)} %param.26) | copy-start | bytes 589828
  263.6 4.3 %copy-start.16 = (f32[512,96]{0,1:T(8,128)S(1)}, f32[512,96]{0,1:T(8,128)}, u32[]{:S(2)}) copy-start(f32[512,96]{0,1:T(8,128)} %param.31) | copy-start | bytes 589828
  265.3 3.5 %copy-start.19 = (f32[12,32]{1,0:T(8,128)S(1)}, f32[12,32]{1,0:T(8,128)}, u32[]{:S(2)}) copy-start(f32[12,32]{1,0:T(8,128)} %param.25) | copy-start | bytes 4612
  265.3 3.5 %copy-start.20 = (f32[12,32]{1,0:T(8,128)S(1)}, f32[12,32]{1,0:T(8,128)}, u32[]{:S(2)}) copy-start(f32[12,32]{1,0:T(8,128)} %param.30) | copy-start | bytes 4612
  265.3 3.5 %copy-start.21 = (f32[12,32]{1,0:T(8,128)S(1)}, f32[12,32]{1,0:T(8,128)}, u32[]{:S(2)}) copy-start(f32[12,32]{1,0:T(8,128)} %param.35) | copy-start | bytes 4612
Sparse Core Ops, SparseCore 0:
  34.0 12.4 all-gather.6
  48.7 66.7 all-gather.4
  138.4 88.1 reduce-scatter.1

commit v2 on v1

v2 whole, which is shorter than its diff:
```python
import functools
import jax
import jax.numpy as jnp
from jax import lax
from jax.experimental import pallas as pl
from jax.experimental.pallas import tpu as pltpu
from jax.sharding import Mesh, PartitionSpec as P

HEADS = 8
HEAD_DIM = 64
STEP = 10
WIDTH = 512
HIDDEN = 2048
ROWS = 256
HALF = 128
CHUNK = 512
TILE = 512

epsilon = 1e-05
negative_big = -1e30
beta_first = 0.9
beta_second = 0.95
adam_epsilon = 1e-08
weight_decay = 0.1
gelu_scale = 0.7978845608028654
gelu_cubic = 0.044715
log2_e = 1.4426950408889634

NN = (((1,), (0,)), ((), ()))
NT = (((1,), (1,)), ((), ()))
TN = (((0,), (0,)), ((), ()))
CTX = ("z", "y")


def dot(left, right, dims):
    return lax.dot_general(left, right, dims, preferred_element_type=jnp.float32)


def bfloat(values):
    return values.astype(jnp.bfloat16)


def f32(values):
    return values.astype(jnp.float32)


def normed(values):
    center = values - jnp.mean(values, axis=-1, keepdims=True)
    spread = jnp.mean(center * center, axis=-1, keepdims=True)
    scale = lax.rsqrt(spread + epsilon)
    return center * scale, scale


def norm_back(unit, scale, gain, grad):
    scaled = grad * gain
    first = jnp.mean(scaled, axis=-1, keepdims=True)
    second = jnp.mean(scaled * unit, axis=-1, keepdims=True)
    grad_values = (scaled - first - unit * second) * scale
    grad_gain = jnp.sum(grad * unit, axis=0, keepdims=True)
    grad_bias = jnp.sum(grad, axis=0, keepdims=True)
    return grad_values, grad_gain, grad_bias


def low_lanes(shape):
    return lax.broadcasted_iota(jnp.int32, shape, 1) < HEAD_DIM


def fetch(pairs, done):
    copies = [
        pltpu.make_async_copy(source, target, done.at[index])
        for index, (source, target) in enumerate(pairs)
    ]
    for copy in copies:
        copy.start()
    return copies


def mixed_rows(core, own, other):
    keep = own[pl.ds(pl.multiple_of(core * HALF, HALF), HALF), :]
    first = jnp.where(core == 0, keep, other)
    second = jnp.where(core == 0, other, keep)
    return jnp.concatenate([first, second], axis=0)


def pair_pack(top, bottom):
    low = low_lanes(top.shape)
    first = jnp.where(low, top, pltpu.roll(bottom, HEAD_DIM, 1))
    second = jnp.where(low, pltpu.roll(top, HEAD_DIM, 1), bottom)
    return first, second


def gather_kernel(
    scalars, tokens_in, cotangent_in, qkv_in, proj_in, up_in, down_in, small_in, send, rows_out,
    rows, qkv, proj, up, down, small, block, small_block, done,
):
    core = scalars[0]
    lanes = pl.ds(pl.multiple_of(scalars[1] * 128, 128), 128)
    away = pl.ds(pl.multiple_of((1 - core) * HALF, HALF), HALF)
    pairs = (
        (qkv_in, qkv), (up_in, up), (down_in, down), (proj_in, proj), (small_in, small),
        (tokens_in.at[away], rows.at[0]), (cotangent_in.at[away], rows.at[1]),
    )
    for copy in fetch(pairs, done):
        copy.wait()
    first_core = core == 0
    rows_out[...] = rows[...]
    small_block[...] = jnp.zeros((16, 128), jnp.float32)
    small_block[0:12, 0:32] = small[...]
    for part in range(4):
        columns = slice(part * 128, part * 128 + 128)
        tail = small_block[...] if part == 0 else jnp.zeros((16, 128), jnp.float32)
        second = jnp.concatenate([qkv[64:96, columns], tail, jnp.zeros((16, 128), jnp.float32)])
        half = jnp.where(first_core, qkv[0:64, columns], second)
        block[part * 64 : part * 64 + 64, :] = bfloat(half)
    half = jnp.where(first_core, up[lanes, :].T, down[:, lanes])
    block[256:384, :] = bfloat(half)
    half = jnp.where(first_core, proj[0:16, lanes], proj[16:32, lanes])
    block[384:400, :] = bfloat(half)
    for owner in range(16):
        send[owner] = block[...]


def qkv_kernel(
    scalars, tokens_in, rows_in, wide_own, wide_other, send, weights_out, small_out,
    tokens, rows_other, weights, small, done, stored,
):
    copies = fetch(((tokens_in, tokens), (rows_in, rows_other)), done)
    first_core = scalars[0] == 0

    def wide(half, owner, part, first, count):
        rows = slice(part * 64 + first, part * 64 + first + count)
        own, other = wide_own[owner, rows, :], wide_other[owner, rows, :]
        return jnp.where(first_core, own, other) if half == 0 else jnp.where(first_core, other, own)

    for owner in range(16):
        for piece in range(3):
            first = owner * 96 + piece * 32
            part, offset = divmod(first, 512)
            if part == 0:
                target = first
            else:
                head, inside = divmod(offset, HEAD_DIM)
                target = 512 + head * 128 + (part - 1) * HEAD_DIM + inside
            half, row = divmod(piece * 32, 64)
            for lanes in range(4):
                weights[target : target + 32, lanes * 128 : lanes * 128 + 128] = wide(
                    half, owner, lanes, row, 32
                )
    lane = lax.broadcasted_iota(jnp.int32, (16, 128), 1)
    for block in range(4):
        total = jnp.zeros((16, 128), jnp.float32)
        for inside in range(4):
            piece = f32(wide(1, block * 4 + inside, 0, 32, 16))
            moved = pltpu.roll(piece, inside * 32, 1) if inside else piece
            keep = (lane >= inside * 32) & (lane < inside * 32 + 32)
            total = jnp.where(keep, moved, total)
        small[:, block * 128 : block * 128 + 128] = total
    stores = fetch(((weights, weights_out), (small, small_out)), stored)
    for copy in copies:
        copy.wait()
    unit, _ = normed(f32(mixed_rows(scalars[0], tokens, rows_other[0])))
    hidden = bfloat(unit * small[0:1, :] + small[1:2, :])
    for pair in range(4):
        columns = slice(pair * 128, pair * 128 + 128)
        query = dot(hidden, weights[columns, :], NT) + small[2:3, columns]
        query = f32(bfloat(query)) * HEAD_DIM**-0.5
        for group in range(2):
            rows = group * HALF
            blocks = pair_pack(query[rows : rows + 64], query[rows + 64 : rows + 128])
            for offset, block in enumerate(blocks):
                send[group * 8 + pair * 2 + offset, HALF : HALF + 64, :] = bfloat(block)
    for head in range(HEADS):
        rows = slice(512 + head * 128, 512 + head * 128 + 128)
        bias = small[3:4, (head // 2) * 128 : (head // 2) * 128 + 128]
        if head % 2 == 0:
            bias = pltpu.roll(jnp.broadcast_to(bias, (8, 128)), HEAD_DIM, 1)[0:1]
        bias = jnp.where(low_lanes((1, 128)), 0.0, bias)
        both = bfloat(dot(hidden, weights[rows, :], NT) + bias)
        send[head, 0:HALF, :] = both[0:HALF]
        send[8 + head, 0:HALF, :] = both[HALF:ROWS]
    for copy in stores:
        copy.wait()


def query_positions(step, core):
    lane = lax.broadcasted_iota(jnp.int32, (1, ROWS), 1)
    block = 2 * step + ((lane & 64) >> 6)
    return block * ROWS + core * HALF + (lane & 63) + ((lane & 128) >> 1)


def doc_start(position, first_end, second_end):
    return jnp.where(
        position >= second_end, second_end, jnp.where(position >= first_end, first_end, 0)
    )


def packed_t(block):
    turned = block.T
    return jnp.concatenate([turned[0:HEAD_DIM], turned[HEAD_DIM:128]], axis=1)


def chunk_loops(step, first_end, second_end, body, state):
    low = doc_start(step * CHUNK, first_end, second_end) // CHUNK
    last_start = doc_start(step * CHUNK + 2 * CHUNK - 1, first_end, second_end)
    edge = jnp.minimum(step, (last_start + CHUNK - 1) // CHUNK)
    edge = jnp.maximum(edge, low)

    def masked_body(index, state):
        chunk = jnp.where(index == 0, step, low + index - 1)
        return body(chunk, True, state)

    state = lax.fori_loop(0, edge - low + 1, masked_body, state)
    return lax.fori_loop(edge, step, lambda chunk, state: body(chunk, False, state), state)


def allowed_mask(chunk, position, first_end, second_end):
    key = lax.broadcasted_iota(jnp.int32, (CHUNK, ROWS), 0) + chunk * CHUNK
    start = doc_start(position, first_end, second_end)
    return (key <= position) & (key >= start)


def packed_block(pieces, step):
    return jnp.concatenate(
        [f32(pieces[2 * step, HALF : HALF + 64, :]), f32(pieces[2 * step + 1, HALF : HALF + 64, :])],
        axis=0,
    )


def doc_ends(scalars, lens_own, lens_other, group):
    own = scalars[0] == group
    first = jnp.where(own, lens_own[0, 0], lens_other[0, 0])
    return first, first + jnp.where(own, lens_own[0, 1], lens_other[0, 1])


def attend_kernel(
    scalars, lens_own, lens_other, pieces, others,
    send, keys_hbm, turned_hbm, out_hbm, stats_hbm,
    keys_out, turned_out, out_t, stats, ones_t, done,
):
    core = scalars[0]
    first_end, second_end = doc_ends(scalars, lens_own, lens_other, scalars[2] // HEADS)

    def turn(source, _):
        columns = pl.ds(pl.multiple_of(source * ROWS, ROWS), ROWS)
        own, other = pieces[source, 0:HALF, :], others[source, 0:HALF, :]
        first, second = jnp.where(core == 0, own, other), jnp.where(core == 0, other, own)
        keys = jnp.concatenate([first, second], axis=0)
        keys_out[columns, :] = keys
        turned = f32(keys).T
        turned_out[:, columns] = bfloat(turned)
        row = lax.broadcasted_iota(jnp.int32, (128, ROWS), 0)
        ones_t[:, columns] = bfloat(jnp.where(row < HEAD_DIM, 1.0, turned))
        return 0

    lax.fori_loop(0, 16, turn, 0)
    stores = fetch(((keys_out, keys_hbm), (turned_out, turned_hbm)), done)

    def load_query(step):
        query_t = packed_t(packed_block(pieces, step))
        return bfloat(jnp.concatenate([query_t, jnp.zeros_like(query_t)], axis=0))

    def one_pair(pair, _):
        step = 2 * pair
        positions = tuple(query_positions(step + index, core) for index in range(2))
        queries = tuple(load_query(step + index) for index in range(2))

        def advance(chunk, masked, which, state):
            new_state = []
            columns = pl.ds(pl.multiple_of(chunk * CHUNK, CHUNK), CHUNK)
            keys = keys_out[columns, :]
            values = ones_t[:, columns]
            scores = [dot(keys, queries[index], NN) for index in which]
            for index, score, (run_max, total) in zip(which, scores, state):
                if masked:
                    allowed = allowed_mask(chunk, positions[index], first_end, second_end)
                    score = jnp.where(allowed, score, negative_big)
                new_max = jnp.maximum(run_max, jnp.max(score, axis=0, keepdims=True))
                weights = bfloat(jnp.exp2((score - new_max) * log2_e))
                scale = jnp.exp2((run_max - new_max) * log2_e)
                new_state.append((new_max, total * scale + dot(values, weights, NN)))
            return tuple(new_state)

        start = (
            jnp.full((1, ROWS), negative_big, jnp.float32),
            jnp.zeros((128, ROWS), jnp.float32),
        )
        state = chunk_loops(
            step, first_end, second_end,
            lambda chunk, masked, state: advance(chunk, masked, (0, 1), state),
            (start, start),
        )
        state = (state[0],) + advance(step + 1, True, (1,), state[1:])
        for index, (run_max, total) in enumerate(state):
            row_sum = total[0:1]
            result = total[HEAD_DIM:128] / row_sum
            out_t[step + index] = result
            stats[step + index] = jnp.broadcast_to(run_max + jnp.log(row_sum), (8, ROWS))
            packed = jnp.concatenate([result[:, 0:128], result[:, 128:256]], axis=0).T
            send[2 * (step + index)] = bfloat(packed[0:64])
            send[2 * (step + index) + 1] = bfloat(packed[64:128])
        return 0

    lax.fori_loop(0, 4, one_pair, 0)
    stores += fetch(((out_t, out_hbm), (stats, stats_hbm)), done.at[pl.ds(2, 2)])
    for copy in stores:
        copy.wait()


def attend_back_kernel(
    scalars, lens_own, lens_other, pieces, keys_hbm, turned_hbm, out_hbm, stats_hbm, grads,
    send, send_core, key_rows, turned, out_t, stats, total, done,
):
    copies = fetch(
        ((keys_hbm, key_rows), (turned_hbm, turned), (out_hbm, out_t), (stats_hbm, stats)), done
    )
    core = scalars[0]
    first_end, second_end = doc_ends(scalars, lens_own, lens_other, scalars[2] // HEADS)

    def clear(source, _):
        rows = pl.ds(pl.multiple_of(source * ROWS, ROWS), ROWS)
        total[rows, :] = jnp.zeros((ROWS, 128), jnp.float32)
        return 0

    lax.fori_loop(0, 16, clear, 0)
    for copy in copies:
        copy.wait()

    low = low_lanes((128, 128))

    def load_block(step):
        query = packed_block(pieces, step)
        query_t = packed_t(query)
        query_t = bfloat(jnp.concatenate([query_t, jnp.zeros_like(query_t)], axis=0))
        query = bfloat(
            jnp.concatenate(
                [jnp.where(low, query, 0.0), jnp.where(low, pltpu.roll(query, HEAD_DIM, 1), 0.0)],
                axis=0,
            )
        )
        grad = jnp.concatenate([f32(grads[2 * step]), f32(grads[2 * step + 1])], axis=0)
        grad_t = packed_t(grad)
        dots = jnp.sum(grad_t * out_t[step], axis=0, keepdims=True)
        grad_t = bfloat(jnp.concatenate([jnp.zeros_like(grad_t), grad_t], axis=0))
        grad = bfloat(
            jnp.concatenate(
                [jnp.where(low, 0.0, pltpu.roll(grad, HEAD_DIM, 1)), jnp.where(low, 0.0, grad)],
                axis=0,
            )
        )
        return query_t, grad_t, query, grad, dots, stats[step][0:1]

    def one_pair(pair, _):
        step = 2 * pair
        positions = tuple(query_positions(step + index, core) for index in range(2))
        loaded = tuple(load_block(step + index) for index in range(2))

        def advance(chunk, masked, which, state):
            rows = pl.ds(pl.multiple_of(chunk * CHUNK, CHUNK), CHUNK)
            keys = key_rows[rows, :]
            keys_t = turned[:, rows]
            scores = [dot(keys, loaded[index][0], NN) for index in which]
            grad_weights = [dot(keys, loaded[index][1], NN) for index in which]
            left, right, new_state = [], [], []
            for place, index in enumerate(which):
                _, _, query, grad, dots, stat = loaded[index]
                weights = jnp.exp2((scores[place] - stat) * log2_e)
                if masked:
                    allowed = allowed_mask(chunk, positions[index], first_end, second_end)
                    weights = jnp.where(allowed, weights, 0.0)
                grad_scores = bfloat(weights * (grad_weights[place] - dots))
                left += [grad_scores, bfloat(weights)]
                right += [query, grad]
                new_state.append(state[place] + dot(keys_t, grad_scores, NN))
            total[rows, :] += dot(jnp.concatenate(left, axis=1), jnp.concatenate(right, axis=0), NN)
            return tuple(new_state)

        start = jnp.zeros((128, ROWS), jnp.float32)
        state = chunk_loops(
            step, first_end, second_end,
            lambda chunk, masked, state: advance(chunk, masked, (0, 1), state),
            (start, start),
        )
        state = (state[0],) + advance(step + 1, True, (1,), state[1:])
        for index, grad_query_t in enumerate(state):
            turn = grad_query_t[0:HEAD_DIM] * HEAD_DIM**-0.5
            packed = jnp.concatenate([turn[:, 0:128], turn[:, 128:256]], axis=0).T
            send[2 * (step + index), HALF : HALF + 64, :] = bfloat(packed[0:64])
            send[2 * (step + index) + 1, HALF : HALF + 64, :] = bfloat(packed[64:128])
        return 0

    lax.fori_loop(0, 4, one_pair, 0)

    def emit(source, _):
        mine = pl.ds(pl.multiple_of(source * ROWS + core * HALF, HALF), HALF)
        away = pl.ds(pl.multiple_of(source * ROWS + (1 - core) * HALF, HALF), HALF)
        send[source, 0:HALF, :] = bfloat(total[mine, :])
        send_core[source] = bfloat(total[away, :])
        return 0

    lax.fori_loop(0, 16, emit, 0)


def middle_kernel(
    scalars, lens_own, lens_other, attended_in, tokens_in, cotangent_in, rows_in, later_in,
    later_other, small_in,
    out_own, out_away, send, grad_resid_hbm, small_hbm, grads_out,
    w_proj, grads, tokens, cotangent, rows_other, later_own, small, grad_resid_out, grad_small,
    done, fetched,
):
    pairs = (
        (later_in, later_own), (tokens_in, tokens), (rows_in, rows_other), (small_in, small),
        (cotangent_in, cotangent),
    )
    copies = fetch(pairs, fetched)
    core = scalars[0]
    first_core = core == 0
    slots = (core, 1 - core)
    for copy in copies:
        copy.wait()
    for owner in range(16):
        for lanes in range(4):
            columns = slice(lanes * 128, lanes * 128 + 128)
            own = later_own[lanes, owner, 128:144, :]
            other = later_other[lanes, owner, 128:144, :]
            first = owner * 32
            w_proj[first : first + 16, columns] = jnp.where(first_core, own, other)
            w_proj[first + 16 : first + 32, columns] = jnp.where(first_core, other, own)
    blocks = []
    for pair in range(4):
        parts = []
        for group in range(2):
            head = group * 8 + pair * 2
            parts += pair_pack(f32(attended_in[head]), f32(attended_in[head + 1]))
        blocks.append(jnp.concatenate(parts, axis=0))
    attended = bfloat(jnp.concatenate(blocks, axis=1))
    residual = f32(mixed_rows(core, tokens, rows_other[0])) + dot(attended, w_proj[...], NT) + small[4:5, :]
    unit, scale = normed(residual)
    hidden_in = bfloat(unit * small[5:6, :] + small[6:7, :])
    row = lax.broadcasted_iota(jnp.int32, (ROWS, 1), 0)
    position = (row & (HALF - 1)) + scalars[2] * ROWS + core * HALF
    _, first_live = doc_ends(scalars, lens_own, lens_other, 0)
    _, second_live = doc_ends(scalars, lens_own, lens_other, 1)
    live = position < jnp.where(row < HALF, first_live, second_live)
    grad_out = jnp.where(live, f32(mixed_rows(core, cotangent, rows_other[1])), 0.0)
    grad_out_b = bfloat(grad_out)

    def one_tile(tile, state):
        branch, grad_hidden_in = state
        owners = pl.ds(tile * 4, 4)
        own, other = (
            jnp.concatenate(
                [part[lanes, owners, 0:128, :].reshape(TILE, 128) for lanes in range(4)], axis=1
            )
            for part in (later_own, later_other)
        )
        up_rows = jnp.where(first_core, own, other)
        down_rows = jnp.where(first_core, other, own)
        hidden = dot(hidden_in, up_rows, NT) + small[pl.ds(8 + tile, 1), :]
        square = hidden * hidden
        bend = jnp.tanh(gelu_scale * hidden * (1.0 + gelu_cubic * square))
        half_open = 0.5 * (1.0 + bend)
        activated = bfloat(hidden * half_open)
        slope = half_open + 0.5 * hidden * (1.0 - bend * bend) * gelu_scale * (
            1.0 + 3.0 * gelu_cubic * square
        )
        branch = branch + dot(activated, down_rows, NN)
        grad_hidden = dot(grad_out_b, down_rows, NT) * slope
        grad_hidden_b = bfloat(grad_hidden)
        grad_hidden_in = grad_hidden_in + dot(grad_hidden_b, up_rows, NN)
        grad_small[pl.ds(8 + tile, 1), :] = jnp.sum(grad_hidden, axis=0, keepdims=True)
        grad_up = bfloat(dot(grad_hidden_b, hidden_in, TN))
        grad_down = bfloat(dot(activated, grad_out_b, TN))
        for lanes in range(4):
            columns = slice(lanes * 128, lanes * 128 + 128)
            grads[lanes, slots[0], owners, 0:128, :] = grad_up[:, columns].reshape(4, 128, 128)
            grads[lanes, slots[1], owners, 0:128, :] = grad_down[:, columns].reshape(4, 128, 128)
        here = grads.at[:, :, owners, 0:128, :]
        pltpu.make_async_copy(here, grads_out.at[:, :, owners, 0:128, :], done.at[tile]).start()
        return branch, grad_hidden_in

    zeros = jnp.zeros((ROWS, WIDTH), jnp.float32)
    branch, grad_hidden_in = lax.fori_loop(0, HIDDEN // TILE, one_tile, (zeros, zeros))
    out = bfloat(residual + branch + small[7:8, :])
    out_own[...] = jnp.where(first_core, out[0:HALF], out[HALF:ROWS])
    out_away[...] = jnp.where(first_core, out[HALF:ROWS], out[0:HALF])
    grad_norm, grad_gain, grad_bias = norm_back(unit, scale, small[5:6, :], grad_hidden_in)
    grad_resid = grad_out + grad_norm
    grad_resid_out[...] = grad_resid
    grad_resid_b = bfloat(grad_resid)
    grad_proj = bfloat(dot(grad_resid_b, attended, TN)).reshape(16, 32, WIDTH)
    for lanes in range(4):
        columns = slice(lanes * 128, lanes * 128 + 128)
        grads[lanes, slots[0], :, 128:144, :] = grad_proj[:, 0:16, columns]
        grads[lanes, slots[1], :, 128:144, :] = grad_proj[:, 16:32, columns]
    tail = pltpu.make_async_copy(
        grads.at[:, :, :, 128:144, :], grads_out.at[:, :, :, 128:144, :], done.at[4]
    )
    tail.start()
    grad_small[0:4, :] = jnp.zeros((4, WIDTH), jnp.float32)
    grad_small[12:16, :] = jnp.zeros((4, WIDTH), jnp.float32)
    grad_small[4:5, :] = jnp.sum(grad_resid, axis=0, keepdims=True)
    grad_small[5:6, :] = grad_gain
    grad_small[6:7, :] = grad_bias
    grad_small[7:8, :] = jnp.sum(grad_out, axis=0, keepdims=True)
    stores = fetch(
        ((grad_resid_out, grad_resid_hbm), (grad_small, small_hbm)), done.at[pl.ds(5, 2)]
    )
    grad_attended = f32(bfloat(dot(grad_resid_b, w_proj[...], NN)))
    for pair in range(4):
        columns = slice(pair * 128, pair * 128 + 128)
        for group in range(2):
            first = group * HALF
            halves = grad_attended[first : first + 64, columns], grad_attended[
                first + 64 : first + 128, columns
            ]
            for offset, block in enumerate(pair_pack(*halves)):
                send[group * 8 + pair * 2 + offset] = bfloat(block)
    for tile in range(HIDDEN // TILE):
        owners = pl.ds(tile * 4, 4)
        pltpu.make_async_copy(
            grads.at[:, :, owners, 0:128, :], grads_out.at[:, :, owners, 0:128, :], done.at[tile]
        ).wait()
    tail.wait()
    for copy in stores:
        copy.wait()


def last_kernel(
    scalars, pieces, tokens_in, rows_in, weights_in, small_in, grad_resid_in, part_in,
    grad_in_own, grad_in_away, grads_own, grads_away,
    tokens, rows_other, weights, small, grad_resid, part_small, grads, done,
):
    pairs = (
        (weights_in, weights), (tokens_in, tokens), (rows_in, rows_other), (small_in, small),
        (grad_resid_in, grad_resid), (part_in, part_small),
    )
    copies = fetch(pairs, done)
    core = scalars[0]
    slots = (core, 1 - core)
    for copy in copies:
        copy.wait()
    unit, scale = normed(f32(mixed_rows(core, tokens, rows_other[0])))
    hidden = bfloat(unit * small[0:1, :] + small[1:2, :])
    grad_hidden = jnp.zeros((ROWS, WIDTH), jnp.float32)
    sums_query = []
    sums_value = []

    def store(weight_grad, first_rows):
        for index, first in enumerate(first_rows):
            owner, row = divmod(first, 96)
            for lanes in range(4):
                place = slice(lanes * 64 + row % 64, lanes * 64 + row % 64 + 32)
                grads[slots[row // 64], owner, place, :] = weight_grad[
                    index * 32 : index * 32 + 32, lanes * 128 : lanes * 128 + 128
                ]

    for pair in range(4):
        parts = []
        for group in range(2):
            head = group * 8 + pair * 2
            blocks = (f32(pieces[head + offset, HALF : HALF + 64, :]) for offset in range(2))
            parts += pair_pack(*blocks)
        grad_query = jnp.concatenate(parts, axis=0)
        sums_query.append(jnp.sum(grad_query, axis=0, keepdims=True))
        grad_query = bfloat(grad_query)
        rows = slice(pair * 128, pair * 128 + 128)
        grad_hidden = grad_hidden + dot(grad_query, weights[rows, :], NN)
        store(
            bfloat(dot(grad_query, hidden, TN)), [pair * 128 + inside * 32 for inside in range(4)]
        )
    for head in range(HEADS):
        both = jnp.concatenate([pieces[head, 0:HALF, :], pieces[8 + head, 0:HALF, :]], axis=0)
        sums_value.append(jnp.sum(f32(both), axis=0, keepdims=True))
        rows = slice(512 + head * 128, 512 + head * 128 + 128)
        grad_hidden = grad_hidden + dot(both, weights[rows, :], NN)
        first = 512 + head * HEAD_DIM
        store(
            bfloat(dot(both, hidden, TN)), [first, first + 32, first + 512, first + 512 + 32]
        )
    grad_norm, grad_gain, grad_bias = norm_back(unit, scale, small[0:1, :], grad_hidden)
    grad_in = bfloat(grad_resid[...] + grad_norm)
    grad_in_own[...] = jnp.where(core == 0, grad_in[0:HALF], grad_in[HALF:ROWS])
    grad_in_away[...] = jnp.where(core == 0, grad_in[HALF:ROWS], grad_in[0:HALF])
    row = lax.broadcasted_iota(jnp.int32, (16, 128), 0)
    lane = lax.broadcasted_iota(jnp.int32, (16, 128), 1)
    for block in range(4):
        columns = slice(block * 128, block * 128 + 128)
        first = pltpu.roll(jnp.broadcast_to(sums_value[2 * block], (16, 128)), HEAD_DIM, 1)
        second = jnp.broadcast_to(sums_value[2 * block + 1], (16, 128))
        value_row = jnp.where(lane < HEAD_DIM, first, second)
        total = part_small[:, columns]
        total = jnp.where(row == 0, grad_gain[:, columns], total)
        total = jnp.where(row == 1, grad_bias[:, columns], total)
        total = jnp.where(row == 2, sums_query[block], total)
        total = jnp.where(row == 3, value_row, total)
        for inside in range(4):
            owner = block * 4 + inside
            moved = pltpu.roll(total, 128 - inside * 32, 1) if inside else total
            grads[slots[1], owner, 32:48, :] = bfloat(moved)
            grads[slots[1], owner, 48:64, :] = jnp.zeros((16, 128), jnp.bfloat16)
            for lanes in range(1, 4):
                place = slice(lanes * 64 + 32, lanes * 64 + 64)
                grads[slots[1], owner, place, :] = jnp.zeros((32, 128), jnp.bfloat16)
    for owner in range(16):
        grads_own[owner] = grads[0, owner]
        grads_away[owner] = grads[1, owner]


def adam_update(weight, grad_sum, mean_old, square_old, step_rate, decay_on):
    mean_new = beta_first * mean_old + (1.0 - beta_first) * grad_sum
    square_new = beta_second * square_old + (1.0 - beta_second) * grad_sum * grad_sum
    mean_hat = mean_new / (1.0 - beta_first**STEP)
    square_hat = square_new / (1.0 - beta_second**STEP)
    weight_new = weight - step_rate * (
        mean_hat / (jnp.sqrt(square_hat) + adam_epsilon) + decay_on * weight_decay * weight
    )
    return (weight_new, mean_new, square_new)


rates = ((0.04, 1.0), (1.0, 1.0), (0.04, 1.0), (0.02, 1.0), (2.0, 0.0))


def adam_kernel(scalars, grads_own, grads_other, *refs):
    core = scalars[0]
    for index in range(2):
        own, other = refs[15 + 2 * index], refs[16 + 2 * index]
        whole = refs[19 + index]
        whole[pl.ds(pl.multiple_of(core * HALF, HALF), HALF), :] = own[...]
        whole[pl.ds(pl.multiple_of((1 - core) * HALF, HALF), HALF), :] = other[...]
    first_core = scalars[0] == 0
    olds, news = refs[:15], refs[21:36]

    def picked(half, rows, part=None):
        own, other = (
            jnp.concatenate([f32(ref[lanes, rows, :]) for lanes in range(4)], axis=1)
            if part is None
            else sum(f32(ref[group, part * 64 + rows.start : part * 64 + rows.stop, :]) for group in range(4))
            for ref in (grads_own, grads_other)
        )
        return jnp.where(first_core, own, other) if half == 0 else jnp.where(first_core, other, own)

    def late(half, rows):
        return jnp.concatenate([picked(half, rows, part) for part in range(4)], axis=1)

    grad_qkv = jnp.concatenate([late(0, slice(0, 64)), late(1, slice(0, 32))], axis=0)
    grad_small = picked(1, slice(32, 48), 0)[0:12, 0:32]
    grad_up = picked(0, slice(256, 384)).T
    grad_down = picked(1, slice(256, 384))
    grad_proj = jnp.concatenate([picked(0, slice(384, 400)), picked(1, slice(384, 400))], axis=0)
    for index, grad in enumerate((grad_qkv, grad_proj, grad_up, grad_down, grad_small)):
        results = adam_update(
            olds[index][...], grad, olds[5 + index][...], olds[10 + index][...], *rates[index]
        )
        for group, result in enumerate(results):
            news[group * 5 + index][...] = result


def call(
    kernel, shapes, scratch=(), scalars=1, hbm_in=(), hbm_out=(), flops=0, moved=0, vmem_mib=20
):
    vmem = pl.BlockSpec(memory_space=pltpu.VMEM)
    hbm = pl.BlockSpec(memory_space=pltpu.HBM)
    smem = pl.BlockSpec(memory_space=pltpu.SMEM)

    def run(*args):
        specs = [
            smem if index < scalars else hbm if index in hbm_in else vmem
            for index in range(len(args))
        ]
        args = [
            pltpu.with_memory_space_constraint(arg, pltpu.HBM) if index in hbm_in else arg
            for index, arg in enumerate(args)
        ]
        return pl.pallas_call(
            kernel,
            out_shape=[
                pltpu.HBM(shape, kind) if index in hbm_out else jax.ShapeDtypeStruct(shape, kind)
                for index, (shape, kind) in enumerate(shapes)
            ],
            in_specs=specs,
            out_specs=[hbm if index in hbm_out else vmem for index in range(len(shapes))],
            scratch_shapes=list(scratch),
            compiler_params=pltpu.CompilerParams(vmem_limit_bytes=vmem_mib * 1024 * 1024),
            cost_estimate=pl.CostEstimate(flops=flops, bytes_accessed=moved, transcendentals=0),
        )(*args)

    return run


def exchange(values):
    return lax.all_to_all(values, CTX, 0, 0, tiled=True)


def swap_cores(values):
    return lax.ppermute(values, "c", [(0, 1), (1, 0)])


def on_device(
    tokens, cotangent, lengths,
    w_qkv, w_proj, w_up, w_down, w_small,
    mean_qkv, mean_proj, mean_up, mean_down, mean_small,
    square_qkv, square_proj, square_up, square_down, square_small,
):
    kind = jnp.bfloat16
    core = lax.axis_index("c")
    place = lax.axis_index("z") * 4 + lax.axis_index("y")
    scalars = jnp.stack([core, lax.axis_index("x"), place]).astype(jnp.int32)
    lens_other = swap_cores(lengths)
    turned_olds = (
        w_qkv.T, w_proj.T, w_up, w_down, w_small,
        mean_qkv.T, mean_proj.T, mean_up, mean_down, mean_small,
        square_qkv.T, square_proj.T, square_up, square_down, square_small,
    )
    single = jnp.float32
    rows_kind = pltpu.VMEM((ROWS, WIDTH), kind)
    pair_kind = pltpu.VMEM((2, HALF, WIDTH), kind)
    small_kind = pltpu.VMEM((16, WIDTH), single)

    send, rows_away = call(
        gather_kernel,
        [((16, 400, 128), kind), ((2, HALF, WIDTH), kind)],
        [
            pair_kind,
            pltpu.VMEM((96, WIDTH), single),
            pltpu.VMEM((32, WIDTH), single),
            pltpu.VMEM((WIDTH, 128), single),
            pltpu.VMEM((128, WIDTH), single),
            pltpu.VMEM((12, 32), single),
            pltpu.VMEM((400, 128), kind),
            pltpu.VMEM((16, 128), single),
            pltpu.SemaphoreType.DMA((7,)),
        ],
        hbm_in=range(1, 8), moved=3 << 20,
    )(scalars, tokens, cotangent, *turned_olds[0:5])
    rows_other = swap_cores(rows_away)
    first_own = exchange(send)
    first_other = swap_cores(first_own[:, 0:256])
    later_own = lax.all_gather(first_own[:, 256:400], "x", axis=0, tiled=False)
    first_other, lens_other = lax.optimization_barrier((first_other, lens_other))

    send, weights, small = call(
        qkv_kernel,
        [((16, 192, 128), kind), ((1536, WIDTH), kind), ((16, WIDTH), single)],
        [
            rows_kind, pair_kind, pltpu.VMEM((1536, WIDTH), kind), small_kind,
            pltpu.SemaphoreType.DMA((2,)), pltpu.SemaphoreType.DMA((2,)),
        ],
        hbm_in=(1, 2), hbm_out=(1, 2), flops=2 * 256 * 512 * 1536, moved=6 << 20,
    )(scalars, tokens, rows_other, first_own, first_other)
    pieces = exchange(send)
    kept = [
        ((4096, 128), kind), ((128, 4096), kind),
        ((8, HEAD_DIM, ROWS), single), ((8, 8, ROWS), single),
    ]
    kept_scratch = [pltpu.VMEM(*item) for item in kept]
    send, *kept_values = call(
        attend_kernel,
        [((16, 64, 128), kind)] + kept,
        kept_scratch + [pltpu.VMEM((128, 4096), kind), pltpu.SemaphoreType.DMA((4,))],
        scalars=3, hbm_out=(1, 2, 3, 4), flops=36 * 512 * 256 * 2 * 256 * 2, moved=4 << 20,
    )(scalars, lengths, lens_other, pieces, swap_cores(pieces))
    send, later_own = lax.optimization_barrier((send, later_own))
    later_other = swap_cores(later_own)
    attended = exchange(send)
    out_own, out_away, send, grad_resid, part_small, early = call(
        middle_kernel,
        [
            ((HALF, WIDTH), kind),
            ((HALF, WIDTH), kind),
            ((16, 64, 128), kind),
            ((ROWS, WIDTH), single),
            ((16, WIDTH), single),
            ((4, 2, 16, 144, 128), kind),
        ],
        [
            pltpu.VMEM((WIDTH, WIDTH), kind),
            pltpu.VMEM((4, 2, 16, 144, 128), kind),
            rows_kind, rows_kind, pair_kind,
            pltpu.VMEM((4, 16, 144, 128), kind),
            small_kind,
            pltpu.VMEM((ROWS, WIDTH), single),
            small_kind,
            pltpu.SemaphoreType.DMA((7,)),
            pltpu.SemaphoreType.DMA((5,)),
        ],
        scalars=3, hbm_in=(4, 5, 6, 7, 9), hbm_out=(3, 4, 5),
        flops=2 * 256 * 512 * (3 * 512 + 6 * 2048), moved=12 << 20, vmem_mib=32,
    )(
        scalars, lengths, lens_other, attended, tokens, cotangent, rows_other,
        later_own, later_other, small,
    )
    early = lax.psum_scatter(
        early.reshape(4 * 2 * 16 * 144, 128), "x", scatter_dimension=0, tiled=True
    ).reshape(2, 16, 144, 128)
    grads = exchange(send)
    send, send_core = call(
        attend_back_kernel,
        [((16, 192, 128), kind), ((16, HALF, 128), kind)],
        kept_scratch + [pltpu.VMEM((4096, 128), single), pltpu.SemaphoreType.DMA((4,))],
        scalars=3, hbm_in=(4, 5, 6, 7), flops=36 * 512 * 256 * 2 * 256 * 5, moved=5 << 20,
    )(scalars, lengths, lens_other, pieces, *kept_values, grads)
    whole = f32(send[:, 0:HALF]) + f32(swap_cores(send_core))
    pieces = exchange(jnp.concatenate([bfloat(whole), send[:, HALF:]], axis=1))
    grad_in_own, grad_in_away, late_own, late_away = call(
        last_kernel,
        [((HALF, WIDTH), kind), ((HALF, WIDTH), kind)] + [((16, 256, 128), kind)] * 2,
        [
            rows_kind, pair_kind, pltpu.VMEM((1536, WIDTH), kind), small_kind,
            pltpu.VMEM((ROWS, WIDTH), single), small_kind,
            pltpu.VMEM((2, 16, 256, 128), kind), pltpu.SemaphoreType.DMA((6,)),
        ],
        hbm_in=(2, 3, 4, 5, 6, 7), flops=4 * 256 * 512 * 1536, moved=8 << 20,
    )(scalars, pieces, tokens, rows_other, weights, small, grad_resid, part_small)

    late = f32(late_own) + f32(swap_cores(late_away))
    early = f32(early[0]) + f32(swap_cores(early[1]))
    sums = exchange(jnp.concatenate([bfloat(late), bfloat(early)], axis=1))
    sums = bfloat(jnp.sum(f32(sums), axis=0))
    grads_own = lax.all_to_all(
        jnp.broadcast_to(sums[None], (4, 400, 128)), "x", 0, 0, tiled=True
    )
    out, grad_in, *news = call(
        adam_kernel,
        [((ROWS, WIDTH), kind)] * 2 + [(old.shape, single) for old in turned_olds],
        moved=8 << 20,
    )(
        scalars, grads_own, swap_cores(grads_own), *turned_olds,
        out_own, swap_cores(out_away), grad_in_own, swap_cores(grad_in_away),
    )
    news = [new.T if index % 5 < 2 else new for index, new in enumerate(news)]
    return (out, grad_in, *news)


def solution(mesh):
    fine = Mesh(mesh.devices.reshape(4, 2, 4, 4), ("x", "c", "z", "y"))
    rows = P(("x", "c", "z", "y"), None)
    columns = P(None, CTX)
    shards = (columns, columns, columns, P(CTX, None), columns)
    return jax.shard_map(
        on_device,
        mesh=fine,
        in_specs=(rows, rows, P(("x", "c"), None)) + shards * 3,
        out_specs=(rows, rows) + shards * 3,
        check_vma=False,
    )
```

time: 277 us -> 224 us (0.81)
  waiting for transfers between devices: 90.2 us -> 7.85 us
  blocking collectives: 41.1 us -> 122 us
  starting transfers between devices: 32.7 us -> 12 us
  local copies, waits for them, and re-layouts: 18.8 us -> 3.14 us
  Pallas kernels: 67.7 us -> 59.4 us
  other arithmetic: 9.85 us -> 3.94 us
    all_to_all x2 -> x6, blocking collectives: 37.2 us -> 112 us  [exchange(): return lax.all_to_all(values, CTX, 0, 0, tiled=True)]
    all_to_all x5 -> x0, waiting for transfers between devices: 72.1 us -> none  [the longest x4 60.7 us: exchange(): return lax.all_to_all(values, CTX, 0, 0, tiled=True)]
    all_to_all x5 -> x0, starting transfers between devices: 21.9 us -> none  [the longest x4 17.9 us: exchange(): return lax.all_to_all(values, CTX, 0, 0, tiled=True)]
    all_gather x2 -> x1, waiting for transfers between devices: 11.6 us -> 0.02 us  [on_device(): later_own = lax.all_gather(first_own[:, 256:400], 'x', axis=0, tiled=False)]
    all_to_all x0 -> x1, blocking collectives: none -> 10.4 us  [on_device(): lax.all_to_all(jnp.broadcast_to(sums[None], (4, 400, 128)), 'x', 0, 0, ti...]
    pallas_call x5 -> x7, Pallas kernels: 67.7 us -> 59.4 us  [run(): pl.pallas_call(kernel, out_shape=[pltpu.HBM(shape, kind) if index in hbm_...]
    unnamed x52 -> x34, local copies, waits for them, and re-layouts: 6.21 us -> 0.79 us
    ppermute x2 -> x11, waiting for transfers between devices: 2.63 us -> 7.8 us  [swap_cores(): return lax.ppermute(values, 'c', [(0, 1), (1, 0)])]
  transfers between devices with their start and end apart: 10 -> 13, of which waited for: 8 -> 6; matrix products, arithmetic and copies ran while one was open for 6% -> 1% of each run, Pallas kernels for 20% -> 20%
where the time goes in v2:
time: 224 us; the launch traced here: 223 us
  blocking collectives  122 us (54%)
  Pallas kernels  59.4 us (27%)
  between operations  14.4 us (6%)
  starting transfers between devices  12 us (5%)
  waiting for transfers between devices  7.85 us (4%)
  other arithmetic  3.94 us (2%)
  local copies, waits for them, and re-layouts  3.14 us (1%)
    all_to_all x6, blocking collectives, exchange(): return lax.all_to_all(values, CTX, 0, 0, tiled=True)  112 us
    pallas_call x7, Pallas kernels, run(): pl.pallas_call(kernel, out_shape=[pltpu.HBM(shape, kind) if index in hbm_...  59.4 us
    ppermute x11, starting transfers between devices, swap_cores(): return lax.ppermute(values, 'c', [(0, 1), (1, 0)])  11.9 us
    all_to_all x1, blocking collectives, on_device(): lax.all_to_all(jnp.broadcast_to(sums[None], (4, 400, 128)), 'x', 0, 0, ti...  10.4 us
    ppermute x11, waiting for transfers between devices, swap_cores(): return lax.ppermute(values, 'c', [(0, 1), (1, 0)])  7.8 us
  transfers between devices with their start and end apart: 13, of which 6 were waited for; matrix products, arithmetic and copies ran while one was open for 1% of the time, Pallas kernels for 20%

profile of v2, /device:TPU:1, one launch (start us, length us, event | category | flops | bytes accessed | tf_op | source)
XLA Modules:
  0.0 223.1 jit_solution(7582976438068376805)
XLA Ops:
  7.2 0.0 all-gather.3.cloned.1.call-start
  7.2 0.1 pad_add_fusion.scalars
  7.3 2.1 shard_map.305
  9.4 30.9 %all_to_all.35.wide_own = bf16[16,400,128]{2,1,0:T(8,128)(2,1)S(1)} all-to-all(bf16[16,400,128]{2,1,0:T(8,128)(2,1)S(1)} %get-tuple-element.60), channel_id=1, replica_groups=mesh['x'=4,'c'=2,'z'=4,'y'=4] {'z','y'}, dimensions={0} | all-to-all | bytes 3276800 | tf_op jit(solution)/shard_map/all_to_all | solution.py:691
  40.3 0.9 slice.27
  41.2 0.0 all-gather.3.cloned.1.call-update
  41.2 0.0 reduce-scatter.2.cloned.1.call-start
  41.3 0.1 slice.26
  41.4 2.0 collective-permute-start
  43.4 0.1 collective-permute-start.2
  43.5 0.4 collective-permute-start.1
  43.9 2.1 collective-permute-done.1.lens_other
  46.1 0.7 copy-done.16
  46.8 2.8 %shard_map.306 = (bf16[16,192,128]{2,1,0:T(8,128)(2,1)S(1)}, bf16[1536,512]{1,0:T(8,128)(2,1)}, f32[16,512]{1,0:T(8,128)}) custom-call(s32[3]{0:T(128)S(1)} %pad_add_fusion.scalars, bf16[256,512]{1,0:T(8,128)(2,1)} %tokens_in.7, bf16[2,128,512]{2,1,0:T(8,128)(2,1)} %copy-done.16, bf16[16,400,128]{2,1,0:T(8,128)(2,1)S(1)} %all_to_all.35.wide_own, ...), custom_call_target="tpu_custom_call" | custom-call | flops 402653184 | bytes 6291456 | tf_op jit(solution)/shard_map/pallas_call | solution.py:674
  49.6 16.7 %all_to_all.36.pieces = bf16[16,192,128]{2,1,0:T(8,128)(2,1)S(1)} all-to-all(bf16[16,192,128]{2,1,0:T(8,128)(2,1)S(1)} %get-tuple-element.64), channel_id=1, replica_groups=mesh['x'=4,'c'=2,'z'=4,'y'=4] {'z','y'}, dimensions={0} | all-to-all | bytes 1572864 | tf_op jit(solution)/shard_map/all_to_all | solution.py:691
  66.3 1.5 collective-permute-start.3
  67.8 1.9 collective-permute-done.3.others
  69.7 16.1 %shard_map.307 = (bf16[16,64,128]{2,1,0:T(8,128)(2,1)S(1)}, bf16[4096,128]{1,0:T(8,128)(2,1)}, bf16[128,4096]{1,0:T(8,128)(2,1)}, f32[8,64,256]{2,1,0:T(8,128)}, f32[8,8,256]{2,1,0:T(8,128)}) custom-call(s32[3]{0:T(128)S(1)} %pad_add_fusion.scalars, s32[1,2]{1,0:T(1,128)S(1)} %copy-done.15, s32[1,2]{1,0:T(1,128)S(1)} %collective-permute-done.1.lens_other, ...), custom_call_target="tpu_custom_call" | custom-call | flops 4831838208 | bytes 4194304 | tf_op jit(solution)/shard_map/pallas_call | solution.py:674
  85.8 0.0 all-gather.3.cloned.1.call-done
  85.8 0.4 collective-permute-start.4
  86.3 11.0 %all_to_all.37.attended_in = bf16[16,64,128]{2,1,0:T(8,128)(2,1)S(1)} all-to-all(bf16[16,64,128]{2,1,0:T(8,128)(2,1)S(1)} %get-tuple-element.70), channel_id=1, replica_groups=mesh['x'=4,'c'=2,'z'=4,'y'=4] {'z','y'}, dimensions={0} | all-to-all | bytes 524288 | tf_op jit(solution)/shard_map/all_to_all | solution.py:691
  97.2 11.0 %shard_map.308 = (bf16[128,512]{1,0:T(8,128)(2,1)S(1)}, bf16[128,512]{1,0:T(8,128)(2,1)S(1)}, bf16[16,64,128]{2,1,0:T(8,128)(2,1)S(1)}, f32[256,512]{1,0:T(8,128...) custom-call(s32[3]{0:T(128)S(1)} %pad_add_fusion.scalars, s32[1,2]{1,0:T(1,128)S(1)} %copy-done.15, ...), custom_call_target="tpu_custom_call" | custom-call | flops 3623878656 | bytes 12582912 | tf_op jit(solution)/shard_map/pallas_call | solution.py:674
  108.2 0.0 reduce-scatter.2.cloned.1.call-update
  108.3 10.2 %all_to_all.38.grads = bf16[16,64,128]{2,1,0:T(8,128)(2,1)S(1)} all-to-all(bf16[16,64,128]{2,1,0:T(8,128)(2,1)S(1)} %get-tuple-element.73), channel_id=1, replica_groups=mesh['x'=4,'c'=2,'z'=4,'y'=4] {'z','y'}, dimensions={0} | all-to-all | bytes 524288 | tf_op jit(solution)/shard_map/all_to_all | solution.py:691
  118.5 20.5 %shard_map.309 = (bf16[16,192,128]{2,1,0:T(8,128)(2,1)S(1)}, bf16[16,128,128]{2,1,0:T(8,128)(2,1)S(1)}) custom-call(s32[3]{0:T(128)S(1)} %pad_add_fusion.scalars, s32[1,2]{1,0:T(1,128)S(1)} %copy-done.15, s32[1,2]{1,0:T(1,128)S(1)} %collective-permute-done.1.lens_other, bf16[16,192,128]{2,1,0:T(8,128)(2,1)S(1)} %all_to_all.36.pieces, ...), custom_call_target="tpu_custom_call" | custom-call | flops 12079595520 | bytes 5242880 | tf_op jit(solution)/shard_map/pallas_call | solution.py:674
  139.0 2.7 %collective-permute-start.5 = (bf16[16,128,128]{2,1,0:T(8,128)(2,1)S(1)}, bf16[16,128,128]{2,1,0:T(8,128)(2,1)S(1)}, u32[]{:S(2)}, u32[]{:S(2)}) collective-permute-start(bf16[16,128,128]{2,1,0:T(8,128)(2,1)S(1)} %get-tuple-element.75), channel_id=1, source_target_pairs={{0,16},{16,0},{1,17},{17,1},{2,18},{18,2},{3,19},{19,3},{4,20},{20... | collective-permute-start | bytes 1572872 | tf_op jit(solution)/shard_map/ppermute | solution.py:695
  141.7 1.5 collective-permute-done.5
  143.2 0.1 add_convert_fusion.1
  143.4 0.1 pad_maximum_fusion.1
  143.4 16.5 %all_to_all.39.pieces = bf16[16,192,128]{2,1,0:T(8,128)(2,1)S(1)} all-to-all(bf16[16,192,128]{2,1,0:T(8,128)(2,1)S(1)} %pad_maximum_fusion.1), channel_id=1, replica_groups=mesh['x'=4,'c'=2,'z'=4,'y'=4] {'z','y'}, dimensions={0} | all-to-all | bytes 1572864 | tf_op jit(solution)/shard_map/all_to_all | solution.py:691
  160.0 4.4 %shard_map.310 = (bf16[128,512]{1,0:T(8,128)(2,1)S(1)}, bf16[128,512]{1,0:T(8,128)(2,1)S(1)}, bf16[16,256,128]{2,1,0:T(8,128)(2,1)S(1)}, bf16[16,256,128]{2,1,0:T(8,128)(2,1)S(1)}) custom-call(s32[3]{0:T(128)S(1)} %pad_add_fusion.scalars, bf16[16,192,128]{2,1,0:T(8,128)(2,1)S(1)} %all_to_all.39.pieces, bf16[256,512]{1,0:T(8,128)(2,1)} %tokens_in.7, ...), custom_call_target="tpu_custom_call" | custom-call | flops 805306368 | bytes 8388608 | tf_op jit(solution)/shard_map/pallas_call | solution.py:674
  164.4 1.4 collective-permute-start.6
  165.8 1.3 fusion.1
  167.1 0.1 collective-permute-start.7
  167.3 1.0 collective-permute-done.6
  168.2 1.6 add_convert_fusion
  169.8 0.2 fusion
  170.0 0.1 pad_maximum_fusion
  170.1 26.6 %all_to_all.40 = bf16[16,400,128]{2,1,0:T(8,128)(2,1)} all-to-all(bf16[16,400,128]{2,1,0:T(8,128)(2,1)S(1)} %pad_maximum_fusion), channel_id=1, replica_groups=mesh['x'=4,'c'=2,'z'=4,'y'=4] {'z','y'}, dimensions={0} | all-to-all | bytes 3276800 | tf_op jit(solution)/shard_map/all_to_all | solution.py:691
  196.8 0.0 copy-start.5
  196.9 1.8 reduce_sum.12
  198.7 0.1 broadcast_in_dim.2
  198.8 10.4 %all_to_all.41.grads_own = bf16[4,400,128]{2,1,0:T(8,128)(2,1)S(1)} all-to-all(bf16[4,400,128]{2,1,0:T(8,128)(2,1)S(1)} %broadcast_in_dim.2), channel_id=1, replica_groups=mesh['x'=4,'c'=2,'z'=4,'y'=4] {'x'}, dimensions={0} | all-to-all | bytes 819200 | tf_op jit(solution)/shard_map/all_to_all | solution.py:819
  209.2 2.7 %collective-permute-start.8 = (bf16[4,400,128]{2,1,0:T(8,128)(2,1)S(1)}, bf16[4,400,128]{2,1,0:T(8,128)(2,1)S(1)}, u32[]{:S(2)}, u32[]{:S(2)}) collective-permute-start(bf16[4,400,128]{2,1,0:T(8,128)(2,1)S(1)} %all_to_all.41.grads_own), channel_id=1, source_target_pairs={{0,16},{16,0},{1,17},{17,1},{2,18},{18,2},{3,19},{19,3},{4,20},{20... | collective-permute-start | bytes 1228808 | tf_op jit(solution)/shard_map/ppermute | solution.py:695
  211.9 0.5 collective-permute-start.10
  212.4 1.0 collective-permute-done.9.refs_16_
  213.4 0.2 collective-permute-done.10.refs_18_
  213.7 2.5 %shard_map.311 = (bf16[256,512]{1,0:T(8,128)(2,1)}, bf16[256,512]{1,0:T(8,128)(2,1)}, f32[96,512]{1,0:T(8,128)}, f32[32,512]{1,0:T(8,128)}, f32[512,128]{1,0:T(8...) custom-call(s32[3]{0:T(128)S(1)} %pad_add_fusion.scalars, ...), custom_call_target="tpu_custom_call" | custom-call | bytes 8388608 | tf_op jit(solution)/shard_map/pallas_call | solution.py:674
  (40 shorter events, 0.1 us)
Async XLA Ops:
  7.2 78.6 %all-gather.3.cloned.1.call-start = ((), (), s32[]{:S(2)}) async-start(), calls=%async_computation.9 | async-start | bytes 2949120 | tf_op jit(solution)/shard_map/all_gather | solution.py:738
  41.2 2.3 %copy-start.15 = (s32[1,2]{1,0:T(1,128)S(1)}, s32[1,2]{1,0:T(1,128)}, u32[]{:S(2)}) copy-start(s32[1,2]{1,0:T(1,128)} %lens_own.5) | copy-start | bytes 28
  41.2 124.6 %reduce-scatter.2.cloned.1.call-start = ((), (), s32[]{:S(2)}) async-start(), calls=%async_computation.8 | async-start | bytes 5898240 | tf_op jit(solution)/shard_map/reduce_scatter | solution.py:792
  41.4 4.7 %collective-permute-start = (bf16[16,256,128]{2,1,0:T(8,128)(2,1)S(1)}, bf16[16,256,128]{2,1,0:T(8,128)(2,1)S(1)}, u32[]{:S(2)}, u32[]{:S(2)}) collective-permute-start(bf16[16,256,128]{2,1,0:T(8,128)(2,1)S(1)} %slice.26), channel_id=1, source_target_pairs={{0,16},{16,0},{1,17},{17,1},{2,18},{18,2},{3,19},{19,3},{4,20},{20... | collective-permute-start | bytes 3145736 | tf_op jit(solution)/shard_map/ppermute | solution.py:695
  43.4 2.7 %collective-permute-start.2 = (bf16[2,128,512]{2,1,0:T(8,128)(2,1)S(1)}, bf16[2,128,512]{2,1,0:T(8,128)(2,1)S(1)}, u32[]{:S(2)}, u32[]{:S(2)}) collective-permute-start(bf16[2,128,512]{2,1,0:T(8,128)(2,1)S(1)} %get-tuple-element.62), channel_id=1, source_target_pairs={{0,16},{16,0},{1,17},{17,1},{2,18},{18,2},{3,19},{19,3},{4,20},{20... | collective-permute-start | bytes 786440 | tf_op jit(solution)/shard_map/ppermute | solution.py:695
  43.5 2.6 %collective-permute-start.1 = (s32[1,2]{1,0:T(1,128)S(1)}, s32[1,2]{1,0:T(1,128)S(1)}, u32[]{:S(2)}, u32[]{:S(2)}) collective-permute-start(s32[1,2]{1,0:T(1,128)S(1)} %copy-done.15), channel_id=1, source_target_pairs={{0,16},{16,0},{1,17},{17,1},{2,18},{18,2},{3,19},{19,3},{4,20},{20... | collective-permute-start | bytes 32 | tf_op jit(solution)/shard_map/ppermute | solution.py:695
  46.1 0.7 copy-start.16
  66.3 3.4 %collective-permute-start.3 = (bf16[16,192,128]{2,1,0:T(8,128)(2,1)S(1)}, bf16[16,192,128]{2,1,0:T(8,128)(2,1)S(1)}, u32[]{:S(2)}, u32[]{:S(2)}) collective-permute-start(bf16[16,192,128]{2,1,0:T(8,128)(2,1)S(1)} %all_to_all.36.pieces), channel_id=1, source_target_pairs={{0,16},{16,0},{1,17},{17,1},{2,18},{18,2},{3,19},{19,3},{4,20},{20... | collective-permute-start | bytes 2359304 | tf_op jit(solution)/shard_map/ppermute | solution.py:695
  85.8 11.4 %collective-permute-start.4 = (bf16[4,16,144,128]{3,2,1,0:T(8,128)(2,1)}, bf16[4,16,144,128]{3,2,1,0:T(8,128)(2,1)S(1)}, u32[]{:S(2)}, u32[]{:S(2)}) collective-permute-start(bf16[4,16,144,128]{3,2,1,0:T(8,128)(2,1)} %bitcast.31), channel_id=1, source_target_pairs={{0,16},{16,0},{1,17},{17,1},{2,18},{18,2},{3,19},{19,3},{4,20},{20... | collective-permute-start | bytes 7077896 | tf_op jit(solution)/shard_map/ppermute | solution.py:695
  139.0 4.2 %collective-permute-start.5 = (bf16[16,128,128]{2,1,0:T(8,128)(2,1)S(1)}, bf16[16,128,128]{2,1,0:T(8,128)(2,1)S(1)}, u32[]{:S(2)}, u32[]{:S(2)}) collective-permute-start(bf16[16,128,128]{2,1,0:T(8,128)(2,1)S(1)} %get-tuple-element.75), channel_id=1, source_target_pairs={{0,16},{16,0},{1,17},{17,1},{2,18},{18,2},{3,19},{19,3},{4,20},{20... | collective-permute-start | bytes 1572872 | tf_op jit(solution)/shard_map/ppermute | solution.py:695
  164.4 3.9 %collective-permute-start.6 = (bf16[16,256,128]{2,1,0:T(8,128)(2,1)S(1)}, bf16[16,256,128]{2,1,0:T(8,128)(2,1)}, u32[]{:S(2)}, u32[]{:S(2)}) collective-permute-start(bf16[16,256,128]{2,1,0:T(8,128)(2,1)S(1)} %get-tuple-element.80), channel_id=1, source_target_pairs={{0,16},{16,0},{1,17},{17,1},{2,18},{18,2},{3,19},{19,3},{4,20},{20... | collective-permute-start | bytes 3145736 | tf_op jit(solution)/shard_map/ppermute | solution.py:695
  167.1 2.7 %collective-permute-start.7 = (bf16[16,144,128]{2,1,0:T(8,128)(2,1)S(1)}, bf16[16,144,128]{2,1,0:T(8,128)(2,1)S(1)}, u32[]{:S(2)}, u32[]{:S(2)}) collective-permute-start(bf16[16,144,128]{2,1,0:T(8,128)(2,1)S(1)} %bitcast.30), channel_id=1, source_target_pairs={{0,16},{16,0},{1,17},{17,1},{2,18},{18,2},{3,19},{19,3},{4,20},{20... | collective-permute-start | bytes 1769480 | tf_op jit(solution)/shard_map/ppermute | solution.py:695
  196.8 16.9 %copy-start = (f32[512,128]{1,0:T(8,128)S(1)}, f32[512,128]{1,0:T(8,128)}, u32[]{:S(2)}) copy-start(f32[512,128]{1,0:T(8,128)} %refs_2_.1) | copy-start | bytes 786436
  196.8 16.9 %copy-start.1 = (f32[128,512]{1,0:T(8,128)S(1)}, f32[128,512]{1,0:T(8,128)}, u32[]{:S(2)}) copy-start(f32[128,512]{1,0:T(8,128)} %refs_3_.1) | copy-start | bytes 786436
  196.8 16.9 %copy-start.2 = (f32[512,96]{0,1:T(8,128)S(1)}, f32[512,96]{0,1:T(8,128)}, u32[]{:S(2)}) copy-start(f32[512,96]{0,1:T(8,128)} %param.21) | copy-start | bytes 589828
  196.8 16.9 %copy-start.3 = (f32[512,32]{0,1:T(8,128)S(1)}, f32[512,32]{0,1:T(8,128)}, u32[]{:S(2)}) copy-start(f32[512,32]{0,1:T(8,128)} %param.22) | copy-start | bytes 196612
  196.8 16.9 %copy-start.4 = (f32[512,128]{1,0:T(8,128)S(1)}, f32[512,128]{1,0:T(8,128)}, u32[]{:S(2)}) copy-start(f32[512,128]{1,0:T(8,128)} %refs_7_.1) | copy-start | bytes 786436
  196.8 16.9 %copy-start.5 = (f32[128,512]{1,0:T(8,128)S(1)}, f32[128,512]{1,0:T(8,128)}, u32[]{:S(2)}) copy-start(f32[128,512]{1,0:T(8,128)} %refs_8_.1) | copy-start | bytes 786436
  196.8 16.9 %copy-start.6 = (f32[512,128]{1,0:T(8,128)S(1)}, f32[512,128]{1,0:T(8,128)}, u32[]{:S(2)}) copy-start(f32[512,128]{1,0:T(8,128)} %refs_12_.1) | copy-start | bytes 786436
  196.8 16.9 %copy-start.7 = (f32[128,512]{1,0:T(8,128)S(1)}, f32[128,512]{1,0:T(8,128)}, u32[]{:S(2)}) copy-start(f32[128,512]{1,0:T(8,128)} %refs_13_.1) | copy-start | bytes 786436
  196.8 16.9 %copy-start.8 = (f32[512,96]{0,1:T(8,128)S(1)}, f32[512,96]{0,1:T(8,128)}, u32[]{:S(2)}) copy-start(f32[512,96]{0,1:T(8,128)} %param.26) | copy-start | bytes 589828
  196.8 16.9 %copy-start.9 = (f32[512,96]{0,1:T(8,128)S(1)}, f32[512,96]{0,1:T(8,128)}, u32[]{:S(2)}) copy-start(f32[512,96]{0,1:T(8,128)} %param.31) | copy-start | bytes 589828
  196.8 16.9 %copy-start.10 = (f32[512,32]{0,1:T(8,128)S(1)}, f32[512,32]{0,1:T(8,128)}, u32[]{:S(2)}) copy-start(f32[512,32]{0,1:T(8,128)} %param.27) | copy-start | bytes 196612
  196.8 16.9 %copy-start.11 = (f32[512,32]{0,1:T(8,128)S(1)}, f32[512,32]{0,1:T(8,128)}, u32[]{:S(2)}) copy-start(f32[512,32]{0,1:T(8,128)} %param.32) | copy-start | bytes 196612
  196.9 16.9 %copy-start.12 = (f32[12,32]{1,0:T(8,128)S(1)}, f32[12,32]{1,0:T(8,128)}, u32[]{:S(2)}) copy-start(f32[12,32]{1,0:T(8,128)} %refs_4_.1) | copy-start | bytes 4612
  196.9 16.9 %copy-start.13 = (f32[12,32]{1,0:T(8,128)S(1)}, f32[12,32]{1,0:T(8,128)}, u32[]{:S(2)}) copy-start(f32[12,32]{1,0:T(8,128)} %refs_9_.1) | copy-start | bytes 4612
  196.9 16.9 %copy-start.14 = (f32[12,32]{1,0:T(8,128)S(1)}, f32[12,32]{1,0:T(8,128)}, u32[]{:S(2)}) copy-start(f32[12,32]{1,0:T(8,128)} %refs_14_.1) | copy-start | bytes 4612
  209.2 4.5 %collective-permute-start.8 = (bf16[4,400,128]{2,1,0:T(8,128)(2,1)S(1)}, bf16[4,400,128]{2,1,0:T(8,128)(2,1)S(1)}, u32[]{:S(2)}, u32[]{:S(2)}) collective-permute-start(bf16[4,400,128]{2,1,0:T(8,128)(2,1)S(1)} %all_to_all.41.grads_own), channel_id=1, source_target_pairs={{0,16},{16,0},{1,17},{17,1},{2,18},{18,2},{3,19},{19,3},{4,20},{20... | collective-permute-start | bytes 1228808 | tf_op jit(solution)/shard_map/ppermute | solution.py:695
  211.9 1.6 collective-permute-start.9
  211.9 1.7 collective-permute-start.10
Sparse Core Ops, SparseCore 0:
  41.3 31.9 all-gather.2
  108.4 49.1 reduce-scatter.1

commit v3 on v2

--- a/solution.py
+++ b/solution.py
@@ -15,6 +15,9 @@
 HALF = 128
 CHUNK = 512
 TILE = 512
+WIDE = 1024
+EARLY = 208
+BLOCK = 352
 
 epsilon = 1e-05
 negative_big = -1e30
@@ -108,49 +111,48 @@
     small_block[0:12, 0:32] = small[...]
     for part in range(4):
         columns = slice(part * 128, part * 128 + 128)
-        tail = small_block[...] if part == 0 else jnp.zeros((16, 128), jnp.float32)
-        second = jnp.concatenate([qkv[64:96, columns], tail, jnp.zeros((16, 128), jnp.float32)])
-        half = jnp.where(first_core, qkv[0:64, columns], second)
-        block[part * 64 : part * 64 + 64, :] = bfloat(half)
+        half = jnp.where(first_core, qkv[0:48, columns], qkv[48:96, columns])
+        block[part * 48 : part * 48 + 48, :] = bfloat(half)
+    block[192:208, :] = bfloat(small_block[...])
     half = jnp.where(first_core, up[lanes, :].T, down[:, lanes])
-    block[256:384, :] = bfloat(half)
+    block[208:336, :] = bfloat(half)
     half = jnp.where(first_core, proj[0:16, lanes], proj[16:32, lanes])
-    block[384:400, :] = bfloat(half)
+    block[336:352, :] = bfloat(half)
     for owner in range(16):
         send[owner] = block[...]
 
 
 def qkv_kernel(
-    scalars, tokens_in, rows_in, wide_own, wide_other, send, weights_out, small_out,
-    tokens, rows_other, weights, small, done, stored,
+    scalars, tokens_in, rows_other, wide_own, wide_other, send, weights_out, small_out,
+    tokens, weights, small, done, stored,
 ):
-    copies = fetch(((tokens_in, tokens), (rows_in, rows_other)), done)
+    copies = fetch(((tokens_in, tokens),), done)
     first_core = scalars[0] == 0
 
-    def wide(half, owner, part, first, count):
-        rows = slice(part * 64 + first, part * 64 + first + count)
+    def wide(half, owner, part, first):
+        rows = slice(part * 48 + first, part * 48 + first + 16)
         own, other = wide_own[owner, rows, :], wide_other[owner, rows, :]
         return jnp.where(first_core, own, other) if half == 0 else jnp.where(first_core, other, own)
 
     for owner in range(16):
-        for piece in range(3):
-            first = owner * 96 + piece * 32
+        for piece in range(6):
+            first = owner * 96 + piece * 16
             part, offset = divmod(first, 512)
             if part == 0:
                 target = first
             else:
                 head, inside = divmod(offset, HEAD_DIM)
                 target = 512 + head * 128 + (part - 1) * HEAD_DIM + inside
-            half, row = divmod(piece * 32, 64)
+            half, row = divmod(piece * 16, 48)
             for lanes in range(4):
-                weights[target : target + 32, lanes * 128 : lanes * 128 + 128] = wide(
-                    half, owner, lanes, row, 32
+                weights[target : target + 16, lanes * 128 : lanes * 128 + 128] = wide(
+                    half, owner, lanes, row
                 )
     lane = lax.broadcasted_iota(jnp.int32, (16, 128), 1)
     for block in range(4):
         total = jnp.zeros((16, 128), jnp.float32)
         for inside in range(4):
-            piece = f32(wide(1, block * 4 + inside, 0, 32, 16))
+            piece = f32(wide_own[block * 4 + inside, 192:208, :])
             moved = pltpu.roll(piece, inside * 32, 1) if inside else piece
             keep = (lane >= inside * 32) & (lane < inside * 32 + 32)
             total = jnp.where(keep, moved, total)
@@ -182,10 +184,13 @@
         copy.wait()
 
 
-def query_positions(step, core):
+def query_rows(core):
     lane = lax.broadcasted_iota(jnp.int32, (1, ROWS), 1)
-    block = 2 * step + ((lane & 64) >> 6)
-    return block * ROWS + core * HALF + (lane & 63) + ((lane & 128) >> 1)
+    return ((lane & 64) << 2) + core * HALF + (lane & 63) + ((lane & 128) >> 1)
+
+
+def doc_of(position, first_end, second_end):
+    return (position >= first_end).astype(jnp.int32) + (position >= second_end).astype(jnp.int32)
 
 
 def doc_start(position, first_end, second_end):
@@ -199,24 +204,24 @@
     return jnp.concatenate([turned[0:HEAD_DIM], turned[HEAD_DIM:128]], axis=1)
 
 
-def chunk_loops(step, first_end, second_end, body, state):
-    low = doc_start(step * CHUNK, first_end, second_end) // CHUNK
-    last_start = doc_start(step * CHUNK + 2 * CHUNK - 1, first_end, second_end)
-    edge = jnp.minimum(step, (last_start + CHUNK - 1) // CHUNK)
-    edge = jnp.maximum(edge, low)
-
-    def masked_body(index, state):
-        chunk = jnp.where(index == 0, step, low + index - 1)
-        return body(chunk, True, state)
-
-    state = lax.fori_loop(0, edge - low + 1, masked_body, state)
-    return lax.fori_loop(edge, step, lambda chunk, state: body(chunk, False, state), state)
-
-
-def allowed_mask(chunk, position, first_end, second_end):
-    key = lax.broadcasted_iota(jnp.int32, (CHUNK, ROWS), 0) + chunk * CHUNK
-    start = doc_start(position, first_end, second_end)
-    return (key <= position) & (key >= start)
+def causal_bias(bias, core):
+    key = lax.broadcasted_iota(jnp.int32, (CHUNK, ROWS), 0)
+    bias[...] = jnp.where(key <= query_rows(core), 0.0, negative_big)
+
+
+def keyed_rows(rows, first, first_end, second_end):
+    lane = lax.broadcasted_iota(jnp.int32, (ROWS, 128), 1)
+    row = lax.broadcasted_iota(jnp.int32, (ROWS, 128), 0) + first
+    mark = lane - HEAD_DIM == doc_of(row, first_end, second_end)
+    return bfloat(jnp.where(lane < HEAD_DIM, rows, jnp.where(mark, 1.0, 0.0)))
+
+
+def keyed_queries(query_t, step, core, first_end, second_end):
+    position = query_rows(core) + step * CHUNK
+    line = lax.broadcasted_iota(jnp.int32, (HEAD_DIM, ROWS), 0)
+    other = (line < 3) & (line != doc_of(position, first_end, second_end))
+    penalty = jnp.where(other, negative_big, 0.0)
+    return bfloat(jnp.concatenate([query_t, penalty], axis=0))
 
 
 def packed_block(pieces, step):
@@ -234,11 +239,12 @@
 
 def attend_kernel(
     scalars, lens_own, lens_other, pieces, others,
-    send, keys_hbm, turned_hbm, out_hbm, stats_hbm,
-    keys_out, turned_out, out_t, stats, ones_t, done,
+    send, keyed_hbm, keys_hbm, turned_hbm, out_hbm, stats_hbm,
+    keyed, keys_out, turned_out, out_t, stats, ones_t, bias, done,
 ):
     core = scalars[0]
     first_end, second_end = doc_ends(scalars, lens_own, lens_other, scalars[2] // HEADS)
+    causal_bias(bias, core)
 
     def turn(source, _):
         columns = pl.ds(pl.multiple_of(source * ROWS, ROWS), ROWS)
@@ -246,51 +252,52 @@
         first, second = jnp.where(core == 0, own, other), jnp.where(core == 0, other, own)
         keys = jnp.concatenate([first, second], axis=0)
         keys_out[columns, :] = keys
-        turned = f32(keys).T
+        keys = f32(keys)
+        keyed[columns, :] = keyed_rows(keys, source * ROWS, first_end, second_end)
+        turned = keys.T
         turned_out[:, columns] = bfloat(turned)
         row = lax.broadcasted_iota(jnp.int32, (128, ROWS), 0)
         ones_t[:, columns] = bfloat(jnp.where(row < HEAD_DIM, 1.0, turned))
         return 0
 
-    lax.fori_loop(0, 16, turn, 0)
-    stores = fetch(((keys_out, keys_hbm), (turned_out, turned_hbm)), done)
-
-    def load_query(step):
-        query_t = packed_t(packed_block(pieces, step))
-        return bfloat(jnp.concatenate([query_t, jnp.zeros_like(query_t)], axis=0))
+    lax.fori_loop(0, 16, turn, 0, unroll=4)
+    stores = fetch(((keyed, keyed_hbm), (keys_out, keys_hbm), (turned_out, turned_hbm)), done)
 
     def one_pair(pair, _):
         step = 2 * pair
-        positions = tuple(query_positions(step + index, core) for index in range(2))
-        queries = tuple(load_query(step + index) for index in range(2))
-
-        def advance(chunk, masked, which, state):
-            new_state = []
-            columns = pl.ds(pl.multiple_of(chunk * CHUNK, CHUNK), CHUNK)
-            keys = keys_out[columns, :]
-            values = ones_t[:, columns]
-            scores = [dot(keys, queries[index], NN) for index in which]
-            for index, score, (run_max, total) in zip(which, scores, state):
-                if masked:
-                    allowed = allowed_mask(chunk, positions[index], first_end, second_end)
-                    score = jnp.where(allowed, score, negative_big)
-                new_max = jnp.maximum(run_max, jnp.max(score, axis=0, keepdims=True))
-                weights = bfloat(jnp.exp2((score - new_max) * log2_e))
-                scale = jnp.exp2((run_max - new_max) * log2_e)
-                new_state.append((new_max, total * scale + dot(values, weights, NN)))
-            return tuple(new_state)
+        queries = tuple(
+            keyed_queries(
+                packed_t(packed_block(pieces, step + index)), step + index, core, first_end, second_end
+            )
+            for index in range(2)
+        )
+
+        def advance(scores, values, state):
+            run_max, total = state
+            new_max = jnp.maximum(run_max, jnp.max(scores, axis=0, keepdims=True))
+            weights = bfloat(jnp.exp2((scores - new_max) * log2_e))
+            scale = jnp.exp2((run_max - new_max) * log2_e)
+            return new_max, total * scale + dot(values, weights, NN)
+
+        def body(wide, state):
+            rows = pl.ds(pl.multiple_of(wide * WIDE, WIDE), WIDE)
+            keys, values = keyed[rows, :], ones_t[:, rows]
+            scores = [dot(keys, query, NN) for query in queries]
+            return tuple(advance(scores[index], values, state[index]) for index in range(2))
 
         start = (
             jnp.full((1, ROWS), negative_big, jnp.float32),
             jnp.zeros((128, ROWS), jnp.float32),
         )
-        state = chunk_loops(
-            step, first_end, second_end,
-            lambda chunk, masked, state: advance(chunk, masked, (0, 1), state),
-            (start, start),
-        )
-        state = (state[0],) + advance(step + 1, True, (1,), state[1:])
-        for index, (run_max, total) in enumerate(state):
+        low = doc_start(step * CHUNK, first_end, second_end) // WIDE
+        first, second = lax.fori_loop(low, pair, body, (start, start))
+        rows = pl.ds(pl.multiple_of(pair * WIDE, WIDE), WIDE)
+        keys, values = keyed[rows, :], ones_t[:, rows]
+        scores = dot(keys, queries[1], NN)
+        scores = jnp.concatenate([scores[0:CHUNK], scores[CHUNK:WIDE] + bias[...]], axis=0)
+        first = advance(dot(keys[0:CHUNK], queries[0], NN) + bias[...], values[:, 0:CHUNK], first)
+        second = advance(scores, values, second)
+        for index, (run_max, total) in enumerate((first, second)):
             row_sum = total[0:1]
             result = total[HEAD_DIM:128] / row_sum
             out_t[step + index] = result
@@ -301,20 +308,35 @@
         return 0
 
     lax.fori_loop(0, 4, one_pair, 0)
-    stores += fetch(((out_t, out_hbm), (stats, stats_hbm)), done.at[pl.ds(2, 2)])
+    stores += fetch(((out_t, out_hbm), (stats, stats_hbm)), done.at[pl.ds(3, 2)])
     for copy in stores:
         copy.wait()
 
 
 def attend_back_kernel(
-    scalars, lens_own, lens_other, pieces, keys_hbm, turned_hbm, out_hbm, stats_hbm, grads,
-    send, send_core, key_rows, turned, out_t, stats, total, done,
+    scalars, lens_own, lens_other, pieces, keyed_hbm, keys_hbm, turned_hbm, out_hbm, stats_hbm, grads,
+    send, send_core, keyed, key_rows, turned, out_t, stats, total, bias, done, done_small,
 ):
-    copies = fetch(
-        ((keys_hbm, key_rows), (turned_hbm, turned), (out_hbm, out_t), (stats_hbm, stats)), done
-    )
+    small_copies = fetch(((out_hbm, out_t), (stats_hbm, stats)), done_small)
+
+    def wide_copies(pair):
+        rows = pl.ds(pl.multiple_of(pair * WIDE, WIDE), WIDE)
+        places = (
+            (keyed_hbm.at[rows, :], keyed.at[rows, :]),
+            (keys_hbm.at[rows, :], key_rows.at[rows, :]),
+            (turned_hbm.at[:, rows], turned.at[:, rows]),
+        )
+        return [
+            pltpu.make_async_copy(source, target, done.at[pair, index])
+            for index, (source, target) in enumerate(places)
+        ]
+
+    for pair in range(4):
+        for copy in wide_copies(pair):
+            copy.start()
     core = scalars[0]
     first_end, second_end = doc_ends(scalars, lens_own, lens_other, scalars[2] // HEADS)
+    causal_bias(bias, core)
 
     def clear(source, _):
         rows = pl.ds(pl.multiple_of(source * ROWS, ROWS), ROWS)
@@ -322,66 +344,68 @@
         return 0
 
     lax.fori_loop(0, 16, clear, 0)
-    for copy in copies:
+    for copy in small_copies:
         copy.wait()
-
-    low = low_lanes((128, 128))
+    low_half = low_lanes((128, 128))
 
     def load_block(step):
         query = packed_block(pieces, step)
-        query_t = packed_t(query)
-        query_t = bfloat(jnp.concatenate([query_t, jnp.zeros_like(query_t)], axis=0))
-        query = bfloat(
-            jnp.concatenate(
-                [jnp.where(low, query, 0.0), jnp.where(low, pltpu.roll(query, HEAD_DIM, 1), 0.0)],
-                axis=0,
-            )
-        )
+        query_t = keyed_queries(packed_t(query), step, core, first_end, second_end)
+        top = jnp.where(low_half, query, 0.0)
+        bottom = jnp.where(low_half, pltpu.roll(query, HEAD_DIM, 1), 0.0)
+        query = bfloat(jnp.concatenate([top, bottom], axis=0))
         grad = jnp.concatenate([f32(grads[2 * step]), f32(grads[2 * step + 1])], axis=0)
         grad_t = packed_t(grad)
         dots = jnp.sum(grad_t * out_t[step], axis=0, keepdims=True)
         grad_t = bfloat(jnp.concatenate([jnp.zeros_like(grad_t), grad_t], axis=0))
-        grad = bfloat(
-            jnp.concatenate(
-                [jnp.where(low, 0.0, pltpu.roll(grad, HEAD_DIM, 1)), jnp.where(low, 0.0, grad)],
-                axis=0,
-            )
-        )
+        top = jnp.where(low_half, 0.0, pltpu.roll(grad, HEAD_DIM, 1))
+        bottom = jnp.where(low_half, 0.0, grad)
+        grad = bfloat(jnp.concatenate([top, bottom], axis=0))
         return query_t, grad_t, query, grad, dots, stats[step][0:1]
 
     def one_pair(pair, _):
         step = 2 * pair
-        positions = tuple(query_positions(step + index, core) for index in range(2))
+        for copy in wide_copies(pair):
+            copy.wait()
         loaded = tuple(load_block(step + index) for index in range(2))
 
-        def advance(chunk, masked, which, state):
-            rows = pl.ds(pl.multiple_of(chunk * CHUNK, CHUNK), CHUNK)
-            keys = key_rows[rows, :]
-            keys_t = turned[:, rows]
-            scores = [dot(keys, loaded[index][0], NN) for index in which]
-            grad_weights = [dot(keys, loaded[index][1], NN) for index in which]
-            left, right, new_state = [], [], []
-            for place, index in enumerate(which):
-                _, _, query, grad, dots, stat = loaded[index]
-                weights = jnp.exp2((scores[place] - stat) * log2_e)
-                if masked:
-                    allowed = allowed_mask(chunk, positions[index], first_end, second_end)
-                    weights = jnp.where(allowed, weights, 0.0)
-                grad_scores = bfloat(weights * (grad_weights[place] - dots))
-                left += [grad_scores, bfloat(weights)]
-                right += [query, grad]
-                new_state.append(state[place] + dot(keys_t, grad_scores, NN))
-            total[rows, :] += dot(jnp.concatenate(left, axis=1), jnp.concatenate(right, axis=0), NN)
-            return tuple(new_state)
+        def score_grads(index, scores, grad_weights):
+            weights = jnp.exp2((scores - loaded[index][5]) * log2_e)
+            return bfloat(weights * (grad_weights - loaded[index][4])), bfloat(weights)
+
+        both = jnp.concatenate([loaded[0][2], loaded[0][3], loaded[1][2], loaded[1][3]], axis=0)
+
+        def body(wide, state):
+            rows = pl.ds(pl.multiple_of(wide * WIDE, WIDE), WIDE)
+            marked, keys, keys_t = keyed[rows, :], key_rows[rows, :], turned[:, rows]
+            scores = [dot(marked, item[0], NN) for item in loaded]
+            grad_weights = [dot(keys, item[1], NN) for item in loaded]
+            parts = [score_grads(index, scores[index], grad_weights[index]) for index in range(2)]
+            total[rows, :] += dot(jnp.concatenate(parts[0] + parts[1], axis=1), both, NN)
+            return tuple(state[index] + dot(keys_t, parts[index][0], NN) for index in range(2))
 
         start = jnp.zeros((128, ROWS), jnp.float32)
-        state = chunk_loops(
-            step, first_end, second_end,
-            lambda chunk, masked, state: advance(chunk, masked, (0, 1), state),
-            (start, start),
+        low = doc_start(step * CHUNK, first_end, second_end) // WIDE
+        first, second = lax.fori_loop(low, pair, body, (start, start))
+        rows = pl.ds(pl.multiple_of(pair * WIDE, WIDE), CHUNK)
+        rows_next = pl.ds(pl.multiple_of(pair * WIDE + CHUNK, CHUNK), CHUNK)
+        marked, keys, keys_t = keyed[rows, :], key_rows[rows, :], turned[:, rows]
+        marked_next, keys_next = keyed[rows_next, :], key_rows[rows_next, :]
+        parts = (
+            score_grads(
+                0, dot(marked, loaded[0][0], NN) + bias[...], dot(keys, loaded[0][1], NN)
+            ),
+            score_grads(1, dot(marked, loaded[1][0], NN), dot(keys, loaded[1][1], NN)),
+            score_grads(
+                1, dot(marked_next, loaded[1][0], NN) + bias[...], dot(keys_next, loaded[1][1], NN)
+            ),
         )
-        state = (state[0],) + advance(step + 1, True, (1,), state[1:])
-        for index, grad_query_t in enumerate(state):
+        total[rows, :] += dot(jnp.concatenate(parts[0] + parts[1], axis=1), both, NN)
+        total[rows_next, :] += dot(jnp.concatenate(parts[2], axis=1), both[2 * ROWS : 4 * ROWS], NN)
+        first = first + dot(keys_t, parts[0][0], NN)
+        second = second + dot(keys_t, parts[1][0], NN)
+        second = second + dot(turned[:, rows_next], parts[2][0], NN)
+        for index, grad_query_t in enumerate((first, second)):
             turn = grad_query_t[0:HEAD_DIM] * HEAD_DIM**-0.5
             packed = jnp.concatenate([turn[:, 0:128], turn[:, 128:256]], axis=0).T
             send[2 * (step + index), HALF : HALF + 64, :] = bfloat(packed[0:64])
@@ -403,19 +427,20 @@
 def middle_kernel(
     scalars, lens_own, lens_other, attended_in, tokens_in, cotangent_in, rows_in, later_in,
     later_other, small_in,
-    out_own, out_away, send, grad_resid_hbm, small_hbm, grads_out,
-    w_proj, grads, tokens, cotangent, rows_other, later_own, small, grad_resid_out, grad_small,
+    out_own_hbm, out_away_hbm, send, grad_resid_hbm, small_hbm, grads_out,
+    w_proj, grads, out_own, out_away, tokens, cotangent, rows_other, later_own, small, grad_resid_out, grad_small,
     done, fetched,
 ):
     pairs = (
-        (later_in, later_own), (tokens_in, tokens), (rows_in, rows_other), (small_in, small),
-        (cotangent_in, cotangent),
+        (later_in.at[:, :, 128:144, :], later_own.at[:, :, 128:144, :]),
+        (tokens_in, tokens), (rows_in, rows_other), (small_in, small), (cotangent_in, cotangent),
+        (later_in.at[:, :, 0:128, :], later_own.at[:, :, 0:128, :]),
     )
     copies = fetch(pairs, fetched)
     core = scalars[0]
     first_core = core == 0
     slots = (core, 1 - core)
-    for copy in copies:
+    for copy in copies[0:5]:
         copy.wait()
     for owner in range(16):
         for lanes in range(4):
@@ -443,6 +468,8 @@
     live = position < jnp.where(row < HALF, first_live, second_live)
     grad_out = jnp.where(live, f32(mixed_rows(core, cotangent, rows_other[1])), 0.0)
     grad_out_b = bfloat(grad_out)
+
+    copies[5].wait()
 
     def one_tile(tile, state):
         branch, grad_hidden_in = state
@@ -502,9 +529,11 @@
     grad_small[5:6, :] = grad_gain
     grad_small[6:7, :] = grad_bias
     grad_small[7:8, :] = jnp.sum(grad_out, axis=0, keepdims=True)
-    stores = fetch(
-        ((grad_resid_out, grad_resid_hbm), (grad_small, small_hbm)), done.at[pl.ds(5, 2)]
-    )
+    pairs = (
+        (grad_resid_out, grad_resid_hbm), (grad_small, small_hbm),
+        (out_own, out_own_hbm), (out_away, out_away_hbm),
+    )
+    stores = fetch(pairs, done.at[pl.ds(5, 4)])
     grad_attended = f32(bfloat(dot(grad_resid_b, w_proj[...], NN)))
     for pair in range(4):
         columns = slice(pair * 128, pair * 128 + 128)
@@ -527,8 +556,8 @@
 
 def last_kernel(
     scalars, pieces, tokens_in, rows_in, weights_in, small_in, grad_resid_in, part_in,
-    grad_in_own, grad_in_away, grads_own, grads_away,
-    tokens, rows_other, weights, small, grad_resid, part_small, grads, done,
+    grad_in_own_hbm, grad_in_away_hbm, grads_own, grads_away,
+    grad_in_own, grad_in_away, tokens, rows_other, weights, small, grad_resid, part_small, grads, done,
 ):
     pairs = (
         (weights_in, weights), (tokens_in, tokens), (rows_in, rows_other), (small_in, small),
@@ -537,21 +566,22 @@
     copies = fetch(pairs, done)
     core = scalars[0]
     slots = (core, 1 - core)
-    for copy in copies:
+    for copy in copies[1:4]:
         copy.wait()
     unit, scale = normed(f32(mixed_rows(core, tokens, rows_other[0])))
     hidden = bfloat(unit * small[0:1, :] + small[1:2, :])
     grad_hidden = jnp.zeros((ROWS, WIDTH), jnp.float32)
+    parts_all = []
     sums_query = []
     sums_value = []
 
     def store(weight_grad, first_rows):
-        for index, first in enumerate(first_rows):
-            owner, row = divmod(first, 96)
+        for index in range(8):
+            owner, row = divmod(first_rows[index // 4] + index % 4 * 16, 96)
             for lanes in range(4):
-                place = slice(lanes * 64 + row % 64, lanes * 64 + row % 64 + 32)
-                grads[slots[row // 64], owner, place, :] = weight_grad[
-                    index * 32 : index * 32 + 32, lanes * 128 : lanes * 128 + 128
+                place = slice(lanes * 48 + row % 48, lanes * 48 + row % 48 + 16)
+                grads[slots[row // 48], owner, place, :] = weight_grad[
+                    index * 16 : index * 16 + 16, lanes * 128 : lanes * 128 + 128
                 ]
 
     for pair in range(4):
@@ -564,23 +594,25 @@
         sums_query.append(jnp.sum(grad_query, axis=0, keepdims=True))
         grad_query = bfloat(grad_query)
         rows = slice(pair * 128, pair * 128 + 128)
-        grad_hidden = grad_hidden + dot(grad_query, weights[rows, :], NN)
-        store(
-            bfloat(dot(grad_query, hidden, TN)), [pair * 128 + inside * 32 for inside in range(4)]
-        )
+        store(bfloat(dot(grad_query, hidden, TN)), (pair * 128, pair * 128 + HEAD_DIM))
+        parts_all.append((grad_query, rows))
     for head in range(HEADS):
         both = jnp.concatenate([pieces[head, 0:HALF, :], pieces[8 + head, 0:HALF, :]], axis=0)
         sums_value.append(jnp.sum(f32(both), axis=0, keepdims=True))
         rows = slice(512 + head * 128, 512 + head * 128 + 128)
-        grad_hidden = grad_hidden + dot(both, weights[rows, :], NN)
         first = 512 + head * HEAD_DIM
-        store(
-            bfloat(dot(both, hidden, TN)), [first, first + 32, first + 512, first + 512 + 32]
-        )
+        store(bfloat(dot(both, hidden, TN)), (first, first + 512))
+        parts_all.append((both, rows))
+    for copy in copies[0:1] + copies[4:6]:
+        copy.wait()
+    for part, rows in parts_all:
+        grad_hidden = grad_hidden + dot(part, weights[rows, :], NN)
     grad_norm, grad_gain, grad_bias = norm_back(unit, scale, small[0:1, :], grad_hidden)
     grad_in = bfloat(grad_resid[...] + grad_norm)
     grad_in_own[...] = jnp.where(core == 0, grad_in[0:HALF], grad_in[HALF:ROWS])
     grad_in_away[...] = jnp.where(core == 0, grad_in[HALF:ROWS], grad_in[0:HALF])
+    pairs = ((grad_in_own, grad_in_own_hbm), (grad_in_away, grad_in_away_hbm))
+    stores = fetch(pairs, done.at[pl.ds(6, 2)])
     row = lax.broadcasted_iota(jnp.int32, (16, 128), 0)
     lane = lax.broadcasted_iota(jnp.int32, (16, 128), 1)
     for block in range(4):
@@ -596,14 +628,29 @@
         for inside in range(4):
             owner = block * 4 + inside
             moved = pltpu.roll(total, 128 - inside * 32, 1) if inside else total
-            grads[slots[1], owner, 32:48, :] = bfloat(moved)
-            grads[slots[1], owner, 48:64, :] = jnp.zeros((16, 128), jnp.bfloat16)
-            for lanes in range(1, 4):
-                place = slice(lanes * 64 + 32, lanes * 64 + 64)
-                grads[slots[1], owner, place, :] = jnp.zeros((32, 128), jnp.bfloat16)
+            grads[slots[0], owner, 192:208, :] = bfloat(moved)
+            grads[slots[1], owner, 192:208, :] = jnp.zeros((16, 128), jnp.bfloat16)
     for owner in range(16):
         grads_own[owner] = grads[0, owner]
         grads_away[owner] = grads[1, owner]
+    for copy in stores:
+        copy.wait()
+
+
+def combine_kernel(late_own, late_other, early_in, early_other, sums, early, done):
+    copy = pltpu.make_async_copy(early_in.at[0], early, done)
+    copy.start()
+    for owner in range(16):
+        sums[owner, 0:EARLY, :] = bfloat(f32(late_own[owner]) + f32(late_other[owner]))
+    copy.wait()
+    for owner in range(16):
+        sums[owner, EARLY:BLOCK, :] = bfloat(f32(early[owner]) + f32(early_other[owner]))
+
+
+def reduce_kernel(pieces, sums):
+    total = bfloat(sum(f32(pieces[owner]) for owner in range(16)))
+    for group in range(4):
+        sums[group] = total
 
 
 def adam_update(weight, grad_sum, mean_old, square_old, step_rate, decay_on):
@@ -634,7 +681,7 @@
         own, other = (
             jnp.concatenate([f32(ref[lanes, rows, :]) for lanes in range(4)], axis=1)
             if part is None
-            else sum(f32(ref[group, part * 64 + rows.start : part * 64 + rows.stop, :]) for group in range(4))
+            else sum(f32(ref[group, part * 48 + rows.start : part * 48 + rows.stop, :]) for group in range(4))
             for ref in (grads_own, grads_other)
         )
         return jnp.where(first_core, own, other) if half == 0 else jnp.where(first_core, other, own)
@@ -642,11 +689,11 @@
     def late(half, rows):
         return jnp.concatenate([picked(half, rows, part) for part in range(4)], axis=1)
 
-    grad_qkv = jnp.concatenate([late(0, slice(0, 64)), late(1, slice(0, 32))], axis=0)
-    grad_small = picked(1, slice(32, 48), 0)[0:12, 0:32]
-    grad_up = picked(0, slice(256, 384)).T
-    grad_down = picked(1, slice(256, 384))
-    grad_proj = jnp.concatenate([picked(0, slice(384, 400)), picked(1, slice(384, 400))], axis=0)
+    grad_qkv = jnp.concatenate([late(0, slice(0, 48)), late(1, slice(0, 48))], axis=0)
+    grad_small = picked(0, slice(192, 208), 0)[0:12, 0:32]
+    grad_up = picked(0, slice(208, 336)).T
+    grad_down = picked(1, slice(208, 336))
+    grad_proj = jnp.concatenate([picked(0, slice(336, 352)), picked(1, slice(336, 352))], axis=0)
     for index, grad in enumerate((grad_qkv, grad_proj, grad_up, grad_down, grad_small)):
         results = adam_update(
             olds[index][...], grad, olds[5 + index][...], olds[10 + index][...], *rates[index]
@@ -718,7 +765,7 @@
 
     send, rows_away = call(
         gather_kernel,
-        [((16, 400, 128), kind), ((2, HALF, WIDTH), kind)],
+        [((16, BLOCK, 128), kind), ((2, HALF, WIDTH), kind)],
         [
             pair_kind,
             pltpu.VMEM((96, WIDTH), single),
@@ -726,7 +773,7 @@
             pltpu.VMEM((WIDTH, 128), single),
             pltpu.VMEM((128, WIDTH), single),
             pltpu.VMEM((12, 32), single),
-            pltpu.VMEM((400, 128), kind),
+            pltpu.VMEM((BLOCK, 128), kind),
             pltpu.VMEM((16, 128), single),
             pltpu.SemaphoreType.DMA((7,)),
         ],
@@ -734,30 +781,34 @@
     )(scalars, tokens, cotangent, *turned_olds[0:5])
     rows_other = swap_cores(rows_away)
     first_own = exchange(send)
-    first_other = swap_cores(first_own[:, 0:256])
-    later_own = lax.all_gather(first_own[:, 256:400], "x", axis=0, tiled=False)
+    first_other = swap_cores(first_own[:, 0:EARLY])
+    later_own = lax.all_gather(first_own[:, EARLY:BLOCK], "x", axis=0, tiled=False)
     first_other, lens_other = lax.optimization_barrier((first_other, lens_other))
 
     send, weights, small = call(
         qkv_kernel,
         [((16, 192, 128), kind), ((1536, WIDTH), kind), ((16, WIDTH), single)],
         [
-            rows_kind, pair_kind, pltpu.VMEM((1536, WIDTH), kind), small_kind,
-            pltpu.SemaphoreType.DMA((2,)), pltpu.SemaphoreType.DMA((2,)),
+            rows_kind, pltpu.VMEM((1536, WIDTH), kind), small_kind,
+            pltpu.SemaphoreType.DMA((1,)), pltpu.SemaphoreType.DMA((2,)),
         ],
-        hbm_in=(1, 2), hbm_out=(1, 2), flops=2 * 256 * 512 * 1536, moved=6 << 20,
+        hbm_in=(1,), hbm_out=(1, 2), flops=2 * 256 * 512 * 1536, moved=6 << 20,
     )(scalars, tokens, rows_other, first_own, first_other)
     pieces = exchange(send)
     kept = [
-        ((4096, 128), kind), ((128, 4096), kind),
+        ((4096, 128), kind), ((4096, 128), kind), ((128, 4096), kind),
         ((8, HEAD_DIM, ROWS), single), ((8, 8, ROWS), single),
     ]
     kept_scratch = [pltpu.VMEM(*item) for item in kept]
     send, *kept_values = call(
         attend_kernel,
         [((16, 64, 128), kind)] + kept,
-        kept_scratch + [pltpu.VMEM((128, 4096), kind), pltpu.SemaphoreType.DMA((4,))],
-        scalars=3, hbm_out=(1, 2, 3, 4), flops=36 * 512 * 256 * 2 * 256 * 2, moved=4 << 20,
+        kept_scratch
+        + [
+            pltpu.VMEM((128, 4096), kind), pltpu.VMEM((CHUNK, ROWS), single),
+            pltpu.SemaphoreType.DMA((5,)),
+        ],
+        scalars=3, hbm_out=(1, 2, 3, 4, 5), vmem_mib=28, flops=36 * 512 * 256 * 2 * 256 * 2, moved=4 << 20,
     )(scalars, lengths, lens_other, pieces, swap_cores(pieces))
     send, later_own = lax.optimization_barrier((send, later_own))
     later_other = swap_cores(later_own)
@@ -775,15 +826,16 @@
         [
             pltpu.VMEM((WIDTH, WIDTH), kind),
             pltpu.VMEM((4, 2, 16, 144, 128), kind),
+            pltpu.VMEM((HALF, WIDTH), kind), pltpu.VMEM((HALF, WIDTH), kind),
             rows_kind, rows_kind, pair_kind,
             pltpu.VMEM((4, 16, 144, 128), kind),
             small_kind,
             pltpu.VMEM((ROWS, WIDTH), single),
             small_kind,
-            pltpu.SemaphoreType.DMA((7,)),
-            pltpu.SemaphoreType.DMA((5,)),
+            pltpu.SemaphoreType.DMA((9,)),
+            pltpu.SemaphoreType.DMA((6,)),
         ],
-        scalars=3, hbm_in=(4, 5, 6, 7, 9), hbm_out=(3, 4, 5),
+        scalars=3, hbm_in=(4, 5, 6, 7, 9), hbm_out=(0, 1, 3, 4, 5),
         flops=2 * 256 * 512 * (3 * 512 + 6 * 2048), moved=12 << 20, vmem_mib=32,
     )(
         scalars, lengths, lens_other, attended, tokens, cotangent, rows_other,
@@ -796,36 +848,48 @@
     send, send_core = call(
         attend_back_kernel,
         [((16, 192, 128), kind), ((16, HALF, 128), kind)],
-        kept_scratch + [pltpu.VMEM((4096, 128), single), pltpu.SemaphoreType.DMA((4,))],
-        scalars=3, hbm_in=(4, 5, 6, 7), flops=36 * 512 * 256 * 2 * 256 * 5, moved=5 << 20,
+        kept_scratch
+        + [
+            pltpu.VMEM((4096, 128), single), pltpu.VMEM((CHUNK, ROWS), single),
+            pltpu.SemaphoreType.DMA((4, 3)), pltpu.SemaphoreType.DMA((2,)),
+        ],
+        scalars=3, hbm_in=(4, 5, 6, 7, 8), vmem_mib=32, flops=36 * 512 * 256 * 2 * 256 * 5, moved=5 << 20,
     )(scalars, lengths, lens_other, pieces, *kept_values, grads)
     whole = f32(send[:, 0:HALF]) + f32(swap_cores(send_core))
     pieces = exchange(jnp.concatenate([bfloat(whole), send[:, HALF:]], axis=1))
     grad_in_own, grad_in_away, late_own, late_away = call(
         last_kernel,
-        [((HALF, WIDTH), kind), ((HALF, WIDTH), kind)] + [((16, 256, 128), kind)] * 2,
+        [((HALF, WIDTH), kind), ((HALF, WIDTH), kind)] + [((16, EARLY, 128), kind)] * 2,
         [
+            pltpu.VMEM((HALF, WIDTH), kind), pltpu.VMEM((HALF, WIDTH), kind),
             rows_kind, pair_kind, pltpu.VMEM((1536, WIDTH), kind), small_kind,
             pltpu.VMEM((ROWS, WIDTH), single), small_kind,
-            pltpu.VMEM((2, 16, 256, 128), kind), pltpu.SemaphoreType.DMA((6,)),
+            pltpu.VMEM((2, 16, EARLY, 128), kind), pltpu.SemaphoreType.DMA((8,)),
         ],
-        hbm_in=(2, 3, 4, 5, 6, 7), flops=4 * 256 * 512 * 1536, moved=8 << 20,
+        hbm_in=(2, 3, 4, 5, 6, 7), hbm_out=(0, 1), flops=4 * 256 * 512 * 1536, moved=8 << 20,
     )(scalars, pieces, tokens, rows_other, weights, small, grad_resid, part_small)
 
-    late = f32(late_own) + f32(swap_cores(late_away))
-    early = f32(early[0]) + f32(swap_cores(early[1]))
-    sums = exchange(jnp.concatenate([bfloat(late), bfloat(early)], axis=1))
-    sums = bfloat(jnp.sum(f32(sums), axis=0))
-    grads_own = lax.all_to_all(
-        jnp.broadcast_to(sums[None], (4, 400, 128)), "x", 0, 0, tiled=True
-    )
+    late_other, out_other, grad_in_other = lax.optimization_barrier(
+        (swap_cores(late_away), swap_cores(out_away), swap_cores(grad_in_away))
+    )
+    (sums,) = call(
+        combine_kernel, [((16, BLOCK, 128), kind)],
+        [pltpu.VMEM((16, 144, 128), kind), pltpu.SemaphoreType.DMA],
+        scalars=0, hbm_in=(2,), moved=4 << 20,
+    )(
+        late_own, late_other, early, swap_cores(early[1])
+    )
+    (sums,) = call(reduce_kernel, [((4, BLOCK, 128), kind)], scalars=0, moved=2 << 20)(
+        exchange(sums)
+    )
+    grads_own = lax.all_to_all(sums, "x", 0, 0, tiled=True)
     out, grad_in, *news = call(
         adam_kernel,
         [((ROWS, WIDTH), kind)] * 2 + [(old.shape, single) for old in turned_olds],
         moved=8 << 20,
     )(
         scalars, grads_own, swap_cores(grads_own), *turned_olds,
-        out_own, swap_cores(out_away), grad_in_own, swap_cores(grad_in_away),
+        out_own, out_other, grad_in_own, grad_in_other,
     )
     news = [new.T if index % 5 < 2 else new for index, new in enumerate(news)]
     return (out, grad_in, *news)

time: 224 us -> 210 us (0.938)
  blocking collectives: 122 us -> 117 us
  Pallas kernels: 59.4 us -> 54.6 us
  other arithmetic: 3.94 us -> 0.27 us
    all_to_all x6, blocking collectives: 112 us -> 107 us  [exchange(): return lax.all_to_all(values, CTX, 0, 0, tiled=True)]
    pallas_call x7 -> x9, Pallas kernels: 59.4 us -> 54.6 us  [run(): pl.pallas_call(kernel, out_shape=[pltpu.HBM(shape, kind) if index in hbm_...]
  transfers between devices with their start and end apart: 13 -> 13, of which waited for: 6 -> 6; matrix products, arithmetic and copies ran while one was open for 1% -> 1% of each run, Pallas kernels for 20% -> 18%
where the time goes in v3:
time: 210 us; the launch traced here: 209 us
  blocking collectives  117 us (56%)
  Pallas kernels  54.6 us (26%)
  between operations  14.4 us (7%)
  starting transfers between devices  12.5 us (6%)
  waiting for transfers between devices  8.64 us (4%)
  local copies, waits for them, and re-layouts  2.14 us (1%)
    all_to_all x6, blocking collectives, exchange(): return lax.all_to_all(values, CTX, 0, 0, tiled=True)  107 us
    pallas_call x9, Pallas kernels, run(): pl.pallas_call(kernel, out_shape=[pltpu.HBM(shape, kind) if index in hbm_...  54.6 us
    ppermute x11, starting transfers between devices, swap_cores(): return lax.ppermute(values, 'c', [(0, 1), (1, 0)])  12.4 us
    all_to_all x1, blocking collectives, on_device(): grads_own = lax.all_to_all(sums, 'x', 0, 0, tiled=True)  10 us
    ppermute x11, waiting for transfers between devices, swap_cores(): return lax.ppermute(values, 'c', [(0, 1), (1, 0)])  8.59 us
  transfers between devices with their start and end apart: 13, of which 6 were waited for; matrix products, arithmetic and copies ran while one was open for 1% of the time, Pallas kernels for 18%

profile of v3, /device:TPU:1, one launch (start us, length us, event | category | flops | bytes accessed | tf_op | source)
XLA Modules:
  0.0 209.1 jit_solution(8051369840263294656)
XLA Ops:
  7.2 0.0 all-gather.3.cloned.1.call-start
  7.2 0.1 pad_add_fusion.scalars
  7.3 2.1 shard_map.305
  9.4 28.9 %all_to_all.35.wide_own = bf16[16,352,128]{2,1,0:T(8,128)(2,1)S(1)} all-to-all(bf16[16,352,128]{2,1,0:T(8,128)(2,1)S(1)} %get-tuple-element.64), channel_id=1, replica_groups=mesh['x'=4,'c'=2,'z'=4,'y'=4] {'z','y'}, dimensions={0} | all-to-all | bytes 2883584 | tf_op jit(solution)/shard_map/all_to_all | solution.py:738
  38.3 0.9 slice.22
  39.1 0.0 all-gather.3.cloned.1.call-update
  39.2 0.0 reduce-scatter.2.cloned.1.call-start
  39.2 0.1 slice.21
  39.3 1.9 collective-permute-start
  41.2 0.1 collective-permute-start.2
  41.3 0.4 collective-permute-start.1
  41.7 1.9 collective-permute-done.1.lens_other
  43.6 3.2 %shard_map.306 = (bf16[16,192,128]{2,1,0:T(8,128)(2,1)S(1)}, bf16[1536,512]{1,0:T(8,128)(2,1)}, f32[16,512]{1,0:T(8,128)}) custom-call(s32[3]{0:T(128)S(1)} %pad_add_fusion.scalars, bf16[256,512]{1,0:T(8,128)(2,1)} %tokens_in.7, bf16[2,128,512]{2,1,0:T(8,128)(2,1)S(1)} %collective-permute-done.2.rows_other.rows_in, ...), custom_call_target="tpu_custom_call" | custom-call | flops 402653184 | bytes 6291456 | tf_op jit(solution)/shard_map/pallas_call | solution.py:721
  46.8 16.4 %all_to_all.36.pieces = bf16[16,192,128]{2,1,0:T(8,128)(2,1)S(1)} all-to-all(bf16[16,192,128]{2,1,0:T(8,128)(2,1)S(1)} %get-tuple-element.68), channel_id=1, replica_groups=mesh['x'=4,'c'=2,'z'=4,'y'=4] {'z','y'}, dimensions={0} | all-to-all | bytes 1572864 | tf_op jit(solution)/shard_map/all_to_all | solution.py:738
  63.2 1.5 collective-permute-start.3
  64.7 1.9 collective-permute-done.3.others
  66.6 13.5 %shard_map.307 = (bf16[16,64,128]{2,1,0:T(8,128)(2,1)S(1)}, bf16[4096,128]{1,0:T(8,128)(2,1)}, bf16[4096,128]{1,0:T(8,128)(2,1)}, bf16[128,4096]{1,0:T(8,128)(2,...) custom-call(s32[3]{0:T(128)S(1)} %pad_add_fusion.scalars, s32[1,2]{1,0:T(1,128)S(1)} %copy-done.18, ...), custom_call_target="tpu_custom_call" | custom-call | flops 4831838208 | bytes 4194304 | tf_op jit(solution)/shard_map/pallas_call | solution.py:721
  80.1 0.0 all-gather.3.cloned.1.call-done
  80.1 0.5 collective-permute-start.4
  80.6 11.0 %all_to_all.37.attended_in = bf16[16,64,128]{2,1,0:T(8,128)(2,1)S(1)} all-to-all(bf16[16,64,128]{2,1,0:T(8,128)(2,1)S(1)} %get-tuple-element.75), channel_id=1, replica_groups=mesh['x'=4,'c'=2,'z'=4,'y'=4] {'z','y'}, dimensions={0} | all-to-all | bytes 524288 | tf_op jit(solution)/shard_map/all_to_all | solution.py:738
  91.6 10.4 %shard_map.308 = (bf16[128,512]{1,0:T(8,128)(2,1)}, bf16[128,512]{1,0:T(8,128)(2,1)}, bf16[16,64,128]{2,1,0:T(8,128)(2,1)S(1)}, f32[256,512]{1,0:T(8,128)}, f32[...) custom-call(s32[3]{0:T(128)S(1)} %pad_add_fusion.scalars, s32[1,2]{1,0:T(1,128)S(1)} %copy-done.18, ...), custom_call_target="tpu_custom_call" | custom-call | flops 3623878656 | bytes 12582912 | tf_op jit(solution)/shard_map/pallas_call | solution.py:721
  102.0 0.0 reduce-scatter.2.cloned.1.call-update
  102.0 10.2 %all_to_all.38.grads = bf16[16,64,128]{2,1,0:T(8,128)(2,1)S(1)} all-to-all(bf16[16,64,128]{2,1,0:T(8,128)(2,1)S(1)} %get-tuple-element.78), channel_id=1, replica_groups=mesh['x'=4,'c'=2,'z'=4,'y'=4] {'z','y'}, dimensions={0} | all-to-all | bytes 524288 | tf_op jit(solution)/shard_map/all_to_all | solution.py:738
  112.3 16.4 %shard_map.309 = (bf16[16,192,128]{2,1,0:T(8,128)(2,1)S(1)}, bf16[16,128,128]{2,1,0:T(8,128)(2,1)S(1)}) custom-call(s32[3]{0:T(128)S(1)} %pad_add_fusion.scalars, s32[1,2]{1,0:T(1,128)S(1)} %copy-done.18, s32[1,2]{1,0:T(1,128)S(1)} %collective-permute-done.1.lens_other, bf16[16,192,128]{2,1,0:T(8,128)(2,1)S(1)} %all_to_all.36.pieces, ...), custom_call_target="tpu_custom_call" | custom-call | flops 12079595520 | bytes 5242880 | tf_op jit(solution)/shard_map/pallas_call | solution.py:721
  128.7 2.9 %collective-permute-start.5 = (bf16[16,128,128]{2,1,0:T(8,128)(2,1)S(1)}, bf16[16,128,128]{2,1,0:T(8,128)(2,1)S(1)}, u32[]{:S(2)}, u32[]{:S(2)}) collective-permute-start(bf16[16,128,128]{2,1,0:T(8,128)(2,1)S(1)} %get-tuple-element.80), channel_id=1, source_target_pairs={{0,16},{16,0},{1,17},{17,1},{2,18},{18,2},{3,19},{19,3},{4,20},{20... | collective-permute-start | bytes 1572872 | tf_op jit(solution)/shard_map/ppermute | solution.py:742
  131.6 1.5 collective-permute-done.5
  133.1 0.1 add_convert_fusion
  133.2 0.1 pad_maximum_fusion
  133.3 16.4 %all_to_all.39.pieces = bf16[16,192,128]{2,1,0:T(8,128)(2,1)S(1)} all-to-all(bf16[16,192,128]{2,1,0:T(8,128)(2,1)S(1)} %pad_maximum_fusion), channel_id=1, replica_groups=mesh['x'=4,'c'=2,'z'=4,'y'=4] {'z','y'}, dimensions={0} | all-to-all | bytes 1572864 | tf_op jit(solution)/shard_map/all_to_all | solution.py:738
  149.7 5.1 %shard_map.310 = (bf16[128,512]{1,0:T(8,128)(2,1)}, bf16[128,512]{1,0:T(8,128)(2,1)}, bf16[16,208,128]{2,1,0:T(8,128)(2,1)S(1)}, bf16[16,208,128]{2,1,0:T(8,128)(2,1)S(1)}) custom-call(s32[3]{0:T(128)S(1)} %pad_add_fusion.scalars, bf16[16,192,128]{2,1,0:T(8,128)(2,1)S(1)} %all_to_all.39.pieces, bf16[256,512]{1,0:T(8,128)(2,1)} %tokens_in.7, ...), custom_call_target="tpu_custom_call" | custom-call | flops 805306368 | bytes 8388608 | tf_op jit(solution)/shard_map/pallas_call | solution.py:721
  154.8 1.5 collective-permute-start.6
  156.3 1.1 slice.23
  157.4 0.1 collective-permute-start.9
  157.5 0.5 collective-permute-start.7
  158.0 0.1 collective-permute-start.8
  158.1 1.8 collective-permute-done.7.refs_16_
  159.8 0.2 collective-permute-done.8.refs_18_
  160.1 1.2 shard_map.311
  161.3 23.6 %all_to_all.40.pieces = bf16[16,352,128]{2,1,0:T(8,128)(2,1)S(1)} all-to-all(bf16[16,352,128]{2,1,0:T(8,128)(2,1)S(1)} %shard_map.311), channel_id=1, replica_groups=mesh['x'=4,'c'=2,'z'=4,'y'=4] {'z','y'}, dimensions={0} | all-to-all | bytes 2883584 | tf_op jit(solution)/shard_map/all_to_all | solution.py:738
  184.9 0.0 copy-start.5
  184.9 0.0 copy-start.7
  185.0 0.0 copy-start.8
  185.0 0.0 copy-start.11
  185.1 0.2 shard_map.312
  185.3 10.0 %all_to_all.41.grads_own = bf16[4,352,128]{2,1,0:T(8,128)(2,1)S(1)} all-to-all(bf16[4,352,128]{2,1,0:T(8,128)(2,1)S(1)} %shard_map.312), channel_id=1, replica_groups=mesh['x'=4,'c'=2,'z'=4,'y'=4] {'x'}, dimensions={0} | all-to-all | bytes 720896 | tf_op jit(solution)/shard_map/all_to_all | solution.py:885
  195.3 3.0 %collective-permute-start.10 = (bf16[4,352,128]{2,1,0:T(8,128)(2,1)S(1)}, bf16[4,352,128]{2,1,0:T(8,128)(2,1)S(1)}, u32[]{:S(2)}, u32[]{:S(2)}) collective-permute-start(bf16[4,352,128]{2,1,0:T(8,128)(2,1)S(1)} %all_to_all.41.grads_own), channel_id=1, source_target_pairs={{0,16},{16,0},{1,17},{17,1},{2,18},{18,2},{3,19},{19,3},{4,20},{20... | collective-permute-start | bytes 1081352 | tf_op jit(solution)/shard_map/ppermute | solution.py:742
  198.3 1.3 collective-permute-done.10.grads_other
  199.7 2.5 %shard_map.313 = (bf16[256,512]{1,0:T(8,128)(2,1)}, bf16[256,512]{1,0:T(8,128)(2,1)}, f32[96,512]{1,0:T(8,128)}, f32[32,512]{1,0:T(8,128)}, f32[512,128]{1,0:T(8...) custom-call(s32[3]{0:T(128)S(1)} %pad_add_fusion.scalars, ...), custom_call_target="tpu_custom_call" | custom-call | bytes 8388608 | tf_op jit(solution)/shard_map/pallas_call | solution.py:721
  (43 shorter events, 0.1 us)
Async XLA Ops:
  7.2 72.9 %all-gather.3.cloned.1.call-start = ((), (), s32[]{:S(2)}) async-start(), calls=%async_computation.9 | async-start | bytes 2949120 | tf_op jit(solution)/shard_map/all_gather | solution.py:785
  38.3 3.0 %copy-start.18 = (s32[1,2]{1,0:T(1,128)S(1)}, s32[1,2]{1,0:T(1,128)}, u32[]{:S(2)}) copy-start(s32[1,2]{1,0:T(1,128)} %lens_own.5) | copy-start | bytes 28
  39.2 117.1 %reduce-scatter.2.cloned.1.call-start = ((), (), s32[]{:S(2)}) async-start(), calls=%async_computation.8 | async-start | bytes 5898240 | tf_op jit(solution)/shard_map/reduce_scatter | solution.py:844
  39.3 4.3 %collective-permute-start = (bf16[16,208,128]{2,1,0:T(8,128)(2,1)S(1)}, bf16[16,208,128]{2,1,0:T(8,128)(2,1)S(1)}, u32[]{:S(2)}, u32[]{:S(2)}) collective-permute-start(bf16[16,208,128]{2,1,0:T(8,128)(2,1)S(1)} %slice.21), channel_id=1, source_target_pairs={{0,16},{16,0},{1,17},{17,1},{2,18},{18,2},{3,19},{19,3},{4,20},{20... | collective-permute-start | bytes 2555912 | tf_op jit(solution)/shard_map/ppermute | solution.py:742
  41.2 2.4 %collective-permute-start.2 = (bf16[2,128,512]{2,1,0:T(8,128)(2,1)S(1)}, bf16[2,128,512]{2,1,0:T(8,128)(2,1)S(1)}, u32[]{:S(2)}, u32[]{:S(2)}) collective-permute-start(bf16[2,128,512]{2,1,0:T(8,128)(2,1)S(1)} %get-tuple-element.66), channel_id=1, source_target_pairs={{0,16},{16,0},{1,17},{17,1},{2,18},{18,2},{3,19},{19,3},{4,20},{20... | collective-permute-start | bytes 786440 | tf_op jit(solution)/shard_map/ppermute | solution.py:742
  41.3 2.3 %collective-permute-start.1 = (s32[1,2]{1,0:T(1,128)S(1)}, s32[1,2]{1,0:T(1,128)S(1)}, u32[]{:S(2)}, u32[]{:S(2)}) collective-permute-start(s32[1,2]{1,0:T(1,128)S(1)} %copy-done.18), channel_id=1, source_target_pairs={{0,16},{16,0},{1,17},{17,1},{2,18},{18,2},{3,19},{19,3},{4,20},{20... | collective-permute-start | bytes 32 | tf_op jit(solution)/shard_map/ppermute | solution.py:742
  43.6 19.6 %copy-start = (bf16[2,128,512]{2,1,0:T(8,128)(2,1)}, bf16[2,128,512]{2,1,0:T(8,128)(2,1)S(1)}, u32[]{:S(2)}) copy-start(bf16[2,128,512]{2,1,0:T(8,128)(2,1)S(1)} %collective-permute-done.2.rows_other.rows_in) | copy-start | bytes 786436
  63.2 3.4 %collective-permute-start.3 = (bf16[16,192,128]{2,1,0:T(8,128)(2,1)S(1)}, bf16[16,192,128]{2,1,0:T(8,128)(2,1)S(1)}, u32[]{:S(2)}, u32[]{:S(2)}) collective-permute-start(bf16[16,192,128]{2,1,0:T(8,128)(2,1)S(1)} %all_to_all.36.pieces), channel_id=1, source_target_pairs={{0,16},{16,0},{1,17},{17,1},{2,18},{18,2},{3,19},{19,3},{4,20},{20... | collective-permute-start | bytes 2359304 | tf_op jit(solution)/shard_map/ppermute | solution.py:742
  80.1 11.4 %collective-permute-start.4 = (bf16[4,16,144,128]{3,2,1,0:T(8,128)(2,1)}, bf16[4,16,144,128]{3,2,1,0:T(8,128)(2,1)S(1)}, u32[]{:S(2)}, u32[]{:S(2)}) collective-permute-start(bf16[4,16,144,128]{3,2,1,0:T(8,128)(2,1)} %bitcast.30), channel_id=1, source_target_pairs={{0,16},{16,0},{1,17},{17,1},{2,18},{18,2},{3,19},{19,3},{4,20},{20... | collective-permute-start | bytes 7077896 | tf_op jit(solution)/shard_map/ppermute | solution.py:742
  128.7 4.4 %collective-permute-start.5 = (bf16[16,128,128]{2,1,0:T(8,128)(2,1)S(1)}, bf16[16,128,128]{2,1,0:T(8,128)(2,1)S(1)}, u32[]{:S(2)}, u32[]{:S(2)}) collective-permute-start(bf16[16,128,128]{2,1,0:T(8,128)(2,1)S(1)} %get-tuple-element.80), channel_id=1, source_target_pairs={{0,16},{16,0},{1,17},{17,1},{2,18},{18,2},{3,19},{19,3},{4,20},{20... | collective-permute-start | bytes 1572872 | tf_op jit(solution)/shard_map/ppermute | solution.py:742
  149.7 7.8 %copy-start.19 = (bf16[128,512]{1,0:T(8,128)(2,1)S(1)}, bf16[128,512]{1,0:T(8,128)(2,1)}, u32[]{:S(2)}) copy-start(bf16[128,512]{1,0:T(8,128)(2,1)} %get-tuple-element.86) | copy-start | bytes 393220
  154.8 5.3 %collective-permute-start.6 = (bf16[16,208,128]{2,1,0:T(8,128)(2,1)S(1)}, bf16[16,208,128]{2,1,0:T(8,128)(2,1)S(1)}, u32[]{:S(2)}, u32[]{:S(2)}) collective-permute-start(bf16[16,208,128]{2,1,0:T(8,128)(2,1)S(1)} %get-tuple-element.85), channel_id=1, source_target_pairs={{0,16},{16,0},{1,17},{17,1},{2,18},{18,2},{3,19},{19,3},{4,20},{20... | collective-permute-start | bytes 2555912 | tf_op jit(solution)/shard_map/ppermute | solution.py:742
  157.4 2.7 %collective-permute-start.9 = (bf16[16,144,128]{2,1,0:T(8,128)(2,1)S(1)}, bf16[16,144,128]{2,1,0:T(8,128)(2,1)S(1)}, u32[]{:S(2)}, u32[]{:S(2)}) collective-permute-start(bf16[16,144,128]{2,1,0:T(8,128)(2,1)S(1)} %bitcast.29), channel_id=1, source_target_pairs={{0,16},{16,0},{1,17},{17,1},{2,18},{18,2},{3,19},{19,3},{4,20},{20... | collective-permute-start | bytes 1769480 | tf_op jit(solution)/shard_map/ppermute | solution.py:742
  157.5 2.3 %collective-permute-start.7 = (bf16[128,512]{1,0:T(8,128)(2,1)S(1)}, bf16[128,512]{1,0:T(8,128)(2,1)S(1)}, u32[]{:S(2)}, u32[]{:S(2)}) collective-permute-start(bf16[128,512]{1,0:T(8,128)(2,1)S(1)} %copy-done.19), channel_id=1, source_target_pairs={{0,16},{16,0},{1,17},{17,1},{2,18},{18,2},{3,19},{19,3},{4,20},{20... | collective-permute-start | bytes 393224 | tf_op jit(solution)/shard_map/ppermute | solution.py:742
  158.0 2.1 collective-permute-start.8
  161.3 38.3 %copy-start.13 = (f32[512,32]{0,1:T(8,128)S(1)}, f32[512,32]{0,1:T(8,128)}, u32[]{:S(2)}) copy-start(f32[512,32]{0,1:T(8,128)} %param.27) | copy-start | bytes 196612
  161.3 38.3 %copy-start.14 = (f32[512,32]{0,1:T(8,128)S(1)}, f32[512,32]{0,1:T(8,128)}, u32[]{:S(2)}) copy-start(f32[512,32]{0,1:T(8,128)} %param.32) | copy-start | bytes 196612
  184.9 14.7 %copy-start.1 = (f32[512,128]{1,0:T(8,128)S(1)}, f32[512,128]{1,0:T(8,128)}, u32[]{:S(2)}) copy-start(f32[512,128]{1,0:T(8,128)} %refs_2_.1) | copy-start | bytes 786436
  184.9 14.7 %copy-start.2 = (f32[128,512]{1,0:T(8,128)S(1)}, f32[128,512]{1,0:T(8,128)}, u32[]{:S(2)}) copy-start(f32[128,512]{1,0:T(8,128)} %refs_3_.1) | copy-start | bytes 786436
  184.9 14.7 %copy-start.3 = (f32[512,96]{0,1:T(8,128)S(1)}, f32[512,96]{0,1:T(8,128)}, u32[]{:S(2)}) copy-start(f32[512,96]{0,1:T(8,128)} %param.21) | copy-start | bytes 589828
  184.9 14.7 %copy-start.4 = (f32[512,32]{0,1:T(8,128)S(1)}, f32[512,32]{0,1:T(8,128)}, u32[]{:S(2)}) copy-start(f32[512,32]{0,1:T(8,128)} %param.22) | copy-start | bytes 196612
  184.9 14.7 %copy-start.5 = (f32[512,128]{1,0:T(8,128)S(1)}, f32[512,128]{1,0:T(8,128)}, u32[]{:S(2)}) copy-start(f32[512,128]{1,0:T(8,128)} %refs_7_.1) | copy-start | bytes 786436
  184.9 14.7 %copy-start.6 = (f32[128,512]{1,0:T(8,128)S(1)}, f32[128,512]{1,0:T(8,128)}, u32[]{:S(2)}) copy-start(f32[128,512]{1,0:T(8,128)} %refs_8_.1) | copy-start | bytes 786436
  184.9 14.7 %copy-start.7 = (f32[512,128]{1,0:T(8,128)S(1)}, f32[512,128]{1,0:T(8,128)}, u32[]{:S(2)}) copy-start(f32[512,128]{1,0:T(8,128)} %refs_12_.1) | copy-start | bytes 786436
  185.0 14.7 %copy-start.8 = (f32[128,512]{1,0:T(8,128)S(1)}, f32[128,512]{1,0:T(8,128)}, u32[]{:S(2)}) copy-start(f32[128,512]{1,0:T(8,128)} %refs_13_.1) | copy-start | bytes 786436
  185.0 14.7 %copy-start.9 = (f32[512,96]{0,1:T(8,128)S(1)}, f32[512,96]{0,1:T(8,128)}, u32[]{:S(2)}) copy-start(f32[512,96]{0,1:T(8,128)} %param.26) | copy-start | bytes 589828
  185.0 14.7 %copy-start.10 = (f32[512,96]{0,1:T(8,128)S(1)}, f32[512,96]{0,1:T(8,128)}, u32[]{:S(2)}) copy-start(f32[512,96]{0,1:T(8,128)} %param.31) | copy-start | bytes 589828
  185.0 14.7 %copy-start.11 = (bf16[128,512]{1,0:T(8,128)(2,1)S(1)}, bf16[128,512]{1,0:T(8,128)(2,1)}, u32[]{:S(2)}) copy-start(bf16[128,512]{1,0:T(8,128)(2,1)} %get-tuple-element.90.refs_15_) | copy-start | bytes 393220
  185.0 14.7 %copy-start.12 = (bf16[128,512]{1,0:T(8,128)(2,1)S(1)}, bf16[128,512]{1,0:T(8,128)(2,1)}, u32[]{:S(2)}) copy-start(bf16[128,512]{1,0:T(8,128)(2,1)} %get-tuple-element.92.refs_17_) | copy-start | bytes 393220
  185.0 14.7 %copy-start.15 = (f32[12,32]{1,0:T(8,128)S(1)}, f32[12,32]{1,0:T(8,128)}, u32[]{:S(2)}) copy-start(f32[12,32]{1,0:T(8,128)} %refs_4_.1) | copy-start | bytes 4612
  185.0 14.7 %copy-start.16 = (f32[12,32]{1,0:T(8,128)S(1)}, f32[12,32]{1,0:T(8,128)}, u32[]{:S(2)}) copy-start(f32[12,32]{1,0:T(8,128)} %refs_9_.1) | copy-start | bytes 4612
  185.0 14.6 %copy-start.17 = (f32[12,32]{1,0:T(8,128)S(1)}, f32[12,32]{1,0:T(8,128)}, u32[]{:S(2)}) copy-start(f32[12,32]{1,0:T(8,128)} %refs_14_.1) | copy-start | bytes 4612
  195.3 4.3 %collective-permute-start.10 = (bf16[4,352,128]{2,1,0:T(8,128)(2,1)S(1)}, bf16[4,352,128]{2,1,0:T(8,128)(2,1)S(1)}, u32[]{:S(2)}, u32[]{:S(2)}) collective-permute-start(bf16[4,352,128]{2,1,0:T(8,128)(2,1)S(1)} %all_to_all.41.grads_own), channel_id=1, source_target_pairs={{0,16},{16,0},{1,17},{17,1},{2,18},{18,2},{3,19},{19,3},{4,20},{20... | collective-permute-start | bytes 1081352 | tf_op jit(solution)/shard_map/ppermute | solution.py:742
Sparse Core Ops, SparseCore 0:
  39.3 31.5 all-gather.2
  102.2 49.1 reduce-scatter.1

commit v4 on v3

--- a/solution.py
+++ b/solution.py
@@ -100,7 +100,11 @@
     lanes = pl.ds(pl.multiple_of(scalars[1] * 128, 128), 128)
     away = pl.ds(pl.multiple_of((1 - core) * HALF, HALF), HALF)
     pairs = (
-        (qkv_in, qkv), (up_in, up), (down_in, down), (proj_in, proj), (small_in, small),
+        (qkv_in.at[pl.ds(pl.multiple_of(core * 48, 16), 48)], qkv),
+        (up_in.at[lanes], up),
+        (down_in.at[:, lanes], down),
+        (proj_in.at[pl.ds(pl.multiple_of(core * 16, 16), 16), lanes], proj),
+        (small_in, small),
         (tokens_in.at[away], rows.at[0]), (cotangent_in.at[away], rows.at[1]),
     )
     for copy in fetch(pairs, done):
@@ -111,20 +115,18 @@
     small_block[0:12, 0:32] = small[...]
     for part in range(4):
         columns = slice(part * 128, part * 128 + 128)
-        half = jnp.where(first_core, qkv[0:48, columns], qkv[48:96, columns])
-        block[part * 48 : part * 48 + 48, :] = bfloat(half)
+        block[part * 48 : part * 48 + 48, :] = bfloat(qkv[:, columns])
     block[192:208, :] = bfloat(small_block[...])
-    half = jnp.where(first_core, up[lanes, :].T, down[:, lanes])
+    half = jnp.where(first_core, up[...].T, down[...])
     block[208:336, :] = bfloat(half)
-    half = jnp.where(first_core, proj[0:16, lanes], proj[16:32, lanes])
-    block[336:352, :] = bfloat(half)
+    block[336:352, :] = bfloat(proj[...])
     for owner in range(16):
         send[owner] = block[...]
 
 
 def qkv_kernel(
-    scalars, tokens_in, rows_other, wide_own, wide_other, send, weights_out, small_out,
-    tokens, weights, small, done, stored,
+    scalars, tokens_in, rows_other, wide_own, wide_other, send, weights, small_out,
+    tokens, small, done, stored,
 ):
     copies = fetch(((tokens_in, tokens),), done)
     first_core = scalars[0] == 0
@@ -157,7 +159,7 @@
             keep = (lane >= inside * 32) & (lane < inside * 32 + 32)
             total = jnp.where(keep, moved, total)
         small[:, block * 128 : block * 128 + 128] = total
-    stores = fetch(((weights, weights_out), (small, small_out)), stored)
+    stores = fetch(((small, small_out),), stored)
     for copy in copies:
         copy.wait()
     unit, _ = normed(f32(mixed_rows(scalars[0], tokens, rows_other[0])))
@@ -427,8 +429,8 @@
 def middle_kernel(
     scalars, lens_own, lens_other, attended_in, tokens_in, cotangent_in, rows_in, later_in,
     later_other, small_in,
-    out_own_hbm, out_away_hbm, send, grad_resid_hbm, small_hbm, grads_out,
-    w_proj, grads, out_own, out_away, tokens, cotangent, rows_other, later_own, small, grad_resid_out, grad_small,
+    out_own_hbm, out_away_hbm, send, grad_resid_out, small_hbm, grads_out,
+    w_proj, grads, out_own, out_away, tokens, cotangent, rows_other, later_own, small, grad_small,
     done, fetched,
 ):
     pairs = (
@@ -530,10 +532,9 @@
     grad_small[6:7, :] = grad_bias
     grad_small[7:8, :] = jnp.sum(grad_out, axis=0, keepdims=True)
     pairs = (
-        (grad_resid_out, grad_resid_hbm), (grad_small, small_hbm),
-        (out_own, out_own_hbm), (out_away, out_away_hbm),
-    )
-    stores = fetch(pairs, done.at[pl.ds(5, 4)])
+        (grad_small, small_hbm), (out_own, out_own_hbm), (out_away, out_away_hbm),
+    )
+    stores = fetch(pairs, done.at[pl.ds(5, 3)])
     grad_attended = f32(bfloat(dot(grad_resid_b, w_proj[...], NN)))
     for pair in range(4):
         columns = slice(pair * 128, pair * 128 + 128)
@@ -555,18 +556,17 @@
 
 
 def last_kernel(
-    scalars, pieces, tokens_in, rows_in, weights_in, small_in, grad_resid_in, part_in,
+    scalars, pieces, tokens_in, rows_in, weights, small_in, grad_resid, part_in,
     grad_in_own_hbm, grad_in_away_hbm, grads_own, grads_away,
-    grad_in_own, grad_in_away, tokens, rows_other, weights, small, grad_resid, part_small, grads, done,
+    grad_in_own, grad_in_away, tokens, rows_other, small, part_small, grads, done,
 ):
     pairs = (
-        (weights_in, weights), (tokens_in, tokens), (rows_in, rows_other), (small_in, small),
-        (grad_resid_in, grad_resid), (part_in, part_small),
+        (tokens_in, tokens), (rows_in, rows_other), (small_in, small), (part_in, part_small)
     )
     copies = fetch(pairs, done)
     core = scalars[0]
     slots = (core, 1 - core)
-    for copy in copies[1:4]:
+    for copy in copies:
         copy.wait()
     unit, scale = normed(f32(mixed_rows(core, tokens, rows_other[0])))
     hidden = bfloat(unit * small[0:1, :] + small[1:2, :])
@@ -603,8 +603,6 @@
         first = 512 + head * HEAD_DIM
         store(bfloat(dot(both, hidden, TN)), (first, first + 512))
         parts_all.append((both, rows))
-    for copy in copies[0:1] + copies[4:6]:
-        copy.wait()
     for part, rows in parts_all:
         grad_hidden = grad_hidden + dot(part, weights[rows, :], NN)
     grad_norm, grad_gain, grad_bias = norm_back(unit, scale, small[0:1, :], grad_hidden)
@@ -612,7 +610,7 @@
     grad_in_own[...] = jnp.where(core == 0, grad_in[0:HALF], grad_in[HALF:ROWS])
     grad_in_away[...] = jnp.where(core == 0, grad_in[HALF:ROWS], grad_in[0:HALF])
     pairs = ((grad_in_own, grad_in_own_hbm), (grad_in_away, grad_in_away_hbm))
-    stores = fetch(pairs, done.at[pl.ds(6, 2)])
+    stores = fetch(pairs, done.at[pl.ds(4, 2)])
     row = lax.broadcasted_iota(jnp.int32, (16, 128), 0)
     lane = lax.broadcasted_iota(jnp.int32, (16, 128), 1)
     for block in range(4):
@@ -768,10 +766,10 @@
         [((16, BLOCK, 128), kind), ((2, HALF, WIDTH), kind)],
         [
             pair_kind,
-            pltpu.VMEM((96, WIDTH), single),
-            pltpu.VMEM((32, WIDTH), single),
-            pltpu.VMEM((WIDTH, 128), single),
-            pltpu.VMEM((128, WIDTH), single),
+            pltpu.VMEM((48, WIDTH), single),
+            pltpu.VMEM((16, 128), single),
+            pltpu.VMEM((128, 128), single),
+            pltpu.VMEM((128, 128), single),
             pltpu.VMEM((12, 32), single),
             pltpu.VMEM((BLOCK, 128), kind),
             pltpu.VMEM((16, 128), single),
@@ -789,10 +787,10 @@
         qkv_kernel,
         [((16, 192, 128), kind), ((1536, WIDTH), kind), ((16, WIDTH), single)],
         [
-            rows_kind, pltpu.VMEM((1536, WIDTH), kind), small_kind,
-            pltpu.SemaphoreType.DMA((1,)), pltpu.SemaphoreType.DMA((2,)),
+            rows_kind, small_kind,
+            pltpu.SemaphoreType.DMA((1,)), pltpu.SemaphoreType.DMA((1,)),
         ],
-        hbm_in=(1,), hbm_out=(1, 2), flops=2 * 256 * 512 * 1536, moved=6 << 20,
+        hbm_in=(1,), hbm_out=(2,), flops=2 * 256 * 512 * 1536, moved=6 << 20,
     )(scalars, tokens, rows_other, first_own, first_other)
     pieces = exchange(send)
     kept = [
@@ -830,12 +828,11 @@
             rows_kind, rows_kind, pair_kind,
             pltpu.VMEM((4, 16, 144, 128), kind),
             small_kind,
-            pltpu.VMEM((ROWS, WIDTH), single),
             small_kind,
-            pltpu.SemaphoreType.DMA((9,)),
+            pltpu.SemaphoreType.DMA((8,)),
             pltpu.SemaphoreType.DMA((6,)),
         ],
-        scalars=3, hbm_in=(4, 5, 6, 7, 9), hbm_out=(0, 1, 3, 4, 5),
+        scalars=3, hbm_in=(4, 5, 6, 7, 9), hbm_out=(0, 1, 4, 5),
         flops=2 * 256 * 512 * (3 * 512 + 6 * 2048), moved=12 << 20, vmem_mib=32,
     )(
         scalars, lengths, lens_other, attended, tokens, cotangent, rows_other,
@@ -862,11 +859,10 @@
         [((HALF, WIDTH), kind), ((HALF, WIDTH), kind)] + [((16, EARLY, 128), kind)] * 2,
         [
             pltpu.VMEM((HALF, WIDTH), kind), pltpu.VMEM((HALF, WIDTH), kind),
-            rows_kind, pair_kind, pltpu.VMEM((1536, WIDTH), kind), small_kind,
-            pltpu.VMEM((ROWS, WIDTH), single), small_kind,
-            pltpu.VMEM((2, 16, EARLY, 128), kind), pltpu.SemaphoreType.DMA((8,)),
+            rows_kind, pair_kind, small_kind, small_kind,
+            pltpu.VMEM((2, 16, EARLY, 128), kind), pltpu.SemaphoreType.DMA((6,)),
         ],
-        hbm_in=(2, 3, 4, 5, 6, 7), hbm_out=(0, 1), flops=4 * 256 * 512 * 1536, moved=8 << 20,
+        hbm_in=(2, 3, 5, 7), hbm_out=(0, 1), flops=4 * 256 * 512 * 1536, moved=8 << 20,
     )(scalars, pieces, tokens, rows_other, weights, small, grad_resid, part_small)
 
     late_other, out_other, grad_in_other = lax.optimization_barrier(

time: 210 us -> 209 us (level)
  no operation moved by 1% of the time
where the time goes in v4:
time: 209 us
  blocking collectives  117 us (56%)
  Pallas kernels  54.2 us (26%)
  between operations  14.4 us (7%)
  starting transfers between devices  12.5 us (6%)
  waiting for transfers between devices  8.64 us (4%)
  local copies, waits for them, and re-layouts  2.14 us (1%)
    all_to_all x6, blocking collectives, exchange(): return lax.all_to_all(values, CTX, 0, 0, tiled=True)  107 us
    pallas_call x9, Pallas kernels, run(): pl.pallas_call(kernel, out_shape=[pltpu.HBM(shape, kind) if index in hbm_...  54.2 us
    ppermute x11, starting transfers between devices, swap_cores(): return lax.ppermute(values, 'c', [(0, 1), (1, 0)])  12.5 us
    all_to_all x1, blocking collectives, on_device(): grads_own = lax.all_to_all(sums, 'x', 0, 0, tiled=True)  10 us
    ppermute x11, waiting for transfers between devices, swap_cores(): return lax.ppermute(values, 'c', [(0, 1), (1, 0)])  8.59 us
  transfers between devices with their start and end apart: 13, of which 6 were waited for; matrix products, arithmetic and copies ran while one was open for 1% of the time, Pallas kernels for 18%

profile of v4, /device:TPU:1, one launch (start us, length us, event | category | flops | bytes accessed | tf_op | source)
XLA Modules:
  0.0 208.8 jit_solution(11740770612107583613)
XLA Ops:
  7.2 0.0 all-gather.3.cloned.1.call-start
  7.2 0.1 pad_add_fusion.scalars
  7.3 1.9 shard_map.305
  9.3 28.9 %all_to_all.35.wide_own = bf16[16,352,128]{2,1,0:T(8,128)(2,1)S(1)} all-to-all(bf16[16,352,128]{2,1,0:T(8,128)(2,1)S(1)} %get-tuple-element.64), channel_id=1, replica_groups=mesh['x'=4,'c'=2,'z'=4,'y'=4] {'z','y'}, dimensions={0} | all-to-all | bytes 2883584 | tf_op jit(solution)/shard_map/all_to_all | solution.py:736
  38.2 0.9 slice.22
  39.0 0.0 all-gather.3.cloned.1.call-update
  39.0 0.0 reduce-scatter.2.cloned.1.call-start
  39.1 0.1 slice.21
  39.2 1.9 collective-permute-start
  41.1 0.1 collective-permute-start.2
  41.2 0.4 collective-permute-start.1
  41.6 1.9 collective-permute-done.1.lens_other
  43.5 2.7 %shard_map.306 = (bf16[16,192,128]{2,1,0:T(8,128)(2,1)S(1)}, bf16[1536,512]{1,0:T(8,128)(2,1)S(1)}, f32[16,512]{1,0:T(8,128)}) custom-call(s32[3]{0:T(128)S(1)} %pad_add_fusion.scalars, bf16[256,512]{1,0:T(8,128)(2,1)} %tokens_in.7, bf16[2,128,512]{2,1,0:T(8,128)(2,1)S(1)} %collective-permute-done.2.rows_other.rows_in, ...), custom_call_target="tpu_custom_call" | custom-call | flops 402653184 | bytes 6291456 | tf_op jit(solution)/shard_map/pallas_call | solution.py:719
  46.2 16.4 %all_to_all.36.pieces = bf16[16,192,128]{2,1,0:T(8,128)(2,1)S(1)} all-to-all(bf16[16,192,128]{2,1,0:T(8,128)(2,1)S(1)} %get-tuple-element.68), channel_id=1, replica_groups=mesh['x'=4,'c'=2,'z'=4,'y'=4] {'z','y'}, dimensions={0} | all-to-all | bytes 1572864 | tf_op jit(solution)/shard_map/all_to_all | solution.py:736
  62.6 1.5 collective-permute-start.3
  64.1 1.9 collective-permute-done.3.others
  66.0 13.5 %shard_map.307 = (bf16[16,64,128]{2,1,0:T(8,128)(2,1)S(1)}, bf16[4096,128]{1,0:T(8,128)(2,1)}, bf16[4096,128]{1,0:T(8,128)(2,1)}, bf16[128,4096]{1,0:T(8,128)(2,...) custom-call(s32[3]{0:T(128)S(1)} %pad_add_fusion.scalars, s32[1,2]{1,0:T(1,128)S(1)} %copy-done.18, ...), custom_call_target="tpu_custom_call" | custom-call | flops 4831838208 | bytes 4194304 | tf_op jit(solution)/shard_map/pallas_call | solution.py:719
  79.5 0.0 all-gather.3.cloned.1.call-done
  79.5 0.5 collective-permute-start.4
  80.0 11.0 %all_to_all.37.attended_in = bf16[16,64,128]{2,1,0:T(8,128)(2,1)S(1)} all-to-all(bf16[16,64,128]{2,1,0:T(8,128)(2,1)S(1)} %get-tuple-element.75), channel_id=1, replica_groups=mesh['x'=4,'c'=2,'z'=4,'y'=4] {'z','y'}, dimensions={0} | all-to-all | bytes 524288 | tf_op jit(solution)/shard_map/all_to_all | solution.py:736
  91.0 10.4 %shard_map.308 = (bf16[128,512]{1,0:T(8,128)(2,1)}, bf16[128,512]{1,0:T(8,128)(2,1)}, bf16[16,64,128]{2,1,0:T(8,128)(2,1)S(1)}, f32[256,512]{1,0:T(8,128)S(1)}, ...) custom-call(s32[3]{0:T(128)S(1)} %pad_add_fusion.scalars, s32[1,2]{1,0:T(1,128)S(1)} %copy-done.18, ...), custom_call_target="tpu_custom_call" | custom-call | flops 3623878656 | bytes 12582912 | tf_op jit(solution)/shard_map/pallas_call | solution.py:719
  101.4 0.0 reduce-scatter.2.cloned.1.call-update
  101.4 10.3 %all_to_all.38.grads = bf16[16,64,128]{2,1,0:T(8,128)(2,1)S(1)} all-to-all(bf16[16,64,128]{2,1,0:T(8,128)(2,1)S(1)} %get-tuple-element.78), channel_id=1, replica_groups=mesh['x'=4,'c'=2,'z'=4,'y'=4] {'z','y'}, dimensions={0} | all-to-all | bytes 524288 | tf_op jit(solution)/shard_map/all_to_all | solution.py:736
  111.7 16.4 %shard_map.309 = (bf16[16,192,128]{2,1,0:T(8,128)(2,1)S(1)}, bf16[16,128,128]{2,1,0:T(8,128)(2,1)S(1)}) custom-call(s32[3]{0:T(128)S(1)} %pad_add_fusion.scalars, s32[1,2]{1,0:T(1,128)S(1)} %copy-done.18, s32[1,2]{1,0:T(1,128)S(1)} %collective-permute-done.1.lens_other, bf16[16,192,128]{2,1,0:T(8,128)(2,1)S(1)} %all_to_all.36.pieces, ...), custom_call_target="tpu_custom_call" | custom-call | flops 12079595520 | bytes 5242880 | tf_op jit(solution)/shard_map/pallas_call | solution.py:719
  128.1 2.9 %collective-permute-start.5 = (bf16[16,128,128]{2,1,0:T(8,128)(2,1)S(1)}, bf16[16,128,128]{2,1,0:T(8,128)(2,1)S(1)}, u32[]{:S(2)}, u32[]{:S(2)}) collective-permute-start(bf16[16,128,128]{2,1,0:T(8,128)(2,1)S(1)} %get-tuple-element.80), channel_id=1, source_target_pairs={{0,16},{16,0},{1,17},{17,1},{2,18},{18,2},{3,19},{19,3},{4,20},{20... | collective-permute-start | bytes 1572872 | tf_op jit(solution)/shard_map/ppermute | solution.py:740
  131.0 1.5 collective-permute-done.5
  132.5 0.1 add_convert_fusion
  132.6 0.1 pad_maximum_fusion
  132.7 16.4 %all_to_all.39.pieces = bf16[16,192,128]{2,1,0:T(8,128)(2,1)S(1)} all-to-all(bf16[16,192,128]{2,1,0:T(8,128)(2,1)S(1)} %pad_maximum_fusion), channel_id=1, replica_groups=mesh['x'=4,'c'=2,'z'=4,'y'=4] {'z','y'}, dimensions={0} | all-to-all | bytes 1572864 | tf_op jit(solution)/shard_map/all_to_all | solution.py:736
  149.1 5.3 %shard_map.310 = (bf16[128,512]{1,0:T(8,128)(2,1)}, bf16[128,512]{1,0:T(8,128)(2,1)}, bf16[16,208,128]{2,1,0:T(8,128)(2,1)S(1)}, bf16[16,208,128]{2,1,0:T(8,128)(2,1)}) custom-call(s32[3]{0:T(128)S(1)} %pad_add_fusion.scalars, bf16[16,192,128]{2,1,0:T(8,128)(2,1)S(1)} %all_to_all.39.pieces, bf16[256,512]{1,0:T(8,128)(2,1)} %tokens_in.7, ...), custom_call_target="tpu_custom_call" | custom-call | flops 805306368 | bytes 8388608 | tf_op jit(solution)/shard_map/pallas_call | solution.py:719
  154.5 1.6 collective-permute-start.6
  156.0 1.1 slice.23
  157.1 0.1 collective-permute-start.9
  157.2 0.5 collective-permute-start.7
  157.7 0.1 collective-permute-start.8
  157.8 1.8 collective-permute-done.7.refs_16_
  159.6 0.2 collective-permute-done.8.refs_18_
  159.8 1.2 shard_map.311
  161.0 0.0 copy-start.14
  161.0 23.5 %all_to_all.40.pieces = bf16[16,352,128]{2,1,0:T(8,128)(2,1)S(1)} all-to-all(bf16[16,352,128]{2,1,0:T(8,128)(2,1)S(1)} %shard_map.311), channel_id=1, replica_groups=mesh['x'=4,'c'=2,'z'=4,'y'=4] {'z','y'}, dimensions={0} | all-to-all | bytes 2883584 | tf_op jit(solution)/shard_map/all_to_all | solution.py:736
  184.6 0.0 copy-start.7
  184.6 0.0 copy-start.8
  184.7 0.0 copy-start.11
  184.7 0.2 shard_map.312
  184.9 10.0 %all_to_all.41.grads_own = bf16[4,352,128]{2,1,0:T(8,128)(2,1)S(1)} all-to-all(bf16[4,352,128]{2,1,0:T(8,128)(2,1)S(1)} %shard_map.312), channel_id=1, replica_groups=mesh['x'=4,'c'=2,'z'=4,'y'=4] {'x'}, dimensions={0} | all-to-all | bytes 720896 | tf_op jit(solution)/shard_map/all_to_all | solution.py:881
  195.0 3.0 %collective-permute-start.10 = (bf16[4,352,128]{2,1,0:T(8,128)(2,1)S(1)}, bf16[4,352,128]{2,1,0:T(8,128)(2,1)S(1)}, u32[]{:S(2)}, u32[]{:S(2)}) collective-permute-start(bf16[4,352,128]{2,1,0:T(8,128)(2,1)S(1)} %all_to_all.41.grads_own), channel_id=1, source_target_pairs={{0,16},{16,0},{1,17},{17,1},{2,18},{18,2},{3,19},{19,3},{4,20},{20... | collective-permute-start | bytes 1081352 | tf_op jit(solution)/shard_map/ppermute | solution.py:740
  198.0 1.3 collective-permute-done.10.grads_other
  199.4 2.5 %shard_map.313 = (bf16[256,512]{1,0:T(8,128)(2,1)}, bf16[256,512]{1,0:T(8,128)(2,1)}, f32[96,512]{1,0:T(8,128)}, f32[32,512]{1,0:T(8,128)}, f32[512,128]{1,0:T(8...) custom-call(s32[3]{0:T(128)S(1)} %pad_add_fusion.scalars, ...), custom_call_target="tpu_custom_call" | custom-call | bytes 8388608 | tf_op jit(solution)/shard_map/pallas_call | solution.py:719
  (43 shorter events, 0.1 us)
Async XLA Ops:
  7.2 72.4 %all-gather.3.cloned.1.call-start = ((), (), s32[]{:S(2)}) async-start(), calls=%async_computation.9 | async-start | bytes 2949120 | tf_op jit(solution)/shard_map/all_gather | solution.py:783
  38.2 3.0 %copy-start.18 = (s32[1,2]{1,0:T(1,128)S(1)}, s32[1,2]{1,0:T(1,128)}, u32[]{:S(2)}) copy-start(s32[1,2]{1,0:T(1,128)} %lens_own.5) | copy-start | bytes 28
  39.0 117.0 %reduce-scatter.2.cloned.1.call-start = ((), (), s32[]{:S(2)}) async-start(), calls=%async_computation.8 | async-start | bytes 5898240 | tf_op jit(solution)/shard_map/reduce_scatter | solution.py:841
  39.2 4.3 %collective-permute-start = (bf16[16,208,128]{2,1,0:T(8,128)(2,1)S(1)}, bf16[16,208,128]{2,1,0:T(8,128)(2,1)S(1)}, u32[]{:S(2)}, u32[]{:S(2)}) collective-permute-start(bf16[16,208,128]{2,1,0:T(8,128)(2,1)S(1)} %slice.21), channel_id=1, source_target_pairs={{0,16},{16,0},{1,17},{17,1},{2,18},{18,2},{3,19},{19,3},{4,20},{20... | collective-permute-start | bytes 2555912 | tf_op jit(solution)/shard_map/ppermute | solution.py:740
  41.1 2.4 %collective-permute-start.2 = (bf16[2,128,512]{2,1,0:T(8,128)(2,1)S(1)}, bf16[2,128,512]{2,1,0:T(8,128)(2,1)S(1)}, u32[]{:S(2)}, u32[]{:S(2)}) collective-permute-start(bf16[2,128,512]{2,1,0:T(8,128)(2,1)S(1)} %get-tuple-element.66), channel_id=1, source_target_pairs={{0,16},{16,0},{1,17},{17,1},{2,18},{18,2},{3,19},{19,3},{4,20},{20... | collective-permute-start | bytes 786440 | tf_op jit(solution)/shard_map/ppermute | solution.py:740
  41.2 2.3 %collective-permute-start.1 = (s32[1,2]{1,0:T(1,128)S(1)}, s32[1,2]{1,0:T(1,128)S(1)}, u32[]{:S(2)}, u32[]{:S(2)}) collective-permute-start(s32[1,2]{1,0:T(1,128)S(1)} %copy-done.18), channel_id=1, source_target_pairs={{0,16},{16,0},{1,17},{17,1},{2,18},{18,2},{3,19},{19,3},{4,20},{20... | collective-permute-start | bytes 32 | tf_op jit(solution)/shard_map/ppermute | solution.py:740
  43.4 19.2 %copy-start = (bf16[2,128,512]{2,1,0:T(8,128)(2,1)}, bf16[2,128,512]{2,1,0:T(8,128)(2,1)S(1)}, u32[]{:S(2)}) copy-start(bf16[2,128,512]{2,1,0:T(8,128)(2,1)S(1)} %collective-permute-done.2.rows_other.rows_in) | copy-start | bytes 786436
  62.6 3.4 %collective-permute-start.3 = (bf16[16,192,128]{2,1,0:T(8,128)(2,1)S(1)}, bf16[16,192,128]{2,1,0:T(8,128)(2,1)S(1)}, u32[]{:S(2)}, u32[]{:S(2)}) collective-permute-start(bf16[16,192,128]{2,1,0:T(8,128)(2,1)S(1)} %all_to_all.36.pieces), channel_id=1, source_target_pairs={{0,16},{16,0},{1,17},{17,1},{2,18},{18,2},{3,19},{19,3},{4,20},{20... | collective-permute-start | bytes 2359304 | tf_op jit(solution)/shard_map/ppermute | solution.py:740
  79.5 11.4 %collective-permute-start.4 = (bf16[4,16,144,128]{3,2,1,0:T(8,128)(2,1)}, bf16[4,16,144,128]{3,2,1,0:T(8,128)(2,1)S(1)}, u32[]{:S(2)}, u32[]{:S(2)}) collective-permute-start(bf16[4,16,144,128]{3,2,1,0:T(8,128)(2,1)} %bitcast.30), channel_id=1, source_target_pairs={{0,16},{16,0},{1,17},{17,1},{2,18},{18,2},{3,19},{19,3},{4,20},{20... | collective-permute-start | bytes 7077896 | tf_op jit(solution)/shard_map/ppermute | solution.py:740
  128.1 4.4 %collective-permute-start.5 = (bf16[16,128,128]{2,1,0:T(8,128)(2,1)S(1)}, bf16[16,128,128]{2,1,0:T(8,128)(2,1)S(1)}, u32[]{:S(2)}, u32[]{:S(2)}) collective-permute-start(bf16[16,128,128]{2,1,0:T(8,128)(2,1)S(1)} %get-tuple-element.80), channel_id=1, source_target_pairs={{0,16},{16,0},{1,17},{17,1},{2,18},{18,2},{3,19},{19,3},{4,20},{20... | collective-permute-start | bytes 1572872 | tf_op jit(solution)/shard_map/ppermute | solution.py:740
  149.1 8.1 %copy-start.19 = (bf16[128,512]{1,0:T(8,128)(2,1)S(1)}, bf16[128,512]{1,0:T(8,128)(2,1)}, u32[]{:S(2)}) copy-start(bf16[128,512]{1,0:T(8,128)(2,1)} %get-tuple-element.86) | copy-start | bytes 393220
  154.5 5.3 %collective-permute-start.6 = (bf16[16,208,128]{2,1,0:T(8,128)(2,1)}, bf16[16,208,128]{2,1,0:T(8,128)(2,1)S(1)}, u32[]{:S(2)}, u32[]{:S(2)}) collective-permute-start(bf16[16,208,128]{2,1,0:T(8,128)(2,1)} %get-tuple-element.85), channel_id=1, source_target_pairs={{0,16},{16,0},{1,17},{17,1},{2,18},{18,2},{3,19},{19,3},{4,20},{20... | collective-permute-start | bytes 2555912 | tf_op jit(solution)/shard_map/ppermute | solution.py:740
  157.1 2.7 %collective-permute-start.9 = (bf16[16,144,128]{2,1,0:T(8,128)(2,1)S(1)}, bf16[16,144,128]{2,1,0:T(8,128)(2,1)S(1)}, u32[]{:S(2)}, u32[]{:S(2)}) collective-permute-start(bf16[16,144,128]{2,1,0:T(8,128)(2,1)S(1)} %bitcast.29), channel_id=1, source_target_pairs={{0,16},{16,0},{1,17},{17,1},{2,18},{18,2},{3,19},{19,3},{4,20},{20... | collective-permute-start | bytes 1769480 | tf_op jit(solution)/shard_map/ppermute | solution.py:740
  157.2 2.3 %collective-permute-start.7 = (bf16[128,512]{1,0:T(8,128)(2,1)S(1)}, bf16[128,512]{1,0:T(8,128)(2,1)S(1)}, u32[]{:S(2)}, u32[]{:S(2)}) collective-permute-start(bf16[128,512]{1,0:T(8,128)(2,1)S(1)} %copy-done.19), channel_id=1, source_target_pairs={{0,16},{16,0},{1,17},{17,1},{2,18},{18,2},{3,19},{19,3},{4,20},{20... | collective-permute-start | bytes 393224 | tf_op jit(solution)/shard_map/ppermute | solution.py:740
  157.7 2.1 collective-permute-start.8
  161.0 38.3 %copy-start.13 = (f32[512,32]{0,1:T(8,128)S(1)}, f32[512,32]{0,1:T(8,128)}, u32[]{:S(2)}) copy-start(f32[512,32]{0,1:T(8,128)} %param.27) | copy-start | bytes 196612
  161.0 38.2 %copy-start.14 = (f32[512,32]{0,1:T(8,128)S(1)}, f32[512,32]{0,1:T(8,128)}, u32[]{:S(2)}) copy-start(f32[512,32]{0,1:T(8,128)} %param.32) | copy-start | bytes 196612
  184.6 14.7 %copy-start.1 = (f32[512,128]{1,0:T(8,128)S(1)}, f32[512,128]{1,0:T(8,128)}, u32[]{:S(2)}) copy-start(f32[512,128]{1,0:T(8,128)} %refs_2_.1) | copy-start | bytes 786436
  184.6 14.7 %copy-start.2 = (f32[128,512]{1,0:T(8,128)S(1)}, f32[128,512]{1,0:T(8,128)}, u32[]{:S(2)}) copy-start(f32[128,512]{1,0:T(8,128)} %refs_3_.1) | copy-start | bytes 786436
  184.6 14.7 %copy-start.3 = (f32[512,96]{0,1:T(8,128)S(1)}, f32[512,96]{0,1:T(8,128)}, u32[]{:S(2)}) copy-start(f32[512,96]{0,1:T(8,128)} %param.21) | copy-start | bytes 589828
  184.6 14.7 %copy-start.4 = (f32[512,32]{0,1:T(8,128)S(1)}, f32[512,32]{0,1:T(8,128)}, u32[]{:S(2)}) copy-start(f32[512,32]{0,1:T(8,128)} %param.22) | copy-start | bytes 196612
  184.6 14.7 %copy-start.5 = (f32[512,128]{1,0:T(8,128)S(1)}, f32[512,128]{1,0:T(8,128)}, u32[]{:S(2)}) copy-start(f32[512,128]{1,0:T(8,128)} %refs_7_.1) | copy-start | bytes 786436
  184.6 14.7 %copy-start.6 = (f32[128,512]{1,0:T(8,128)S(1)}, f32[128,512]{1,0:T(8,128)}, u32[]{:S(2)}) copy-start(f32[128,512]{1,0:T(8,128)} %refs_8_.1) | copy-start | bytes 786436
  184.6 14.7 %copy-start.7 = (f32[512,128]{1,0:T(8,128)S(1)}, f32[512,128]{1,0:T(8,128)}, u32[]{:S(2)}) copy-start(f32[512,128]{1,0:T(8,128)} %refs_12_.1) | copy-start | bytes 786436
  184.6 14.7 %copy-start.8 = (f32[128,512]{1,0:T(8,128)S(1)}, f32[128,512]{1,0:T(8,128)}, u32[]{:S(2)}) copy-start(f32[128,512]{1,0:T(8,128)} %refs_13_.1) | copy-start | bytes 786436
  184.6 14.7 %copy-start.9 = (f32[512,96]{0,1:T(8,128)S(1)}, f32[512,96]{0,1:T(8,128)}, u32[]{:S(2)}) copy-start(f32[512,96]{0,1:T(8,128)} %param.26) | copy-start | bytes 589828
  184.6 14.7 %copy-start.10 = (f32[512,96]{0,1:T(8,128)S(1)}, f32[512,96]{0,1:T(8,128)}, u32[]{:S(2)}) copy-start(f32[512,96]{0,1:T(8,128)} %param.31) | copy-start | bytes 589828
  184.7 14.7 %copy-start.11 = (bf16[128,512]{1,0:T(8,128)(2,1)S(1)}, bf16[128,512]{1,0:T(8,128)(2,1)}, u32[]{:S(2)}) copy-start(bf16[128,512]{1,0:T(8,128)(2,1)} %get-tuple-element.90.refs_15_) | copy-start | bytes 393220
  184.7 14.7 %copy-start.12 = (bf16[128,512]{1,0:T(8,128)(2,1)S(1)}, bf16[128,512]{1,0:T(8,128)(2,1)}, u32[]{:S(2)}) copy-start(bf16[128,512]{1,0:T(8,128)(2,1)} %get-tuple-element.92.refs_17_) | copy-start | bytes 393220
  184.7 14.7 %copy-start.15 = (f32[12,32]{1,0:T(8,128)S(1)}, f32[12,32]{1,0:T(8,128)}, u32[]{:S(2)}) copy-start(f32[12,32]{1,0:T(8,128)} %refs_4_.1) | copy-start | bytes 4612
  184.7 14.7 %copy-start.16 = (f32[12,32]{1,0:T(8,128)S(1)}, f32[12,32]{1,0:T(8,128)}, u32[]{:S(2)}) copy-start(f32[12,32]{1,0:T(8,128)} %refs_9_.1) | copy-start | bytes 4612
  184.7 14.7 %copy-start.17 = (f32[12,32]{1,0:T(8,128)S(1)}, f32[12,32]{1,0:T(8,128)}, u32[]{:S(2)}) copy-start(f32[12,32]{1,0:T(8,128)} %refs_14_.1) | copy-start | bytes 4612
  195.0 4.3 %collective-permute-start.10 = (bf16[4,352,128]{2,1,0:T(8,128)(2,1)S(1)}, bf16[4,352,128]{2,1,0:T(8,128)(2,1)S(1)}, u32[]{:S(2)}, u32[]{:S(2)}) collective-permute-start(bf16[4,352,128]{2,1,0:T(8,128)(2,1)S(1)} %all_to_all.41.grads_own), channel_id=1, source_target_pairs={{0,16},{16,0},{1,17},{17,1},{2,18},{18,2},{3,19},{19,3},{4,20},{20... | collective-permute-start | bytes 1081352 | tf_op jit(solution)/shard_map/ppermute | solution.py:740
Sparse Core Ops, SparseCore 0:
  39.2 31.5 all-gather.2
  101.5 49.1 reduce-scatter.1

commit v5 on v4

--- a/solution.py
+++ b/solution.py
@@ -557,8 +557,8 @@
 
 def last_kernel(
     scalars, pieces, tokens_in, rows_in, weights, small_in, grad_resid, part_in,
-    grad_in_own_hbm, grad_in_away_hbm, grads_own, grads_away,
-    grad_in_own, grad_in_away, tokens, rows_other, small, part_small, grads, done,
+    grad_in_own, grad_in_away, grads_own, grads_away,
+    tokens, rows_other, small, part_small, grads, done,
 ):
     pairs = (
         (tokens_in, tokens), (rows_in, rows_other), (small_in, small), (part_in, part_small)
@@ -609,8 +609,6 @@
     grad_in = bfloat(grad_resid[...] + grad_norm)
     grad_in_own[...] = jnp.where(core == 0, grad_in[0:HALF], grad_in[HALF:ROWS])
     grad_in_away[...] = jnp.where(core == 0, grad_in[HALF:ROWS], grad_in[0:HALF])
-    pairs = ((grad_in_own, grad_in_own_hbm), (grad_in_away, grad_in_away_hbm))
-    stores = fetch(pairs, done.at[pl.ds(4, 2)])
     row = lax.broadcasted_iota(jnp.int32, (16, 128), 0)
     lane = lax.broadcasted_iota(jnp.int32, (16, 128), 1)
     for block in range(4):
@@ -631,8 +629,6 @@
     for owner in range(16):
         grads_own[owner] = grads[0, owner]
         grads_away[owner] = grads[1, owner]
-    for copy in stores:
-        copy.wait()
 
 
 def combine_kernel(late_own, late_other, early_in, early_other, sums, early, done):
@@ -858,11 +854,10 @@
         last_kernel,
         [((HALF, WIDTH), kind), ((HALF, WIDTH), kind)] + [((16, EARLY, 128), kind)] * 2,
         [
-            pltpu.VMEM((HALF, WIDTH), kind), pltpu.VMEM((HALF, WIDTH), kind),
             rows_kind, pair_kind, small_kind, small_kind,
-            pltpu.VMEM((2, 16, EARLY, 128), kind), pltpu.SemaphoreType.DMA((6,)),
+            pltpu.VMEM((2, 16, EARLY, 128), kind), pltpu.SemaphoreType.DMA((4,)),
         ],
-        hbm_in=(2, 3, 5, 7), hbm_out=(0, 1), flops=4 * 256 * 512 * 1536, moved=8 << 20,
+        hbm_in=(2, 3, 5, 7), flops=4 * 256 * 512 * 1536, moved=8 << 20,
     )(scalars, pieces, tokens, rows_other, weights, small, grad_resid, part_small)
 
     late_other, out_other, grad_in_other = lax.optimization_barrier(

time: 209 us -> 208 us (level)
  no operation moved by 1% of the time
where the time goes in v5:
time: 208 us
  blocking collectives  116 us (56%)
  Pallas kernels  53.6 us (26%)
  between operations  14.4 us (7%)
  starting transfers between devices  12.5 us (6%)
  waiting for transfers between devices  8.43 us (4%)
  local copies, waits for them, and re-layouts  2.15 us (1%)
    all_to_all x6, blocking collectives, exchange(): return lax.all_to_all(values, CTX, 0, 0, tiled=True)  106 us
    pallas_call x9, Pallas kernels, run(): pl.pallas_call(kernel, out_shape=[pltpu.HBM(shape, kind) if index in hbm_...  53.6 us
    ppermute x11, starting transfers between devices, swap_cores(): return lax.ppermute(values, 'c', [(0, 1), (1, 0)])  12.4 us
    all_to_all x1, blocking collectives, on_device(): grads_own = lax.all_to_all(sums, 'x', 0, 0, tiled=True)  10 us
    ppermute x11, waiting for transfers between devices, swap_cores(): return lax.ppermute(values, 'c', [(0, 1), (1, 0)])  8.38 us
  transfers between devices with their start and end apart: 13, of which 6 were waited for; matrix products, arithmetic and copies ran while one was open for 1% of the time, Pallas kernels for 18%

profile of v5, /device:TPU:1, one launch (start us, length us, event | category | flops | bytes accessed | tf_op | source)
XLA Modules:
  0.0 207.9 jit_solution(7920041752413423997)
XLA Ops:
  7.2 0.0 all-gather.3.cloned.1.call-start
  7.2 0.1 pad_add_fusion.scalars
  7.3 1.9 shard_map.305
  9.3 28.9 %all_to_all.35.wide_own = bf16[16,352,128]{2,1,0:T(8,128)(2,1)S(1)} all-to-all(bf16[16,352,128]{2,1,0:T(8,128)(2,1)S(1)} %get-tuple-element.64), channel_id=1, replica_groups=mesh['x'=4,'c'=2,'z'=4,'y'=4] {'z','y'}, dimensions={0} | all-to-all | bytes 2883584 | tf_op jit(solution)/shard_map/all_to_all | solution.py:732
  38.2 0.9 slice.22
  39.0 0.0 all-gather.3.cloned.1.call-update
  39.1 0.0 reduce-scatter.2.cloned.1.call-start
  39.1 0.1 slice.21
  39.2 1.9 collective-permute-start
  41.1 0.1 collective-permute-start.2
  41.2 0.4 collective-permute-start.1
  41.6 1.9 collective-permute-done.1.lens_other
  43.5 2.7 %shard_map.306 = (bf16[16,192,128]{2,1,0:T(8,128)(2,1)S(1)}, bf16[1536,512]{1,0:T(8,128)(2,1)S(1)}, f32[16,512]{1,0:T(8,128)}) custom-call(s32[3]{0:T(128)S(1)} %pad_add_fusion.scalars, bf16[256,512]{1,0:T(8,128)(2,1)} %tokens_in.7, bf16[2,128,512]{2,1,0:T(8,128)(2,1)S(1)} %collective-permute-done.2.rows_other.rows_in, ...), custom_call_target="tpu_custom_call" | custom-call | flops 402653184 | bytes 6291456 | tf_op jit(solution)/shard_map/pallas_call | solution.py:715
  46.2 16.4 %all_to_all.36.pieces = bf16[16,192,128]{2,1,0:T(8,128)(2,1)S(1)} all-to-all(bf16[16,192,128]{2,1,0:T(8,128)(2,1)S(1)} %get-tuple-element.68), channel_id=1, replica_groups=mesh['x'=4,'c'=2,'z'=4,'y'=4] {'z','y'}, dimensions={0} | all-to-all | bytes 1572864 | tf_op jit(solution)/shard_map/all_to_all | solution.py:732
  62.6 1.5 collective-permute-start.3
  64.1 1.9 collective-permute-done.3.others
  66.0 13.5 %shard_map.307 = (bf16[16,64,128]{2,1,0:T(8,128)(2,1)S(1)}, bf16[4096,128]{1,0:T(8,128)(2,1)}, bf16[4096,128]{1,0:T(8,128)(2,1)}, bf16[128,4096]{1,0:T(8,128)(2,...) custom-call(s32[3]{0:T(128)S(1)} %pad_add_fusion.scalars, s32[1,2]{1,0:T(1,128)S(1)} %copy-done.17, ...), custom_call_target="tpu_custom_call" | custom-call | flops 4831838208 | bytes 4194304 | tf_op jit(solution)/shard_map/pallas_call | solution.py:715
  79.5 0.0 all-gather.3.cloned.1.call-done
  79.6 0.5 collective-permute-start.4
  80.0 11.0 %all_to_all.37.attended_in = bf16[16,64,128]{2,1,0:T(8,128)(2,1)S(1)} all-to-all(bf16[16,64,128]{2,1,0:T(8,128)(2,1)S(1)} %get-tuple-element.75), channel_id=1, replica_groups=mesh['x'=4,'c'=2,'z'=4,'y'=4] {'z','y'}, dimensions={0} | all-to-all | bytes 524288 | tf_op jit(solution)/shard_map/all_to_all | solution.py:732
  91.0 10.4 %shard_map.308 = (bf16[128,512]{1,0:T(8,128)(2,1)}, bf16[128,512]{1,0:T(8,128)(2,1)}, bf16[16,64,128]{2,1,0:T(8,128)(2,1)S(1)}, f32[256,512]{1,0:T(8,128)S(1)}, ...) custom-call(s32[3]{0:T(128)S(1)} %pad_add_fusion.scalars, s32[1,2]{1,0:T(1,128)S(1)} %copy-done.17, ...), custom_call_target="tpu_custom_call" | custom-call | flops 3623878656 | bytes 12582912 | tf_op jit(solution)/shard_map/pallas_call | solution.py:715
  101.4 0.0 reduce-scatter.2.cloned.1.call-update
  101.4 10.2 %all_to_all.38.grads = bf16[16,64,128]{2,1,0:T(8,128)(2,1)S(1)} all-to-all(bf16[16,64,128]{2,1,0:T(8,128)(2,1)S(1)} %get-tuple-element.78), channel_id=1, replica_groups=mesh['x'=4,'c'=2,'z'=4,'y'=4] {'z','y'}, dimensions={0} | all-to-all | bytes 524288 | tf_op jit(solution)/shard_map/all_to_all | solution.py:732
  111.7 16.4 %shard_map.309 = (bf16[16,192,128]{2,1,0:T(8,128)(2,1)S(1)}, bf16[16,128,128]{2,1,0:T(8,128)(2,1)S(1)}) custom-call(s32[3]{0:T(128)S(1)} %pad_add_fusion.scalars, s32[1,2]{1,0:T(1,128)S(1)} %copy-done.17, s32[1,2]{1,0:T(1,128)S(1)} %collective-permute-done.1.lens_other, bf16[16,192,128]{2,1,0:T(8,128)(2,1)S(1)} %all_to_all.36.pieces, ...), custom_call_target="tpu_custom_call" | custom-call | flops 12079595520 | bytes 5242880 | tf_op jit(solution)/shard_map/pallas_call | solution.py:715
  128.1 2.9 %collective-permute-start.5 = (bf16[16,128,128]{2,1,0:T(8,128)(2,1)S(1)}, bf16[16,128,128]{2,1,0:T(8,128)(2,1)S(1)}, u32[]{:S(2)}, u32[]{:S(2)}) collective-permute-start(bf16[16,128,128]{2,1,0:T(8,128)(2,1)S(1)} %get-tuple-element.80), channel_id=1, source_target_pairs={{0,16},{16,0},{1,17},{17,1},{2,18},{18,2},{3,19},{19,3},{4,20},{20... | collective-permute-start | bytes 1572872 | tf_op jit(solution)/shard_map/ppermute | solution.py:736
  131.0 1.5 collective-permute-done.5
  132.5 0.1 add_convert_fusion
  132.6 0.1 pad_maximum_fusion
  132.7 16.4 %all_to_all.39.pieces = bf16[16,192,128]{2,1,0:T(8,128)(2,1)S(1)} all-to-all(bf16[16,192,128]{2,1,0:T(8,128)(2,1)S(1)} %pad_maximum_fusion), channel_id=1, replica_groups=mesh['x'=4,'c'=2,'z'=4,'y'=4] {'z','y'}, dimensions={0} | all-to-all | bytes 1572864 | tf_op jit(solution)/shard_map/all_to_all | solution.py:732
  149.1 4.7 %shard_map.310 = (bf16[128,512]{1,0:T(8,128)(2,1)S(1)}, bf16[128,512]{1,0:T(8,128)(2,1)S(1)}, bf16[16,208,128]{2,1,0:T(8,128)(2,1)S(1)}, bf16[16,208,128]{2,1,0:T(8,128)(2,1)}) custom-call(s32[3]{0:T(128)S(1)} %pad_add_fusion.scalars, bf16[16,192,128]{2,1,0:T(8,128)(2,1)S(1)} %all_to_all.39.pieces, bf16[256,512]{1,0:T(8,128)(2,1)} %tokens_in.7, ...), custom_call_target="tpu_custom_call" | custom-call | flops 805306368 | bytes 8388608 | tf_op jit(solution)/shard_map/pallas_call | solution.py:715
  153.9 1.6 collective-permute-start.6
  155.4 1.1 slice.23
  156.5 0.1 collective-permute-start.9
  156.7 0.5 collective-permute-start.7
  157.1 0.1 collective-permute-start.8
  157.2 1.6 collective-permute-done.7.refs_16_
  158.8 0.2 collective-permute-done.8.refs_18_
  159.0 1.2 shard_map.311
  160.2 23.4 %all_to_all.40.pieces = bf16[16,352,128]{2,1,0:T(8,128)(2,1)S(1)} all-to-all(bf16[16,352,128]{2,1,0:T(8,128)(2,1)S(1)} %shard_map.311), channel_id=1, replica_groups=mesh['x'=4,'c'=2,'z'=4,'y'=4] {'z','y'}, dimensions={0} | all-to-all | bytes 2883584 | tf_op jit(solution)/shard_map/all_to_all | solution.py:732
  183.7 0.0 copy-start.6
  183.7 0.0 copy-start.7
  183.7 0.0 copy-start.9
  183.7 0.0 copy-start.10
  183.8 0.2 shard_map.312
  184.0 10.0 %all_to_all.41.grads_own = bf16[4,352,128]{2,1,0:T(8,128)(2,1)S(1)} all-to-all(bf16[4,352,128]{2,1,0:T(8,128)(2,1)S(1)} %shard_map.312), channel_id=1, replica_groups=mesh['x'=4,'c'=2,'z'=4,'y'=4] {'x'}, dimensions={0} | all-to-all | bytes 720896 | tf_op jit(solution)/shard_map/all_to_all | solution.py:876
  194.0 3.0 %collective-permute-start.10 = (bf16[4,352,128]{2,1,0:T(8,128)(2,1)S(1)}, bf16[4,352,128]{2,1,0:T(8,128)(2,1)S(1)}, u32[]{:S(2)}, u32[]{:S(2)}) collective-permute-start(bf16[4,352,128]{2,1,0:T(8,128)(2,1)S(1)} %all_to_all.41.grads_own), channel_id=1, source_target_pairs={{0,16},{16,0},{1,17},{17,1},{2,18},{18,2},{3,19},{19,3},{4,20},{20... | collective-permute-start | bytes 1081352 | tf_op jit(solution)/shard_map/ppermute | solution.py:736
  197.0 1.3 collective-permute-done.10.grads_other
  198.5 2.5 %shard_map.313 = (bf16[256,512]{1,0:T(8,128)(2,1)}, bf16[256,512]{1,0:T(8,128)(2,1)}, f32[96,512]{1,0:T(8,128)}, f32[32,512]{1,0:T(8,128)}, f32[512,128]{1,0:T(8...) custom-call(s32[3]{0:T(128)S(1)} %pad_add_fusion.scalars, ...), custom_call_target="tpu_custom_call" | custom-call | bytes 8388608 | tf_op jit(solution)/shard_map/pallas_call | solution.py:715
  (41 shorter events, 0.1 us)
Async XLA Ops:
  7.2 72.4 %all-gather.3.cloned.1.call-start = ((), (), s32[]{:S(2)}) async-start(), calls=%async_computation.9 | async-start | bytes 2949120 | tf_op jit(solution)/shard_map/all_gather | solution.py:779
  38.2 3.0 %copy-start.17 = (s32[1,2]{1,0:T(1,128)S(1)}, s32[1,2]{1,0:T(1,128)}, u32[]{:S(2)}) copy-start(s32[1,2]{1,0:T(1,128)} %lens_own.5) | copy-start | bytes 28
  39.1 116.4 %reduce-scatter.2.cloned.1.call-start = ((), (), s32[]{:S(2)}) async-start(), calls=%async_computation.8 | async-start | bytes 5898240 | tf_op jit(solution)/shard_map/reduce_scatter | solution.py:837
  39.2 4.3 %collective-permute-start = (bf16[16,208,128]{2,1,0:T(8,128)(2,1)S(1)}, bf16[16,208,128]{2,1,0:T(8,128)(2,1)S(1)}, u32[]{:S(2)}, u32[]{:S(2)}) collective-permute-start(bf16[16,208,128]{2,1,0:T(8,128)(2,1)S(1)} %slice.21), channel_id=1, source_target_pairs={{0,16},{16,0},{1,17},{17,1},{2,18},{18,2},{3,19},{19,3},{4,20},{20... | collective-permute-start | bytes 2555912 | tf_op jit(solution)/shard_map/ppermute | solution.py:736
  41.1 2.4 %collective-permute-start.2 = (bf16[2,128,512]{2,1,0:T(8,128)(2,1)S(1)}, bf16[2,128,512]{2,1,0:T(8,128)(2,1)S(1)}, u32[]{:S(2)}, u32[]{:S(2)}) collective-permute-start(bf16[2,128,512]{2,1,0:T(8,128)(2,1)S(1)} %get-tuple-element.66), channel_id=1, source_target_pairs={{0,16},{16,0},{1,17},{17,1},{2,18},{18,2},{3,19},{19,3},{4,20},{20... | collective-permute-start | bytes 786440 | tf_op jit(solution)/shard_map/ppermute | solution.py:736
  41.2 2.3 %collective-permute-start.1 = (s32[1,2]{1,0:T(1,128)S(1)}, s32[1,2]{1,0:T(1,128)S(1)}, u32[]{:S(2)}, u32[]{:S(2)}) collective-permute-start(s32[1,2]{1,0:T(1,128)S(1)} %copy-done.17), channel_id=1, source_target_pairs={{0,16},{16,0},{1,17},{17,1},{2,18},{18,2},{3,19},{19,3},{4,20},{20... | collective-permute-start | bytes 32 | tf_op jit(solution)/shard_map/ppermute | solution.py:736
  43.5 19.2 %copy-start = (bf16[2,128,512]{2,1,0:T(8,128)(2,1)}, bf16[2,128,512]{2,1,0:T(8,128)(2,1)S(1)}, u32[]{:S(2)}) copy-start(bf16[2,128,512]{2,1,0:T(8,128)(2,1)S(1)} %collective-permute-done.2.rows_other.rows_in) | copy-start | bytes 786436
  62.6 3.4 %collective-permute-start.3 = (bf16[16,192,128]{2,1,0:T(8,128)(2,1)S(1)}, bf16[16,192,128]{2,1,0:T(8,128)(2,1)S(1)}, u32[]{:S(2)}, u32[]{:S(2)}) collective-permute-start(bf16[16,192,128]{2,1,0:T(8,128)(2,1)S(1)} %all_to_all.36.pieces), channel_id=1, source_target_pairs={{0,16},{16,0},{1,17},{17,1},{2,18},{18,2},{3,19},{19,3},{4,20},{20... | collective-permute-start | bytes 2359304 | tf_op jit(solution)/shard_map/ppermute | solution.py:736
  79.6 11.4 %collective-permute-start.4 = (bf16[4,16,144,128]{3,2,1,0:T(8,128)(2,1)}, bf16[4,16,144,128]{3,2,1,0:T(8,128)(2,1)S(1)}, u32[]{:S(2)}, u32[]{:S(2)}) collective-permute-start(bf16[4,16,144,128]{3,2,1,0:T(8,128)(2,1)} %bitcast.30), channel_id=1, source_target_pairs={{0,16},{16,0},{1,17},{17,1},{2,18},{18,2},{3,19},{19,3},{4,20},{20... | collective-permute-start | bytes 7077896 | tf_op jit(solution)/shard_map/ppermute | solution.py:736
  128.1 4.4 %collective-permute-start.5 = (bf16[16,128,128]{2,1,0:T(8,128)(2,1)S(1)}, bf16[16,128,128]{2,1,0:T(8,128)(2,1)S(1)}, u32[]{:S(2)}, u32[]{:S(2)}) collective-permute-start(bf16[16,128,128]{2,1,0:T(8,128)(2,1)S(1)} %get-tuple-element.80), channel_id=1, source_target_pairs={{0,16},{16,0},{1,17},{17,1},{2,18},{18,2},{3,19},{19,3},{4,20},{20... | collective-permute-start | bytes 1572872 | tf_op jit(solution)/shard_map/ppermute | solution.py:736
  149.1 7.5 %copy-start.18 = (bf16[128,512]{1,0:T(8,128)(2,1)S(1)}, bf16[128,512]{1,0:T(8,128)(2,1)}, u32[]{:S(2)}) copy-start(bf16[128,512]{1,0:T(8,128)(2,1)} %get-tuple-element.86) | copy-start | bytes 393220
  153.9 5.1 %collective-permute-start.6 = (bf16[16,208,128]{2,1,0:T(8,128)(2,1)}, bf16[16,208,128]{2,1,0:T(8,128)(2,1)S(1)}, u32[]{:S(2)}, u32[]{:S(2)}) collective-permute-start(bf16[16,208,128]{2,1,0:T(8,128)(2,1)} %get-tuple-element.85), channel_id=1, source_target_pairs={{0,16},{16,0},{1,17},{17,1},{2,18},{18,2},{3,19},{19,3},{4,20},{20... | collective-permute-start | bytes 2555912 | tf_op jit(solution)/shard_map/ppermute | solution.py:736
  156.5 2.5 %collective-permute-start.9 = (bf16[16,144,128]{2,1,0:T(8,128)(2,1)S(1)}, bf16[16,144,128]{2,1,0:T(8,128)(2,1)S(1)}, u32[]{:S(2)}, u32[]{:S(2)}) collective-permute-start(bf16[16,144,128]{2,1,0:T(8,128)(2,1)S(1)} %bitcast.29), channel_id=1, source_target_pairs={{0,16},{16,0},{1,17},{17,1},{2,18},{18,2},{3,19},{19,3},{4,20},{20... | collective-permute-start | bytes 1769480 | tf_op jit(solution)/shard_map/ppermute | solution.py:736
  156.7 2.1 %collective-permute-start.7 = (bf16[128,512]{1,0:T(8,128)(2,1)S(1)}, bf16[128,512]{1,0:T(8,128)(2,1)S(1)}, u32[]{:S(2)}, u32[]{:S(2)}) collective-permute-start(bf16[128,512]{1,0:T(8,128)(2,1)S(1)} %copy-done.18), channel_id=1, source_target_pairs={{0,16},{16,0},{1,17},{17,1},{2,18},{18,2},{3,19},{19,3},{4,20},{20... | collective-permute-start | bytes 393224 | tf_op jit(solution)/shard_map/ppermute | solution.py:736
  157.1 1.9 collective-permute-start.8
  183.6 14.7 %copy-start.1 = (f32[512,128]{1,0:T(8,128)S(1)}, f32[512,128]{1,0:T(8,128)}, u32[]{:S(2)}) copy-start(f32[512,128]{1,0:T(8,128)} %refs_2_.1) | copy-start | bytes 786436
  183.6 14.7 %copy-start.2 = (f32[128,512]{1,0:T(8,128)S(1)}, f32[128,512]{1,0:T(8,128)}, u32[]{:S(2)}) copy-start(f32[128,512]{1,0:T(8,128)} %refs_3_.1) | copy-start | bytes 786436
  183.6 14.7 %copy-start.3 = (f32[512,96]{0,1:T(8,128)S(1)}, f32[512,96]{0,1:T(8,128)}, u32[]{:S(2)}) copy-start(f32[512,96]{0,1:T(8,128)} %param.21) | copy-start | bytes 589828
  183.6 14.7 %copy-start.4 = (f32[512,32]{0,1:T(8,128)S(1)}, f32[512,32]{0,1:T(8,128)}, u32[]{:S(2)}) copy-start(f32[512,32]{0,1:T(8,128)} %param.22) | copy-start | bytes 196612
  183.6 14.7 %copy-start.5 = (f32[512,128]{1,0:T(8,128)S(1)}, f32[512,128]{1,0:T(8,128)}, u32[]{:S(2)}) copy-start(f32[512,128]{1,0:T(8,128)} %refs_7_.1) | copy-start | bytes 786436
  183.7 14.7 %copy-start.6 = (f32[128,512]{1,0:T(8,128)S(1)}, f32[128,512]{1,0:T(8,128)}, u32[]{:S(2)}) copy-start(f32[128,512]{1,0:T(8,128)} %refs_8_.1) | copy-start | bytes 786436
  183.7 14.7 %copy-start.7 = (f32[512,128]{1,0:T(8,128)S(1)}, f32[512,128]{1,0:T(8,128)}, u32[]{:S(2)}) copy-start(f32[512,128]{1,0:T(8,128)} %refs_12_.1) | copy-start | bytes 786436
  183.7 14.7 %copy-start.8 = (f32[128,512]{1,0:T(8,128)S(1)}, f32[128,512]{1,0:T(8,128)}, u32[]{:S(2)}) copy-start(f32[128,512]{1,0:T(8,128)} %refs_13_.1) | copy-start | bytes 786436
  183.7 14.7 %copy-start.9 = (f32[512,96]{0,1:T(8,128)S(1)}, f32[512,96]{0,1:T(8,128)}, u32[]{:S(2)}) copy-start(f32[512,96]{0,1:T(8,128)} %param.26) | copy-start | bytes 589828
  183.7 14.7 %copy-start.10 = (f32[512,96]{0,1:T(8,128)S(1)}, f32[512,96]{0,1:T(8,128)}, u32[]{:S(2)}) copy-start(f32[512,96]{0,1:T(8,128)} %param.31) | copy-start | bytes 589828
  183.7 14.7 %copy-start.11 = (bf16[128,512]{1,0:T(8,128)(2,1)S(1)}, bf16[128,512]{1,0:T(8,128)(2,1)}, u32[]{:S(2)}) copy-start(bf16[128,512]{1,0:T(8,128)(2,1)} %get-tuple-element.90.refs_15_) | copy-start | bytes 393220
  183.7 14.7 %copy-start.12 = (f32[512,32]{0,1:T(8,128)S(1)}, f32[512,32]{0,1:T(8,128)}, u32[]{:S(2)}) copy-start(f32[512,32]{0,1:T(8,128)} %param.27) | copy-start | bytes 196612
  183.7 14.7 %copy-start.13 = (f32[512,32]{0,1:T(8,128)S(1)}, f32[512,32]{0,1:T(8,128)}, u32[]{:S(2)}) copy-start(f32[512,32]{0,1:T(8,128)} %param.32) | copy-start | bytes 196612
  183.8 14.7 %copy-start.14 = (f32[12,32]{1,0:T(8,128)S(1)}, f32[12,32]{1,0:T(8,128)}, u32[]{:S(2)}) copy-start(f32[12,32]{1,0:T(8,128)} %refs_4_.1) | copy-start | bytes 4612
  183.8 14.7 %copy-start.15 = (f32[12,32]{1,0:T(8,128)S(1)}, f32[12,32]{1,0:T(8,128)}, u32[]{:S(2)}) copy-start(f32[12,32]{1,0:T(8,128)} %refs_9_.1) | copy-start | bytes 4612
  183.8 14.7 %copy-start.16 = (f32[12,32]{1,0:T(8,128)S(1)}, f32[12,32]{1,0:T(8,128)}, u32[]{:S(2)}) copy-start(f32[12,32]{1,0:T(8,128)} %refs_14_.1) | copy-start | bytes 4612
  194.0 4.3 %collective-permute-start.10 = (bf16[4,352,128]{2,1,0:T(8,128)(2,1)S(1)}, bf16[4,352,128]{2,1,0:T(8,128)(2,1)S(1)}, u32[]{:S(2)}, u32[]{:S(2)}) collective-permute-start(bf16[4,352,128]{2,1,0:T(8,128)(2,1)S(1)} %all_to_all.41.grads_own), channel_id=1, source_target_pairs={{0,16},{16,0},{1,17},{17,1},{2,18},{18,2},{3,19},{19,3},{4,20},{20... | collective-permute-start | bytes 1081352 | tf_op jit(solution)/shard_map/ppermute | solution.py:736
Sparse Core Ops, SparseCore 0:
  39.2 31.5 all-gather.2
  101.6 49.1 reduce-scatter.1
